TPU v7x, 128 devices: a whole 4x4x4 slice. The times are simulated.
128 devices in a mesh: section: 2 (over core), exp: 16 (over x, z), tp: 4 (over y).
Axes of the slice: x: 4, y: 4, z: 4, core: 2. Of those that a mesh axis runs over, the one named last changes fastest.
Arguments:
- activations: bfloat16 [4, 2048, 1024], P(None, ('exp', 'tp')), may hold values from -6 to 6
- cotangent: bfloat16 [4, 2048, 1024], P(None, ('exp', 'tp')), may hold values from -6 to 6
- segments: int32 [4, 2048], P(None, 'exp'), may hold values from 0 to 127, as said below
- routes: int32 [4, 2048, 8], P(None, ('exp', 'tp')), may hold values from 0 to 31, all different within a row; in each aligned block of 32 rows (0 to 31, 32 to 63, ..., all dimensions but the last counted through in order) at most 16 rows name the same one
- attention_gain: bfloat16 [2, 1024], P('section'), may hold values from 0.5 to 1.5
- query_weight: bfloat16 [2, 1024, 1024], P('section', None, 'tp'), may hold values from -0.1875 to 0.1875
- key_weight: bfloat16 [2, 1024, 512], P('section', None, 'tp'), may hold values from -0.1875 to 0.1875
- value_weight: bfloat16 [2, 1024, 512], P('section', None, 'tp'), may hold values from -0.1875 to 0.1875
- output_weight: bfloat16 [2, 1024, 1024], P('section', 'tp'), may hold values from -0.75 to 0.75
- mixture_gain: bfloat16 [2, 1024], P('section'), may hold values from 0.5 to 1.5
- router_weight: bfloat16 [2, 1024, 32], P('section'), may hold values from -0.09375 to 0.09375
- expert_gate_up: bfloat16 [2, 32, 1024, 1024], P('section', 'exp'), may hold values from -0.1875 to 0.1875
- expert_down: bfloat16 [2, 32, 512, 1024], P('section', 'exp'), may hold values from -0.75 to 0.75
Outputs:
- section_output: bfloat16 [2, 4, 2048, 1024], P('section', None, ('exp', 'tp'))
- section_input_grad: float32 [2, 4, 2048, 1024], P('section', None, ('exp', 'tp'))
- grad_attention_gain: float32 [2, 1024], P('section')
- grad_query: float32 [2, 1024, 1024], P('section', 'exp', 'tp')
- grad_key: float32 [2, 1024, 512], P('section', 'exp', 'tp')
- grad_value: float32 [2, 1024, 512], P('section', 'exp', 'tp')
- grad_output: float32 [2, 1024, 1024], P('section', 'tp', 'exp')
- grad_mixture_gain: float32 [2, 1024], P('section')
- grad_router: float32 [2, 1024, 32], P('section')
- grad_gate_up: float32 [2, 32, 1024, 1024], P('section', 'exp', None, 'tp')
- grad_down: float32 [2, 32, 512, 1024], P('section', 'exp', None, 'tp')
Inputs may be any that keep to these rules, and one draw needn't show every extreme that they name: `segments`: segment numbers never fall within each group of 128 rows; in each group one sequence starts within the first 32 rows and ends within the last 32; in each micro-batch one group is a single sequence of 128 rows. `routes`: within each aligned block of 32 rows (the rows of one device in one micro-batch) no expert is named by more than 16 rows.
All inputs are finite; a program needn't handle non-finite values.
Results may differ from a plain program's by a relative error of at most 0.039.
Values may be sent and summed in bfloat16 or wider, within the bound.
A program may use at most 192 MiB of HBM per device.

v0:
```python
import jax
import jax.numpy as jnp
from jax import lax
from jax.sharding import PartitionSpec as P

HD = 64
E = 32
F = 512
CAP = 16


EPSILON = 1e-06
ROPE_BASE = 10000.0
SCORE_SCALE = 0.125
MASKED = -1e30
HIGHEST = lax.Precision.HIGHEST


def from_behind(x, axis, by):
    length = lax.axis_size(axis)
    pairs = [(i, i + by) for i in range(length) if 0 <= i + by < length]
    return lax.ppermute(x, axis, pairs)


def rotate_half(values):
    middle = values.shape[-1] // 2
    return jnp.concatenate([-values[..., middle:], values[..., :middle]], axis=-1)


def rotary(values, cosine_part, sine_part):
    return values * cosine_part + rotate_half(values) * sine_part


def unrotary(values, cosine_part, sine_part):
    return values * cosine_part - rotate_half(values * sine_part)


def rope_tables(seg_rows, head_size):
    length = seg_rows.shape[0]
    before = jnp.sum((seg_rows[None, :] < seg_rows[:, None]).astype(jnp.int32), axis=1)
    places = (jnp.arange(length, dtype=jnp.int32) - before).astype(jnp.float32)
    powers = jnp.arange(0, head_size, 2, dtype=jnp.int32).astype(jnp.float32) / head_size
    angles = places[:, None] * (ROPE_BASE ** (-powers))[None, :]
    angles = jnp.concatenate([angles, angles], axis=1)
    indices = jnp.arange(length, dtype=jnp.int32)
    allowed = (seg_rows[:, None] == seg_rows[None, :]) & (indices[None, :] <= indices[:, None])
    return (jnp.cos(angles), jnp.sin(angles), allowed)


def routing_plan(route_rows, experts, capacity):
    row_count, pick_count = route_rows.shape
    labels = jnp.arange(experts, dtype=jnp.int32)
    onehot = (route_rows[:, :, None] == labels[None, None, :]).astype(jnp.int32)
    flattened = onehot.reshape(row_count * pick_count, experts)
    earlier = jnp.cumsum(flattened, axis=0) - flattened
    within = jnp.sum(earlier * flattened, axis=1).reshape(row_count, pick_count)
    target = route_rows * capacity + within
    slot_ids = jnp.arange(experts * capacity, dtype=jnp.int32)
    matched = target.reshape(-1)[:, None] == slot_ids[None, :]
    filled = jnp.any(matched, axis=0)
    pair_ids = jnp.arange(row_count * pick_count, dtype=jnp.int32)
    source = jnp.sum(jnp.where(matched, pair_ids[:, None], 0), axis=0)
    return (onehot, target, filled, source)


def masked_scores(queries, key_heads, allowed):
    scores = (
        jnp.einsum("qgjd,kgd->gjqk", queries, key_heads, preferred_element_type=jnp.float32)
        * SCORE_SCALE
    )
    return jnp.where(allowed[None, None], scores, MASKED)


def layer_forward(layer_in, seg_rows, route_rows, weights):
    (
        attention_gain,
        query_weight,
        key_weight,
        value_weight,
        output_weight,
        mixture_gain,
        router_weight,
        expert_gate_up,
        expert_down,
    ) = weights
    inverse_one = lax.rsqrt(jnp.mean(layer_in * layer_in, axis=1, keepdims=True) + EPSILON)
    normed = (layer_in * inverse_one * attention_gain).astype(jnp.bfloat16)
    rows_all = lax.all_gather(normed, "tp", axis=0, tiled=True)
    group_rows = rows_all.shape[0]
    cosine_table, sine_table, allowed = rope_tables(seg_rows, HD)
    kv_local = key_weight.shape[1] // HD
    group_size = query_weight.shape[1] // key_weight.shape[1]
    queries = jnp.dot(rows_all, query_weight, preferred_element_type=jnp.float32).reshape(
        group_rows, kv_local, group_size, HD
    )
    queries = rotary(queries, cosine_table[:, None, None, :], sine_table[:, None, None, :]).astype(
        jnp.bfloat16
    )
    key_heads = jnp.dot(rows_all, key_weight, preferred_element_type=jnp.float32).reshape(
        group_rows, kv_local, HD
    )
    key_heads = rotary(key_heads, cosine_table[:, None, :], sine_table[:, None, :]).astype(
        jnp.bfloat16
    )
    value_heads = (
        jnp.dot(rows_all, value_weight, preferred_element_type=jnp.float32)
        .reshape(group_rows, kv_local, HD)
        .astype(jnp.bfloat16)
    )
    scores = masked_scores(queries, key_heads, allowed)
    highest = jnp.max(scores, axis=-1, keepdims=True)
    lifted = jnp.exp(scores - highest)
    summed = jnp.sum(lifted, axis=-1, keepdims=True)
    attention = lifted / summed
    log_total = highest + jnp.log(summed)
    attended = jnp.einsum(
        "gjqk,kgd->qgjd",
        attention.astype(jnp.bfloat16),
        value_heads,
        preferred_element_type=jnp.float32,
    )
    attended = attended.reshape(group_rows, -1).astype(jnp.bfloat16)
    after_attn = layer_in + lax.psum_scatter(
        jnp.dot(attended, output_weight, preferred_element_type=jnp.float32).astype(jnp.bfloat16),
        "tp",
        scatter_dimension=0,
        tiled=True,
    ).astype(jnp.float32)
    inverse_two = lax.rsqrt(jnp.mean(after_attn * after_attn, axis=1, keepdims=True) + EPSILON)
    normed_two = (after_attn * inverse_two * mixture_gain).astype(jnp.bfloat16)
    logits = jnp.dot(normed_two, router_weight, preferred_element_type=jnp.float32)
    onehot, target, filled, source = routing_plan(route_rows, E, CAP)
    pick_count = route_rows.shape[1]
    chosen = jnp.sum(onehot.astype(jnp.float32) * logits[:, None, :], axis=2)
    gate_weights = jax.nn.softmax(chosen, axis=1)
    outgoing = jnp.where(
        filled[:, None], normed_two[source // pick_count], jnp.zeros((), jnp.bfloat16)
    ).reshape(E, CAP, -1)
    incoming = lax.all_to_all(outgoing, "exp", split_axis=0, concat_axis=1, tiled=True)
    gate_up = jnp.einsum(
        "esd,edf->esf", incoming, expert_gate_up, preferred_element_type=jnp.float32
    )
    hidden = (jax.nn.silu(gate_up[..., :F]) * gate_up[..., F:]).astype(jnp.bfloat16)
    produced = jnp.einsum(
        "esf,efd->esd", hidden, expert_down, preferred_element_type=jnp.float32
    ).astype(jnp.bfloat16)
    returned = lax.all_to_all(produced, "exp", split_axis=1, concat_axis=0, tiled=True)
    picked = returned.reshape(E * CAP, -1)[target]
    result = after_attn + jnp.sum(gate_weights[:, :, None] * picked.astype(jnp.float32), axis=1)
    stored = (
        layer_in,
        inverse_one,
        rows_all,
        queries,
        key_heads,
        value_heads,
        log_total,
        attended,
        after_attn,
        inverse_two,
        normed_two,
        gate_weights,
        incoming,
        gate_up,
        hidden,
        picked,
    )
    return (result, stored)


def layer_backward(grad_result, stored, seg_rows, route_rows, weights):
    (
        attention_gain,
        query_weight,
        key_weight,
        value_weight,
        output_weight,
        mixture_gain,
        router_weight,
        expert_gate_up,
        expert_down,
    ) = weights
    (
        layer_in,
        inverse_one,
        rows_all,
        queries,
        key_heads,
        value_heads,
        log_total,
        attended,
        after_attn,
        inverse_two,
        normed_two,
        gate_weights,
        incoming,
        gate_up,
        hidden,
        picked,
    ) = stored
    row_count = grad_result.shape[0]
    group_rows = rows_all.shape[0]
    onehot, target, filled, source = routing_plan(route_rows, E, CAP)
    pick_count = route_rows.shape[1]
    scaled_rows = (
        (gate_weights[:, :, None] * grad_result[:, None, :])
        .astype(jnp.bfloat16)
        .reshape(row_count * pick_count, -1)
    )
    outgoing = jnp.where(filled[:, None], scaled_rows[source], jnp.zeros((), jnp.bfloat16)).reshape(
        E, CAP, -1
    )
    grad_gates = jnp.sum(grad_result[:, None, :] * picked.astype(jnp.float32), axis=2)
    arriving = lax.all_to_all(outgoing, "exp", split_axis=0, concat_axis=1, tiled=True)
    grad_down = jnp.einsum("esf,esd->efd", hidden, arriving, preferred_element_type=jnp.float32)
    grad_hidden = jnp.einsum(
        "esd,efd->esf", arriving, expert_down, preferred_element_type=jnp.float32
    )
    gate_part = gate_up[..., :F]
    up_part = gate_up[..., F:]
    sigmoid_gate = jax.nn.sigmoid(gate_part)
    grad_gate = grad_hidden * up_part * sigmoid_gate * (1.0 + gate_part * (1.0 - sigmoid_gate))
    grad_upper = grad_hidden * gate_part * sigmoid_gate
    grad_joined = jnp.concatenate([grad_gate, grad_upper], axis=-1).astype(jnp.bfloat16)
    grad_gate_up = jnp.einsum(
        "esd,esf->edf", incoming, grad_joined, preferred_element_type=jnp.float32
    )
    grad_incoming = jnp.einsum(
        "esf,edf->esd", grad_joined, expert_gate_up, preferred_element_type=jnp.float32
    ).astype(jnp.bfloat16)
    coming_back = lax.all_to_all(
        grad_incoming, "exp", split_axis=1, concat_axis=0, tiled=True
    ).reshape(E * CAP, -1)
    grad_normed_two = jnp.sum(coming_back[target].astype(jnp.float32), axis=1)
    grad_chosen = gate_weights * (
        grad_gates - jnp.sum(gate_weights * grad_gates, axis=1, keepdims=True)
    )
    grad_logits = jnp.sum(onehot.astype(jnp.float32) * grad_chosen[:, :, None], axis=1)
    router_float = router_weight.astype(jnp.float32)
    grad_normed_two = grad_normed_two + jnp.dot(grad_logits, router_float.T, precision=HIGHEST)
    grad_router = jnp.dot(normed_two.astype(jnp.float32).T, grad_logits, precision=HIGHEST)
    scaled_two = mixture_gain * grad_normed_two
    grad_after = (
        grad_result
        + inverse_two * scaled_two
        - after_attn * inverse_two**3 * jnp.mean(after_attn * scaled_two, axis=1, keepdims=True)
    )
    grad_mixture_gain = jnp.sum(grad_normed_two * after_attn * inverse_two, axis=0)
    grad_rows_all = lax.all_gather(grad_after.astype(jnp.bfloat16), "tp", axis=0, tiled=True)
    grad_output = jnp.einsum(
        "rc,rd->cd", attended, grad_rows_all, preferred_element_type=jnp.float32
    )
    grad_attended = jnp.einsum(
        "rd,cd->rc", grad_rows_all, output_weight, preferred_element_type=jnp.float32
    )
    grad_attended = grad_attended.astype(jnp.bfloat16).reshape(queries.shape)
    cosine_table, sine_table, allowed = rope_tables(seg_rows, HD)
    scores = masked_scores(queries, key_heads, allowed)
    attention = jnp.exp(scores - log_total)
    grad_attention = jnp.einsum(
        "qgjd,kgd->gjqk", grad_attended, value_heads, preferred_element_type=jnp.float32
    )
    grad_scores = attention * (
        grad_attention - jnp.sum(attention * grad_attention, axis=-1, keepdims=True)
    )
    grad_scores = grad_scores.astype(jnp.bfloat16)
    grad_queries = (
        jnp.einsum("gjqk,kgd->qgjd", grad_scores, key_heads, preferred_element_type=jnp.float32)
        * SCORE_SCALE
    )
    grad_keys = (
        jnp.einsum("gjqk,qgjd->kgd", grad_scores, queries, preferred_element_type=jnp.float32)
        * SCORE_SCALE
    )
    grad_values = jnp.einsum(
        "gjqk,qgjd->kgd",
        attention.astype(jnp.bfloat16),
        grad_attended,
        preferred_element_type=jnp.float32,
    )
    grad_queries = (
        unrotary(grad_queries, cosine_table[:, None, None, :], sine_table[:, None, None, :])
        .astype(jnp.bfloat16)
        .reshape(group_rows, -1)
    )
    grad_keys = (
        unrotary(grad_keys, cosine_table[:, None, :], sine_table[:, None, :])
        .astype(jnp.bfloat16)
        .reshape(group_rows, -1)
    )
    grad_values = grad_values.astype(jnp.bfloat16).reshape(group_rows, -1)
    grad_query = jnp.einsum("rd,rc->dc", rows_all, grad_queries, preferred_element_type=jnp.float32)
    grad_key = jnp.einsum("rd,rc->dc", rows_all, grad_keys, preferred_element_type=jnp.float32)
    grad_value = jnp.einsum("rd,rc->dc", rows_all, grad_values, preferred_element_type=jnp.float32)
    grad_normed = lax.psum_scatter(
        (
            jnp.einsum("rc,dc->rd", grad_queries, query_weight, preferred_element_type=jnp.float32)
            + jnp.einsum("rc,dc->rd", grad_keys, key_weight, preferred_element_type=jnp.float32)
            + jnp.einsum("rc,dc->rd", grad_values, value_weight, preferred_element_type=jnp.float32)
        ).astype(jnp.bfloat16),
        "tp",
        scatter_dimension=0,
        tiled=True,
    ).astype(jnp.float32)
    scaled_one = attention_gain * grad_normed
    grad_input = (
        grad_after
        + inverse_one * scaled_one
        - layer_in * inverse_one**3 * jnp.mean(layer_in * scaled_one, axis=1, keepdims=True)
    )
    grad_attention_gain = jnp.sum(grad_normed * layer_in * inverse_one, axis=0)
    pieces = (
        (grad_query, grad_key, grad_value, grad_output),
        (grad_attention_gain, grad_mixture_gain, grad_router),
        (grad_gate_up, grad_down),
    )
    return (grad_input, pieces)


def settle(attention_parts, small_parts, expert_parts):
    attention_sums = (
        lax.psum_scatter(
            attention_parts[0].astype(jnp.bfloat16), "exp", scatter_dimension=0, tiled=True
        ).astype(jnp.float32),
        lax.psum_scatter(
            attention_parts[1].astype(jnp.bfloat16), "exp", scatter_dimension=0, tiled=True
        ).astype(jnp.float32),
        lax.psum_scatter(
            attention_parts[2].astype(jnp.bfloat16), "exp", scatter_dimension=0, tiled=True
        ).astype(jnp.float32),
        lax.psum_scatter(
            attention_parts[3].astype(jnp.bfloat16), "exp", scatter_dimension=1, tiled=True
        ).astype(jnp.float32),
    )
    small_totals = lax.psum(small_parts, ("exp", "tp"))
    expert_totals = (
        lax.psum_scatter(
            expert_parts[0].astype(jnp.bfloat16), "tp", scatter_dimension=2, tiled=True
        ).astype(jnp.float32),
        lax.psum_scatter(
            expert_parts[1].astype(jnp.bfloat16), "tp", scatter_dimension=2, tiled=True
        ).astype(jnp.float32),
    )
    return (attention_sums, small_totals, expert_totals)


def per_device(
    activations,
    cotangent,
    segments,
    routes,
    attention_gain,
    query_weight,
    key_weight,
    value_weight,
    output_weight,
    mixture_gain,
    router_weight,
    expert_gate_up,
    expert_down,
):
    section_index = lax.axis_index("section")
    micro_count = activations.shape[0]
    weights = (
        attention_gain[0].astype(jnp.float32),
        query_weight[0],
        key_weight[0],
        value_weight[0],
        output_weight[0],
        mixture_gain[0].astype(jnp.float32),
        router_weight[0],
        expert_gate_up[0],
        expert_down[0],
    )
    received = jnp.zeros(activations.shape[1:], jnp.float32)
    stored_list = []
    output_list = []
    for clock_tick in range(micro_count + 1):
        forward_batch = jnp.clip(clock_tick - section_index, 0, micro_count - 1)
        fresh_input = activations[min(clock_tick, micro_count - 1)].astype(jnp.float32)
        layer_in = jnp.where(section_index == 0, fresh_input, received)
        result, stored = layer_forward(
            layer_in, segments[forward_batch], routes[forward_batch], weights
        )
        rounded = result.astype(jnp.bfloat16)
        stored_list.append(stored)
        output_list.append(rounded)
        if clock_tick < micro_count:
            received = from_behind(rounded, "section", 1).astype(jnp.float32)
    section_output = jnp.stack(
        [
            jnp.where(section_index == 0, output_list[batch_index], output_list[batch_index + 1])
            for batch_index in range(micro_count)
        ]
    )[None]
    is_last = section_index == 1
    grad_received = jnp.zeros(activations.shape[1:], jnp.float32)
    input_grads = []
    totals_all = None
    for clock_tick in range(micro_count + 1):
        batch_raw = clock_tick - 1 + section_index
        back_batch = jnp.clip(batch_raw, 0, micro_count - 1)
        active = (batch_raw >= 0) & (batch_raw < micro_count)
        later_state = stored_list[min(clock_tick + 1, micro_count)]
        earlier_state = stored_list[max(clock_tick - 1, 0)]
        stored = jax.tree.map(
            lambda upper_value, lower_value: jnp.where(is_last, upper_value, lower_value),
            later_state,
            earlier_state,
        )
        fresh_grad = cotangent[min(clock_tick, micro_count - 1)].astype(jnp.float32)
        incoming_grad = jnp.where(is_last, fresh_grad, grad_received)
        grad_input, pieces = layer_backward(
            incoming_grad, stored, segments[back_batch], routes[back_batch], weights
        )
        input_grads.append(grad_input)
        if clock_tick < micro_count:
            grad_received = from_behind(grad_input.astype(jnp.bfloat16), "section", -1).astype(
                jnp.float32
            )
        masked = jax.tree.map(lambda member: jnp.where(active, member, 0.0), pieces)
        totals_all = masked if totals_all is None else jax.tree.map(jnp.add, totals_all, masked)
    settled = settle(totals_all[0], totals_all[1], totals_all[2])
    section_input_grad = jnp.stack(
        [
            jnp.where(is_last, input_grads[batch_index], input_grads[batch_index + 1])
            for batch_index in range(micro_count)
        ]
    )[None]
    attention_sums, small_totals, expert_totals = settled
    return (
        section_output,
        section_input_grad,
        small_totals[0][None],
        attention_sums[0][None],
        attention_sums[1][None],
        attention_sums[2][None],
        attention_sums[3][None],
        small_totals[1][None],
        small_totals[2][None],
        expert_totals[0][None],
        expert_totals[1][None],
    )


def solution(mesh):
    placed = (
        P(None, ("exp", "tp"), None),
        P(None, ("exp", "tp"), None),
        P(None, "exp"),
        P(None, ("exp", "tp"), None),
        P("section", None),
        P("section", None, "tp"),
        P("section", None, "tp"),
        P("section", None, "tp"),
        P("section", "tp", None),
        P("section", None),
        P("section", None, None),
        P("section", "exp", None, None),
        P("section", "exp", None, None),
    )
    return jax.shard_map(
        per_device,
        mesh=mesh,
        in_specs=placed,
        out_specs=(
            P("section", None, ("exp", "tp"), None),
            P("section", None, ("exp", "tp"), None),
            P("section", None),
            P("section", "exp", "tp"),
            P("section", "exp", "tp"),
            P("section", "exp", "tp"),
            P("section", "tp", "exp"),
            P("section", None),
            P("section", None, None),
            P("section", "exp", None, "tp"),
            P("section", "exp", None, "tp"),
        ),
        check_vma=False,
    )
```

profile of v0, /device:TPU:1, one launch (start us, length us, event | category | flops | bytes accessed | tf_op | source)
XLA Modules:
  0.0 1592.3 jit_solution(823000825657110364)
XLA Ops:
  14.6 11.2 all_gather.30
  81.5 7.7 all-to-all-start
  95.2 7.7 all-to-all-done
  123.2 7.5 all-to-all-done.1
  148.3 9.4 all_gather.31
  164.3 14.1 reduce-scatter.19.cloned.1.call-done
  186.0 6.7 all-to-all-start.2
  195.2 11.7 all-to-all-done.2
  226.0 8.3 all-to-all-done.3
  250.7 7.6 all-to-all-start.10
  262.0 10.6 all-to-all-done.10
  287.1 12.5 all-to-all-done.11
  309.7 9.5 all_gather.35
  340.7 9.5 reduce-scatter.27.cloned.1.call-done
  354.1 9.8 all_gather.32
  369.1 22.0 %reduce-scatter.21.cloned.1.call-done = bf16[32,1024]{1,0:T(8,128)(2,1)} async-done(((bf16[128,1024]{1,0:T(8,128)(2,1)}), bf16[32,1024]{1,0:T(8,128)(2,1)}) %reduce-scatter.21.cloned.1.call-update) | async-done | bytes 65552 | tf_op jit(solution)/shard_map/reduce_scatter | solution.py:123
  397.9 6.8 all-to-all-start.4
  439.0 7.0 all-to-all-done.5
  463.7 7.5 all-to-all-start.12
  490.5 7.8 all-to-all-start.13
  500.7 12.0 all-to-all-done.13
  521.9 9.4 all_gather.36
  544.5 6.9 collective-permute-done.2
  551.4 10.7 reduce-scatter.29.cloned.1.call-done
  566.0 9.9 all_gather.33
  585.5 17.3 %reduce-scatter.23.cloned.1.call-done = bf16[32,1024]{1,0:T(8,128)(2,1)} async-done(((bf16[128,1024]{1,0:T(8,128)(2,1)}), bf16[32,1024]{1,0:T(8,128)(2,1)}) %reduce-scatter.23.cloned.1.call-update) | async-done | bytes 65552 | tf_op jit(solution)/shard_map/reduce_scatter | solution.py:123
  641.3 6.9 all-to-all-start.7
  681.9 9.8 all_gather.34
  708.0 7.2 reduce-scatter.25.cloned.1.call-done
  722.1 7.0 all-to-all-start.8
  734.9 8.5 all-to-all-done.8
  785.9 9.4 all_gather.37
  813.4 14.2 reduce-scatter.31.cloned.1.call-done
  854.7 6.9 all-to-all-start.16
  869.2 8.8 all-to-all-done.16
  897.7 9.5 all-to-all-done.17
  917.7 10.6 all_gather.38
  941.3 12.7 reduce-scatter.33.cloned.1.call-done
  986.7 12.6 all-to-all-done.18
  1017.6 9.3 all-to-all-done.19
  1037.5 9.5 all_gather.39
  1102.7 15.0 add_convert_fusion
  1127.6 150.1 %all-reduce = (f32[1,1024]{1,0:T(1,128)}, f32[1,1024]{1,0:T(1,128)}) all-reduce(f32[1,1024]{1,0:T(1,128)S(1)} %bitcast.1465, f32[1,1024]{1,0:T(1,128)S(1)} %bitcast.1464), channel_id=1, replica_groups=mesh['section'=2,'exp'=16,'tp'=4] {'exp','tp'}, use_global_device_ids=true, to_apply=%region_150.151 | all-reduce | flops 2048 | bytes 16384 | tf_op jit(solution)/shard_map/psum | solution.py:335
  1283.3 17.3 %reduce-scatter.43.cloned.1.call-done = bf16[256,64]{0,1:T(8,128)(2,1)} async-done(((bf16[256,1024]{0,1:T(8,128)(2,1)}), bf16[256,64]{0,1:T(8,128)(2,1)}) %reduce-scatter.43.cloned.1.call-update) | async-done | bytes 32784 | tf_op jit(solution)/shard_map/reduce_scatter | solution.py:331
  1301.9 74.2 %reduce-scatter.37.cloned.1.call-done = bf16[64,256]{1,0:T(8,128)(2,1)} async-done(((bf16[1024,256]{1,0:T(8,128)(2,1)}), bf16[64,256]{1,0:T(8,128)(2,1)}) %reduce-scatter.37.cloned.1.call-update) | async-done | bytes 32784 | tf_op jit(solution)/shard_map/reduce_scatter | solution.py:322
  1377.5 32.0 %reduce-scatter.47.cloned.1.call-done = bf16[2,512,256]{2,1,0:T(8,128)(2,1)} async-done(((bf16[2,512,1024]{2,1,0:T(8,128)(2,1)}), bf16[2,512,256]{2,1,0:T(8,128)(2,1)}) %reduce-scatter.47.cloned.1.call-update) | async-done | bytes 524304 | tf_op jit(solution)/shard_map/reduce_scatter | solution.py:340
  1411.7 46.9 %reduce-scatter.45.cloned.1.call-done = bf16[2,1024,256]{2,1,0:T(8,128)(2,1)} async-done(((bf16[2,1024,1024]{2,1,0:T(8,128)(2,1)}), bf16[2,1024,256]{2,1,0:T(8,128)(2,1)}) %reduce-scatter.45.cloned.1.call-update) | async-done | bytes 1048592 | tf_op jit(solution)/shard_map/reduce_scatter | solution.py:337
  1461.3 122.7 %all-reduce.3.cloned.1.call-done = f32[1,1024,32]{1,2,0:T(8,128)} async-done(((f32[1,1024,32]{1,2,0:T(8,128)}), f32[1,1024,32]{1,2,0:T(8,128)}) %all-reduce.3.cloned.1.call-update) | async-done | bytes 131088 | tf_op jit(solution)/shard_map/psum | solution.py:335
  (1572 shorter events, 710.2 us)
Async XLA Ops:
  7.2 67.2 %reduce-scatter.17.cloned.1.call-start = ((), (), s32[]{:S(2)}) async-start(), calls=%async_computation.36 | async-start | bytes 327680 | tf_op jit(solution)/shard_map/reduce_scatter | solution.py:123
  36.8 155.9 %copy-start.278 = (s32[1,32,8]{1,2,0:T(8,128)}, s32[1,32,8]{1,2,0:T(8,128)S(1)}, u32[]{:S(2)}) copy-start(s32[1,32,8]{1,2,0:T(8,128)S(1)} %get-tuple-element.184) | copy-start | bytes 3076
  81.5 21.3 %all-to-all-start = ((bf16[32,16,1024]{2,1,0:T(8,128)(2,1)}), bf16[32,16,1024]{2,1,0:T(8,128)(2,1)}, u32[]{:S(2)}, u32[]{:S(2)}) async-start(bf16[32,16,1024]{2,1,0:T(8,128)(2,1)} %broadcast_select_fusion.14), calls=%async_computation.1 | async-start | bytes 2097152 | tf_op jit(solution)/shard_map/all_to_all | solution.py:139
  113.3 17.3 %all-to-all-start.1 = ((bf16[2,256,1024]{2,0,1:T(2,128)(2,1)}), bf16[2,256,1024]{2,0,1:T(2,128)(2,1)}, u32[]{:S(2)}, u32[]{:S(2)}) async-start(bf16[2,256,1024]{2,0,1:T(2,128)(2,1)} %copy.344), calls=%async_computation.2 | async-start | bytes 2097152 | tf_op jit(solution)/shard_map/all_to_all | solution.py:147
  118.8 59.7 %reduce-scatter.19.cloned.1.call-start = ((), (), s32[]{:S(2)}) async-start(), calls=%async_computation.37 | async-start | bytes 327680 | tf_op jit(solution)/shard_map/reduce_scatter | solution.py:123
  138.4 8.4 collective-permute-start
  186.0 20.9 %all-to-all-start.2 = ((bf16[32,16,1024]{2,1,0:T(8,128)(2,1)}), bf16[32,16,1024]{2,1,0:T(8,128)(2,1)}, u32[]{:S(2)}, u32[]{:S(2)}) async-start(bf16[32,16,1024]{2,1,0:T(8,128)(2,1)} %broadcast_select_fusion.13), calls=%async_computation.4 | async-start | bytes 2097152 | tf_op jit(solution)/shard_map/all_to_all | solution.py:139
  217.0 17.2 %all-to-all-start.3 = ((bf16[2,256,1024]{2,0,1:T(2,128)(2,1)}), bf16[2,256,1024]{2,0,1:T(2,128)(2,1)}, u32[]{:S(2)}, u32[]{:S(2)}) async-start(bf16[2,256,1024]{2,0,1:T(2,128)(2,1)} %copy.354), calls=%async_computation.5 | async-start | bytes 2097152 | tf_op jit(solution)/shard_map/all_to_all | solution.py:147
  250.7 22.0 %all-to-all-start.10 = ((bf16[32,16,1024]{2,1,0:T(8,128)(2,1)}), bf16[32,16,1024]{2,1,0:T(8,128)(2,1)}, u32[]{:S(2)}, u32[]{:S(2)}) async-start(bf16[32,16,1024]{2,1,0:T(8,128)(2,1)} %broadcast_select_fusion.9), calls=%async_computation.15 | async-start | bytes 2097152 | tf_op jit(solution)/shard_map/all_to_all | solution.py:214
  280.2 19.4 %all-to-all-start.11 = ((bf16[2,256,1024]{2,0,1:T(2,128)(2,1)}), bf16[2,256,1024]{2,0,1:T(2,128)(2,1)}, u32[]{:S(2)}, u32[]{:S(2)}) async-start(bf16[2,256,1024]{2,0,1:T(2,128)(2,1)} %copy.392), calls=%async_computation.16 | async-start | bytes 2097152 | tf_op jit(solution)/shard_map/all_to_all | solution.py:231
  285.3 64.9 %reduce-scatter.27.cloned.1.call-start = ((), (), s32[]{:S(2)}) async-start(), calls=%async_computation.41 | async-start | bytes 327680 | tf_op jit(solution)/shard_map/reduce_scatter | solution.py:295
  328.5 62.5 %reduce-scatter.21.cloned.1.call-start = ((), (), s32[]{:S(2)}) async-start(), calls=%async_computation.38 | async-start | bytes 327680 | tf_op jit(solution)/shard_map/reduce_scatter | solution.py:123
  331.5 9.2 collective-permute-start.1
  366.3 133.6 %copy-start.303 = (f32[2,2,128]{2,1,0:T(2,128)}, f32[2,2,128]{2,1,0:T(2,128)S(1)}, u32[]{:S(2)}) copy-start(f32[2,2,128]{2,1,0:T(2,128)S(1)} %get-tuple-element.258) | copy-start | bytes 6148
  397.9 21.1 %all-to-all-start.4 = ((bf16[32,16,1024]{2,1,0:T(8,128)(2,1)}), bf16[32,16,1024]{2,1,0:T(8,128)(2,1)}, u32[]{:S(2)}, u32[]{:S(2)}) async-start(bf16[32,16,1024]{2,1,0:T(8,128)(2,1)} %broadcast_select_fusion.12), calls=%async_computation.7 | async-start | bytes 2097152 | tf_op jit(solution)/shard_map/all_to_all | solution.py:139
  406.6 28.7 %collective-permute-start.4 = (bf16[32,1024]{1,0:T(8,128)(2,1)}, bf16[32,1024]{1,0:T(8,128)(2,1)}, u32[]{:S(2)}, u32[]{:S(2)}) collective-permute-start(bf16[32,1024]{1,0:T(8,128)(2,1)} %get-tuple-element.98), channel_id=1, source_target_pairs={{64,0},{65,1},{66,2},{67,3},{68,4},{69,5},{70,6},{71,7},{72,8},{73... | collective-permute-start | bytes 196616 | tf_op jit(solution)/shard_map/ppermute | solution.py:22
  429.1 16.8 %all-to-all-start.5 = ((bf16[2,256,1024]{2,0,1:T(2,128)(2,1)}), bf16[2,256,1024]{2,0,1:T(2,128)(2,1)}, u32[]{:S(2)}, u32[]{:S(2)}) async-start(bf16[2,256,1024]{2,0,1:T(2,128)(2,1)} %copy.364), calls=%async_computation.8 | async-start | bytes 2097152 | tf_op jit(solution)/shard_map/all_to_all | solution.py:147
  463.7 19.3 %all-to-all-start.12 = ((bf16[32,16,1024]{2,1,0:T(8,128)(2,1)}), bf16[32,16,1024]{2,1,0:T(8,128)(2,1)}, u32[]{:S(2)}, u32[]{:S(2)}) async-start(bf16[32,16,1024]{2,1,0:T(8,128)(2,1)} %broadcast_select_fusion.3), calls=%async_computation.18 | async-start | bytes 2097152 | tf_op jit(solution)/shard_map/all_to_all | solution.py:214
  490.5 22.1 %all-to-all-start.13 = ((bf16[2,256,1024]{2,0,1:T(2,128)(2,1)}), bf16[2,256,1024]{2,0,1:T(2,128)(2,1)}, u32[]{:S(2)}, u32[]{:S(2)}) async-start(bf16[2,256,1024]{2,0,1:T(2,128)(2,1)} %copy.405), calls=%async_computation.19 | async-start | bytes 2097152 | tf_op jit(solution)/shard_map/all_to_all | solution.py:231
  498.3 63.8 %reduce-scatter.29.cloned.1.call-start = ((), (), s32[]{:S(2)}) async-start(), calls=%async_computation.42 | async-start | bytes 327680 | tf_op jit(solution)/shard_map/reduce_scatter | solution.py:295
  540.2 62.7 %reduce-scatter.23.cloned.1.call-start = ((), (), s32[]{:S(2)}) async-start(), calls=%async_computation.39 | async-start | bytes 327680 | tf_op jit(solution)/shard_map/reduce_scatter | solution.py:123
  542.5 8.8 collective-permute-start.2
  609.9 21.0 %all-to-all-start.6 = ((bf16[32,16,1024]{2,1,0:T(8,128)(2,1)}), bf16[32,16,1024]{2,1,0:T(8,128)(2,1)}, u32[]{:S(2)}, u32[]{:S(2)}) async-start(bf16[32,16,1024]{2,1,0:T(8,128)(2,1)} %broadcast_select_fusion.11), calls=%async_computation.10 | async-start | bytes 2097152 | tf_op jit(solution)/shard_map/all_to_all | solution.py:139
  624.8 24.8 %collective-permute-start.5 = (bf16[32,1024]{1,0:T(8,128)(2,1)}, bf16[32,1024]{1,0:T(8,128)(2,1)}, u32[]{:S(2)}, u32[]{:S(2)}) collective-permute-start(bf16[32,1024]{1,0:T(8,128)(2,1)} %convert_element_type.1007), channel_id=1, source_target_pairs={{64,0},{65,1},{66,2},{67,3},{68,4},{69,5},{70,6},{71,7},{72,8},{73... | collective-permute-start | bytes 196616 | tf_op jit(solution)/shard_map/ppermute | solution.py:22
  641.3 22.2 %all-to-all-start.7 = ((bf16[2,256,1024]{2,0,1:T(2,128)(2,1)}), bf16[2,256,1024]{2,0,1:T(2,128)(2,1)}, u32[]{:S(2)}, u32[]{:S(2)}) async-start(bf16[2,256,1024]{2,0,1:T(2,128)(2,1)} %copy.374), calls=%async_computation.11 | async-start | bytes 2097152 | tf_op jit(solution)/shard_map/all_to_all | solution.py:147
  648.3 67.0 %reduce-scatter.25.cloned.1.call-start = ((), (), s32[]{:S(2)}) async-start(), calls=%async_computation.40 | async-start | bytes 327680 | tf_op jit(solution)/shard_map/reduce_scatter | solution.py:123
  672.9 5.8 collective-permute-start.3
  702.2 19.9 %all-to-all-start.14 = ((bf16[32,16,1024]{2,1,0:T(8,128)(2,1)}), bf16[32,16,1024]{2,1,0:T(8,128)(2,1)}, u32[]{:S(2)}, u32[]{:S(2)}) async-start(bf16[32,16,1024]{2,1,0:T(8,128)(2,1)} %broadcast_select_fusion.2), calls=%async_computation.21 | async-start | bytes 2097152 | tf_op jit(solution)/shard_map/all_to_all | solution.py:214
  722.1 21.3 %all-to-all-start.8 = ((bf16[32,16,1024]{2,1,0:T(8,128)(2,1)}), bf16[32,16,1024]{2,1,0:T(8,128)(2,1)}, u32[]{:S(2)}, u32[]{:S(2)}) async-start(bf16[32,16,1024]{2,1,0:T(8,128)(2,1)} %broadcast_select_fusion.10), calls=%async_computation.13 | async-start | bytes 2097152 | tf_op jit(solution)/shard_map/all_to_all | solution.py:139
  758.0 17.2 %all-to-all-start.15 = ((bf16[2,256,1024]{2,0,1:T(2,128)(2,1)}), bf16[2,256,1024]{2,0,1:T(2,128)(2,1)}, u32[]{:S(2)}, u32[]{:S(2)}) async-start(bf16[2,256,1024]{2,0,1:T(2,128)(2,1)} %copy.418), calls=%async_computation.22 | async-start | bytes 2097152 | tf_op jit(solution)/shard_map/all_to_all | solution.py:231
  763.1 64.5 %reduce-scatter.31.cloned.1.call-start = ((), (), s32[]{:S(2)}) async-start(), calls=%async_computation.43 | async-start | bytes 327680 | tf_op jit(solution)/shard_map/reduce_scatter | solution.py:295
  807.8 29.4 %all-to-all-start.9 = ((bf16[2,256,1024]{2,0,1:T(2,128)(2,1)}), bf16[2,256,1024]{2,0,1:T(2,128)(2,1)}, u32[]{:S(2)}, u32[]{:S(2)}) async-start(bf16[2,256,1024]{2,0,1:T(2,128)(2,1)} %copy.384), calls=%async_computation.14 | async-start | bytes 2097152 | tf_op jit(solution)/shard_map/all_to_all | solution.py:147
  830.8 12.8 collective-permute-start.6
  854.7 23.2 %all-to-all-start.16 = ((bf16[32,16,1024]{2,1,0:T(8,128)(2,1)}), bf16[32,16,1024]{2,1,0:T(8,128)(2,1)}, u32[]{:S(2)}, u32[]{:S(2)}) async-start(bf16[32,16,1024]{2,1,0:T(8,128)(2,1)} %broadcast_select_fusion.1), calls=%async_computation.24 | async-start | bytes 2097152 | tf_op jit(solution)/shard_map/all_to_all | solution.py:214
  885.6 21.6 %all-to-all-start.17 = ((bf16[2,256,1024]{2,0,1:T(2,128)(2,1)}), bf16[2,256,1024]{2,0,1:T(2,128)(2,1)}, u32[]{:S(2)}, u32[]{:S(2)}) async-start(bf16[2,256,1024]{2,0,1:T(2,128)(2,1)} %copy.431), calls=%async_computation.25 | async-start | bytes 2097152 | tf_op jit(solution)/shard_map/all_to_all | solution.py:231
  889.9 64.1 %reduce-scatter.33.cloned.1.call-start = ((), (), s32[]{:S(2)}) async-start(), calls=%async_computation.44 | async-start | bytes 327680 | tf_op jit(solution)/shard_map/reduce_scatter | solution.py:295
  957.5 6.6 collective-permute-start.7
  974.0 25.3 %all-to-all-start.18 = ((bf16[32,16,1024]{2,1,0:T(8,128)(2,1)}), bf16[32,16,1024]{2,1,0:T(8,128)(2,1)}, u32[]{:S(2)}, u32[]{:S(2)}) async-start(bf16[32,16,1024]{2,1,0:T(8,128)(2,1)} %broadcast_select_fusion), calls=%async_computation.27 | async-start | bytes 2097152 | tf_op jit(solution)/shard_map/all_to_all | solution.py:214
  1006.8 20.1 %all-to-all-start.19 = ((bf16[2,256,1024]{2,0,1:T(2,128)(2,1)}), bf16[2,256,1024]{2,0,1:T(2,128)(2,1)}, u32[]{:S(2)}, u32[]{:S(2)}) async-start(bf16[2,256,1024]{2,0,1:T(2,128)(2,1)} %copy.444), calls=%async_computation.28 | async-start | bytes 2097152 | tf_op jit(solution)/shard_map/all_to_all | solution.py:231
  1011.3 114.5 %reduce-scatter.35.cloned.1.call-start = ((), (), s32[]{:S(2)}) async-start(), calls=%async_computation.45 | async-start | bytes 327680 | tf_op jit(solution)/shard_map/reduce_scatter | solution.py:295
  1055.6 225.0 %reduce-scatter.41.cloned.1.call-start = ((), (), s32[]{:S(2)}) async-start(), calls=%async_computation.48 | async-start | bytes 278528 | tf_op jit(solution)/shard_map/reduce_scatter | solution.py:328
  1058.3 223.6 %reduce-scatter.39.cloned.1.call-start = ((), (), s32[]{:S(2)}) async-start(), calls=%async_computation.47 | async-start | bytes 278528 | tf_op jit(solution)/shard_map/reduce_scatter | solution.py:325
  1061.0 239.6 %reduce-scatter.43.cloned.1.call-start = ((), (), s32[]{:S(2)}) async-start(), calls=%async_computation.49 | async-start | bytes 557056 | tf_op jit(solution)/shard_map/reduce_scatter | solution.py:331
  1065.0 311.2 %reduce-scatter.37.cloned.1.call-start = ((), (), s32[]{:S(2)}) async-start(), calls=%async_computation.46 | async-start | bytes 557056 | tf_op jit(solution)/shard_map/reduce_scatter | solution.py:322
  1071.7 337.9 %reduce-scatter.47.cloned.1.call-start = ((), (), s32[]{:S(2)}) async-start(), calls=%async_computation.52 | async-start | bytes 2621440 | tf_op jit(solution)/shard_map/reduce_scatter | solution.py:340
  1081.5 377.0 %reduce-scatter.45.cloned.1.call-start = ((), (), s32[]{:S(2)}) async-start(), calls=%async_computation.51 | async-start | bytes 5242880 | tf_op jit(solution)/shard_map/reduce_scatter | solution.py:337
  1117.9 159.8 %copy-start.167 = (f32[32,1024]{1,0:T(8,128)S(1)}, f32[32,1024]{1,0:T(8,128)}, u32[]{:S(2)}) copy-start(f32[32,1024]{1,0:T(8,128)} %copy-done.166) | copy-start | bytes 393220
  1117.9 466.1 %all-reduce.3.cloned.1.call-start = ((), (), s32[]{:S(2)}) async-start(), calls=%async_computation.50 | async-start | bytes 262144 | tf_op jit(solution)/shard_map/psum | solution.py:335
  (424 other events, 3445.2 us)
Sparse Core Ops, SparseCore 0:
  35.4 22.4 reduce-scatter.16
  161.3 17.1 reduce-scatter.18
  328.6 21.5 reduce-scatter.26
  368.3 22.6 reduce-scatter.20
  540.3 21.7 reduce-scatter.28
  580.2 22.6 reduce-scatter.22
  696.0 19.1 reduce-scatter.24
  804.1 23.4 reduce-scatter.30
  937.9 16.0 reduce-scatter.32
  1055.7 19.5 reduce-scatter.34
  1078.5 72.3 reduce-scatter.40
  1154.3 71.2 reduce-scatter.38
  1228.8 71.6 reduce-scatter.42
  1304.5 71.6 reduce-scatter.36
  1379.0 30.5 reduce-scatter.46
  1412.0 46.5 reduce-scatter.44
  1463.1 120.8 all-reduce.2
where the time goes:
time: 1610 us; the launch traced here: 1590 us
  waiting for transfers between devices  570 us (35%)
  blocking collectives  249 us (15%)
  local copies, waits for them, and re-layouts  212 us (13%)
  other arithmetic  206 us (13%)
  matrix products  186 us (12%)
  starting transfers between devices  150 us (9%)
  between operations  20.1 us (1%)
    psum x1, blocking collectives, settle(): small_totals = lax.psum(small_parts, ('exp', 'tp'))  150 us
    psum x1, waiting for transfers between devices, settle(): small_totals = lax.psum(small_parts, ('exp', 'tp'))  123 us
    reduce_scatter x1, waiting for transfers between devices, settle(): lax.psum_scatter(attention_parts[0].astype(jnp.bfloat16), 'exp', scatter_...  74.2 us
    reduce_scatter x5, waiting for transfers between devices, layer_forward(): lax.psum_scatter(jnp.dot(attended, output_weight, preferred_element_type=...  60.6 us
    all_gather x5, blocking collectives, layer_forward(): rows_all = lax.all_gather(normed, 'tp', axis=0, tiled=True)  50.1 us
    all_gather x5, blocking collectives, layer_backward(): lax.all_gather(grad_after.astype(jnp.bfloat16), 'tp', axis=0, tiled=True)  48.4 us
    all_to_all x5, waiting for transfers between devices, layer_backward(): lax.all_to_all(grad_incoming, 'exp', split_axis=1, concat_axis=0, tiled=T...  47.6 us
    reduce_scatter x5, waiting for transfers between devices, layer_backward(): lax.psum_scatter((jnp.einsum('rc,dc->rd', grad_queries, query_weight, pre...  47.2 us
  transfers between devices with their start and end apart: 45, of which 34 were waited for; matrix products, arithmetic and copies ran while one was open for 18% of the time, Pallas kernels for 0%

commit v1 on v0

v1 whole, which is shorter than its diff:
```python
import functools

import jax
import jax.numpy as jnp
from jax import lax
from jax.experimental import pallas as pl
from jax.experimental.pallas import tpu as pltpu
from jax.sharding import PartitionSpec as P

D = 1024
HD = 64
E = 32
F = 512
LANES = 128
EPSILON = 1e-06
ROPE_BASE = 10000.0
SCORE_SCALE = 0.125
MASKED = -1e30
MESH = pl.DeviceIdType.MESH
VMEM_LIMIT = 56 * 1024 * 1024
BF16 = jnp.bfloat16
F32 = jnp.float32


def dot(a, b):
    return jnp.dot(a, b, preferred_element_type=F32)


def dot_nt(a, b):
    return lax.dot_general(a, b, (((1,), (1,)), ((), ())), preferred_element_type=F32)


def dot_tn(a, b):
    return lax.dot_general(a, b, (((0,), (0,)), ((), ())), preferred_element_type=F32)


def in_vmem():
    return pl.BlockSpec(memory_space=pltpu.VMEM)


def in_any():
    return pl.BlockSpec(memory_space=pl.ANY)


def greet(peers):
    barrier = pltpu.get_barrier_semaphore()
    for peer in peers:
        pl.semaphore_signal(barrier, inc=1, device_id=peer, device_id_type=MESH)
    pl.semaphore_wait(barrier, len(peers))


def remote(src, dst, send_sem, recv_sem, peer):
    return pltpu.make_async_remote_copy(
        src_ref=src,
        dst_ref=dst,
        send_sem=send_sem,
        recv_sem=recv_sem,
        device_id=peer,
        device_id_type=MESH,
    )


def comm_params(number):
    return pltpu.CompilerParams(
        collective_id=number, has_side_effects=True, vmem_limit_bytes=VMEM_LIMIT
    )


def pair_kernel(count, *refs):
    ins, outs = refs[:count], refs[count : 2 * count]
    send_sem, recv_sem, own_sem = refs[2 * count :]
    me = lax.axis_index("section")
    peer = {"section": 1 - me}
    greet([peer])
    sends, owns = [], []
    for at in range(count):
        sends.append(
            remote(ins[at].at[0], outs[at].at[me], send_sem.at[at], recv_sem.at[at], peer)
        )
        owns.append(pltpu.make_async_copy(ins[at].at[0], outs[at].at[me], own_sem.at[at]))
        sends[-1].start()
        owns[-1].start()
    for at in range(count):
        owns[at].wait()
        sends[at].wait()


def pair_gather(arrays, number):
    count = len(arrays)
    return pl.pallas_call(
        functools.partial(pair_kernel, count),
        out_shape=[jax.ShapeDtypeStruct((2,) + a.shape[1:], a.dtype) for a in arrays],
        in_specs=[in_any()] * count,
        out_specs=[in_any()] * count,
        scratch_shapes=[pltpu.SemaphoreType.DMA((count,))] * 3,
        compiler_params=comm_params(number),
        name="pair_gather%d" % number,
    )(*arrays)


def tp_gather_kernel(x_ref, out_ref, send_sem, recv_sem):
    me = lax.axis_index("tp")
    peers = [{"tp": lax.rem(me + j, 4)} for j in (1, 2, 3)]
    greet(peers)
    mine = pl.ds(pl.multiple_of(me * 32, 32), 32)
    copies = [
        remote(x_ref, out_ref.at[:, mine], send_sem.at[j], recv_sem.at[j], peers[j])
        for j in range(3)
    ]
    for copy in copies:
        copy.start()
    out_ref[:, mine] = x_ref[...]
    for copy in copies:
        copy.wait()


def tp_gather(x):
    return pl.pallas_call(
        tp_gather_kernel,
        out_shape=jax.ShapeDtypeStruct((2, 128, D), BF16),
        in_specs=[in_vmem()],
        out_specs=in_vmem(),
        scratch_shapes=[pltpu.SemaphoreType.DMA((3,))] * 2,
        compiler_params=comm_params(2),
        name="tp_gather",
    )(x)


def tp_scatter_kernel(x_ref, out_ref, held, send_sem, recv_sem):
    me = lax.axis_index("tp")
    places = [lax.rem(me + j, 4) for j in (1, 2, 3)]
    greet([{"tp": place} for place in places])
    copies = []
    for j in range(3):
        theirs = pl.ds(pl.multiple_of(places[j] * 32, 32), 32)
        copies.append(
            remote(
                x_ref.at[:, theirs], held.at[j], send_sem.at[j], recv_sem.at[j], {"tp": places[j]}
            )
        )
        copies[-1].start()
    total = x_ref[:, pl.ds(pl.multiple_of(me * 32, 32), 32)].astype(F32)
    for j in range(3):
        copies[j].wait_recv()
        total = total + held[j].astype(F32)
    out_ref[...] = total
    for copy in copies:
        copy.wait_send()


def tp_scatter(x):
    return pl.pallas_call(
        tp_scatter_kernel,
        out_shape=jax.ShapeDtypeStruct((2, 32, D), F32),
        in_specs=[in_vmem()],
        out_specs=in_vmem(),
        scratch_shapes=[pltpu.VMEM((3, 2, 32, D), BF16)] + [pltpu.SemaphoreType.DMA((3,))] * 2,
        compiler_params=comm_params(3),
        name="tp_scatter",
    )(x)


def exp_places():
    me = lax.axis_index("exp")
    at_x, at_z = me // 4, lax.rem(me, 4)
    return me, at_x, at_z


def exp_gather_kernel(x_ref, out_ref, send_one, recv_one, send_two, recv_two):
    me, at_x, at_z = exp_places()

    def place(by_x, by_z):
        return lax.rem(at_x + by_x, 4) * 4 + lax.rem(at_z + by_z, 4)

    peers = [[{"exp": place(j, 0)} for j in (1, 2, 3)], [{"exp": place(0, j)} for j in (1, 2, 3)]]
    greet(peers[0] + peers[1])
    rows = [pl.ds(0, 32), pl.ds(32, 32)]
    first = [[], []]
    second = [[], []]
    for j in range(3):
        for half in range(2):
            copy = remote(
                x_ref.at[rows[half]],
                out_ref.at[me, rows[half]],
                send_one.at[half, j],
                recv_one.at[half, j],
                peers[half][j],
            )
            copy.start()
            first[half].append(copy)
    for j in range(3):
        for half in range(2):
            copy = remote(
                x_ref.at[rows[half]],
                out_ref.at[me, rows[half]],
                send_two.at[half, 0, j],
                recv_two.at[half, 0, j],
                peers[1 - half][j],
            )
            copy.start()
            second[half].append(copy)
    out_ref[me] = x_ref[...]
    for back in range(1, 4):
        for half in range(2):
            first[half][back - 1].wait_recv()
            origin = place(4 - back, 0) if half == 0 else place(0, 4 - back)
            for j in range(3):
                copy = remote(
                    out_ref.at[origin, rows[half]],
                    out_ref.at[origin, rows[half]],
                    send_two.at[half, back, j],
                    recv_two.at[half, back, j],
                    peers[1 - half][j],
                )
                copy.start()
                second[half].append(copy)
    for half in range(2):
        for copy in first[half]:
            copy.wait_send()
        for copy in second[half]:
            copy.wait()


def exp_gather(x):
    return pl.pallas_call(
        exp_gather_kernel,
        out_shape=jax.ShapeDtypeStruct((16, 64, D), BF16),
        in_specs=[in_vmem()],
        out_specs=in_vmem(),
        scratch_shapes=[
            pltpu.SemaphoreType.DMA((2, 3)),
            pltpu.SemaphoreType.DMA((2, 3)),
            pltpu.SemaphoreType.DMA((2, 4, 3)),
            pltpu.SemaphoreType.DMA((2, 4, 3)),
        ],
        compiler_params=comm_params(4),
        name="exp_gather",
    )(x)


def exp_scatter_kernel(
    x_ref, out_ref, held_one, ready, held_two, send_one, recv_one, send_two, recv_two
):
    me, at_x, at_z = exp_places()
    to_x = [lax.rem(at_x + j, 4) for j in (1, 2, 3)]
    to_z = [lax.rem(at_z + j, 4) for j in (1, 2, 3)]
    peers = [[{"exp": x * 4 + at_z} for x in to_x], [{"exp": at_x * 4 + z} for z in to_z]]
    greet(peers[0] + peers[1])
    rows = [pl.ds(0, 32), pl.ds(32, 32)]
    first = [[], []]
    second = [[], []]
    for j in range(3):
        for half in range(2):
            src = (
                x_ref.at[to_x[j], :, rows[0]] if half == 0 else x_ref.at[:, to_z[j], rows[1]]
            )
            copy = remote(
                src, held_one.at[half, j], send_one.at[half, j], recv_one.at[half, j], peers[half][j]
            )
            copy.start()
            first[half].append(copy)
    for half in range(2):
        for j in range(3):
            first[half][j].wait_recv()
        for j in range(3):
            to = to_z[j] if half == 0 else to_x[j]
            own = x_ref[at_x, to, rows[0]] if half == 0 else x_ref[to, at_z, rows[1]]
            total = own.astype(F32)
            for k in range(3):
                total = total + held_one[half, k, to].astype(F32)
            ready[half, j] = total.astype(BF16)
            copy = remote(
                ready.at[half, j],
                held_two.at[half, j],
                send_two.at[half, j],
                recv_two.at[half, j],
                peers[1 - half][j],
            )
            copy.start()
            second[half].append(copy)
    for half in range(2):
        total = x_ref[at_x, at_z, rows[half]].astype(F32)
        mine = at_z if half == 0 else at_x
        for k in range(3):
            total = total + held_one[half, k, mine].astype(F32)
        for k in range(3):
            second[half][k].wait_recv()
            total = total + held_two[half, k].astype(F32)
        out_ref[rows[half]] = total
    for half in range(2):
        for copy in first[half] + second[half]:
            copy.wait_send()


def exp_scatter(x, number):
    width = x.shape[-1]
    return pl.pallas_call(
        exp_scatter_kernel,
        out_shape=jax.ShapeDtypeStruct((64, width), F32),
        in_specs=[in_vmem()],
        out_specs=in_vmem(),
        scratch_shapes=[
            pltpu.VMEM((2, 3, 4, 32, width), BF16),
            pltpu.VMEM((2, 3, 32, width), BF16),
            pltpu.VMEM((2, 3, 32, width), BF16),
        ]
        + [pltpu.SemaphoreType.DMA((2, 3))] * 4,
        compiler_params=comm_params(number),
        name="exp_scatter%d" % number,
    )(x.reshape(4, 4, 64, width))


def half_swapped(values):
    width = values.shape[1]
    lane = lax.broadcasted_iota(jnp.int32, values.shape, 1)
    ahead = pltpu.roll(values, width - 32, 1)
    behind = pltpu.roll(values, 32, 1)
    return jnp.where(lax.rem(lane, 64) < 32, ahead, behind)


def three(table):
    return jnp.concatenate([table, table, table], axis=1)


def head(values, batch, first):
    return values[batch * 128 : batch * 128 + 128, first : first + HD]


def attention_forward_kernel(
    rows_ref, wqkv_ref, wo_ref, cos_ref, sin_ref, mask_ref, part_ref, qkv_ref, att_ref
):
    joined = dot(rows_ref[...], wqkv_ref[0])
    turned = joined[:, :384]
    turned = turned * three(cos_ref[...]) + half_swapped(turned) * three(sin_ref[...])
    qkv = jnp.concatenate([turned, joined[:, 384:]], axis=1).astype(BF16)
    qkv_ref[...] = qkv
    for batch in range(2):
        allowed = mask_ref[batch] > 0.5
        outs = []
        for h in range(4):
            q = head(qkv, batch, h * HD)
            k = head(qkv, batch, 256 + (h // 2) * HD)
            v = head(qkv, batch, 384 + (h // 2) * HD)
            scores = jnp.where(allowed, dot_nt(q, k) * SCORE_SCALE, MASKED)
            lifted = jnp.exp(scores - jnp.max(scores, axis=1, keepdims=True))
            share = lifted / jnp.sum(lifted, axis=1, keepdims=True)
            outs.append(dot(share.astype(BF16), v))
        attended = jnp.concatenate(outs, axis=1).astype(BF16)
        att_ref[batch * 128 : batch * 128 + 128] = attended
        part_ref[batch] = dot(attended, wo_ref[0]).astype(BF16)


def layer_block(shape, layer):
    return pl.BlockSpec((1,) + shape, lambda i: (layer,) + (0,) * len(shape))


def whole(*shape):
    return pl.BlockSpec(shape, lambda i: (0,) * len(shape))


def local_params():
    return pltpu.CompilerParams(vmem_limit_bytes=VMEM_LIMIT)


def attention_forward(rows, wqkv, wo, tables, layer):
    cosine, sine, mask = tables
    return pl.pallas_call(
        attention_forward_kernel,
        grid=(1,),
        out_shape=[
            jax.ShapeDtypeStruct((2, 128, D), BF16),
            jax.ShapeDtypeStruct((256, 512), BF16),
            jax.ShapeDtypeStruct((256, 256), BF16),
        ],
        in_specs=[
            whole(256, D),
            layer_block((D, 512), layer),
            layer_block((256, D), layer),
            whole(256, LANES),
            whole(256, LANES),
            whole(2, 128, 128),
        ],
        out_specs=[whole(2, 128, D), whole(256, 512), whole(256, 256)],
        compiler_params=local_params(),
        name="attention_forward",
    )(rows, wqkv, wo, cosine, sine, mask)


def attention_backward_kernel(
    rows_ref,
    ga_ref,
    qkv_ref,
    att_ref,
    wqkv_ref,
    wo_ref,
    cos_ref,
    sin_ref,
    mask_ref,
    dn_ref,
    dw_ref,
):
    ga = ga_ref[...]
    rows = rows_ref[...]
    dw_ref[:, 512:] = dot_tn(ga, att_ref[...]).astype(BF16)
    gatt = dot_nt(ga, wo_ref[0]).astype(BF16)
    qkv = qkv_ref[...]
    by_batch = []
    for batch in range(2):
        allowed = mask_ref[batch] > 0.5
        gqs, gks, gvs = [], [None, None], [None, None]
        for h in range(4):
            kv = h // 2
            q = head(qkv, batch, h * HD)
            k = head(qkv, batch, 256 + kv * HD)
            v = head(qkv, batch, 384 + kv * HD)
            go = head(gatt, batch, h * HD)
            scores = jnp.where(allowed, dot_nt(q, k) * SCORE_SCALE, MASKED)
            lifted = jnp.exp(scores - jnp.max(scores, axis=1, keepdims=True))
            share = lifted / jnp.sum(lifted, axis=1, keepdims=True)
            gp = dot_nt(go, v)
            gs = share * (gp - jnp.sum(share * gp, axis=1, keepdims=True))
            gs = gs.astype(BF16)
            gqs.append(dot(gs, k) * SCORE_SCALE)
            gk = dot_tn(gs, q) * SCORE_SCALE
            gv = dot_tn(share.astype(BF16), go)
            gks[kv] = gk if gks[kv] is None else gks[kv] + gk
            gvs[kv] = gv if gvs[kv] is None else gvs[kv] + gv
        by_batch.append(jnp.concatenate(gqs + gks + gvs, axis=1))
    joined = jnp.concatenate(by_batch, axis=0)
    turned = joined[:, :384]
    turned = turned * three(cos_ref[...]) - half_swapped(turned) * three(sin_ref[...])
    gqkv = jnp.concatenate([turned, joined[:, 384:]], axis=1).astype(BF16)
    dw_ref[:, :512] = dot_tn(rows, gqkv).astype(BF16)
    dn = dot_nt(gqkv, wqkv_ref[0]).astype(BF16)
    dn_ref[0] = dn[:128]
    dn_ref[1] = dn[128:]


def attention_backward(rows, ga, qkv, att, wqkv, wo, tables, layer):
    cosine, sine, mask = tables
    return pl.pallas_call(
        attention_backward_kernel,
        grid=(1,),
        out_shape=[
            jax.ShapeDtypeStruct((2, 128, D), BF16),
            jax.ShapeDtypeStruct((D, 768), BF16),
        ],
        in_specs=[
            whole(256, D),
            whole(256, D),
            whole(256, 512),
            whole(256, 256),
            layer_block((D, 512), layer),
            layer_block((256, D), layer),
            whole(256, LANES),
            whole(256, LANES),
            whole(2, 128, 128),
        ],
        out_specs=[whole(2, 128, D), whole(D, 768)],
        compiler_params=local_params(),
        name="attention_backward",
    )(rows, ga, qkv, att, wqkv, wo, cosine, sine, mask)


def masked_softmax(logits, mask):
    routed = mask > 0.5
    shown = jnp.where(routed, logits, MASKED)
    lifted = jnp.where(routed, jnp.exp(shown - jnp.max(shown, axis=1, keepdims=True)), 0.0)
    return lifted / jnp.sum(lifted, axis=1, keepdims=True)


def experts_forward_kernel(x_ref, wgu_ref, wd_ref, router_ref, mask_ref, sel_ref, y_ref, gu_ref):
    x = x_ref[...]
    gates = masked_softmax(dot(x, router_ref[0]), mask_ref[...])
    total = None
    for e in range(2):
        gate = jnp.sum(gates * sel_ref[e : e + 1], axis=1, keepdims=True)
        gu = dot(x, wgu_ref[0, e])
        gu_ref[e] = gu.astype(BF16)
        part, upper = gu[:, :F], gu[:, F:]
        hidden = part * jax.nn.sigmoid(part) * upper
        made = dot((hidden * gate).astype(BF16), wd_ref[0, e])
        total = made if total is None else total + made
    y_ref[...] = total.astype(BF16)


def experts_forward(x, wgu, wd, router, mask, sel, layer):
    count = x.shape[0]
    tile = 256
    return pl.pallas_call(
        experts_forward_kernel,
        grid=(count // tile,),
        out_shape=[
            jax.ShapeDtypeStruct((count, D), BF16),
            jax.ShapeDtypeStruct((2, count, 2 * F), BF16),
        ],
        in_specs=[
            pl.BlockSpec((tile, D), lambda i: (i, 0)),
            layer_block((2, D, 2 * F), layer),
            layer_block((2, F, D), layer),
            layer_block((D, LANES), layer),
            pl.BlockSpec((tile, LANES), lambda i: (i, 0)),
            whole(8, LANES),
        ],
        out_specs=[
            pl.BlockSpec((tile, D), lambda i: (i, 0)),
            pl.BlockSpec((2, tile, 2 * F), lambda i: (0, i, 0)),
        ],
        compiler_params=local_params(),
        name="experts_forward",
    )(x, wgu, wd, router, mask, sel)


def experts_backward_kernel(
    x_ref,
    g_ref,
    gu_ref,
    wgu_ref,
    wd_ref,
    router_ref,
    mask_ref,
    sel_ref,
    dx_ref,
    dgu_ref,
    dd_ref,
    dr_ref,
    gates,
    gl,
    gj,
    hs,
    dx_sum,
):
    e = pl.program_id(0)
    tile = 256
    tiles = x_ref.shape[0] // tile
    chosen = jnp.where(e == 0, sel_ref[0:1], sel_ref[1:2])

    @pl.when(e == 0)
    def _():
        @pl.loop(0, tiles)
        def _(i):
            r = pl.ds(pl.multiple_of(i * tile, tile), tile)
            gates[r] = masked_softmax(dot(x_ref[r], router_ref[0]), mask_ref[r])
            gl[r] = jnp.zeros((tile, LANES), F32)

    @pl.loop(0, tiles)
    def _(i):
        r = pl.ds(pl.multiple_of(i * tile, tile), tile)
        gate = jnp.sum(gates[r] * chosen, axis=1, keepdims=True)
        gh = dot_nt(g_ref[r], wd_ref[0, 0])
        part = gu_ref[0, r, :F].astype(F32)
        upper = gu_ref[0, r, F:].astype(F32)
        s = jax.nn.sigmoid(part)
        act = part * s
        hidden = act * upper
        gl[r] += (gate * jnp.sum(hidden * gh, axis=1, keepdims=True)) * chosen
        hs[r] = (hidden * gate).astype(BF16)
        gh = gh * gate
        gj[r, :F] = (gh * upper * (s + act * (1.0 - s))).astype(BF16)
        gj[r, F:] = (gh * act).astype(BF16)
        dx = dot_nt(gj[r], wgu_ref[0, 0])

        @pl.when(e == 0)
        def _():
            dx_sum[r] = dx

        @pl.when(e == 1)
        def _():
            dx_ref[r] = (dx_sum[r] + dx + dot_nt(gl[r].astype(BF16), router_ref[0])).astype(BF16)

    @pl.loop(0, D // 256)
    def _(i):
        c = pl.ds(pl.multiple_of(i * 256, 256), 256)
        dgu_ref[0, c] = dot_tn(x_ref[:, c], gj[...]).astype(BF16)

    @pl.loop(0, F // 256)
    def _(i):
        c = pl.ds(pl.multiple_of(i * 256, 256), 256)
        dd_ref[0, c] = dot_tn(hs[:, c], g_ref[...]).astype(BF16)

    @pl.when(e == 1)
    def _():
        dr_ref[...] = dot_tn(gl[...].astype(BF16), x_ref[...])[:E]


def experts_backward(x, g, gu, wgu, wd, router, mask, sel, layer):
    count = x.shape[0]
    return pl.pallas_call(
        experts_backward_kernel,
        grid=(2,),
        out_shape=[
            jax.ShapeDtypeStruct((count, D), BF16),
            jax.ShapeDtypeStruct((2, D, 2 * F), BF16),
            jax.ShapeDtypeStruct((2, F, D), BF16),
            jax.ShapeDtypeStruct((E, D), F32),
        ],
        in_specs=[
            whole(count, D),
            whole(count, D),
            pl.BlockSpec((1, count, 2 * F), lambda e: (e, 0, 0)),
            pl.BlockSpec((1, 1, D, 2 * F), lambda e: (layer, e, 0, 0)),
            pl.BlockSpec((1, 1, F, D), lambda e: (layer, e, 0, 0)),
            layer_block((D, LANES), layer),
            whole(count, LANES),
            whole(8, LANES),
        ],
        out_specs=[
            whole(count, D),
            pl.BlockSpec((1, D, 2 * F), lambda e: (e, 0, 0)),
            pl.BlockSpec((1, F, D), lambda e: (e, 0, 0)),
            whole(E, D),
        ],
        scratch_shapes=[
            pltpu.VMEM((count, LANES), F32),
            pltpu.VMEM((count, LANES), F32),
            pltpu.VMEM((count, 2 * F), BF16),
            pltpu.VMEM((count, F), BF16),
            pltpu.VMEM((count, D), F32),
        ],
        compiler_params=local_params(),
        name="experts_backward",
    )(x, g, gu, wgu, wd, router, mask, sel)


def inverse_rms(values):
    return lax.rsqrt(jnp.mean(values * values, axis=1, keepdims=True) + EPSILON)


def layer_forward(layer_in, layer, common, weights):
    tables, mask_own, mask_all, sel = common
    wqkv, wo, gains, router, wgu, wd = weights
    inverse_one = inverse_rms(layer_in)
    normed = (layer_in * inverse_one * gains[layer, 0:1]).astype(BF16)
    rows = tp_gather(normed.reshape(2, 32, D)).reshape(256, D)
    part, qkv, att = attention_forward(rows, wqkv, wo, tables, layer)
    after = layer_in + tp_scatter(part).reshape(64, D)
    inverse_two = inverse_rms(after)
    normed_two = (after * inverse_two * gains[layer, 1:2]).astype(BF16)
    x_all = exp_gather(normed_two).reshape(1024, D)
    made, gu = experts_forward(x_all, wgu, wd, router, mask_all, sel, layer)
    y = exp_scatter(made, 5)
    stored = (layer_in, inverse_one, rows, qkv, att, after, inverse_two, normed_two, x_all, gu, y)
    return after + y, stored


def layer_backward(grad, stored, layer, common, weights):
    tables, mask_own, mask_all, sel = common
    wqkv, wo, gains, router, wgu, wd = weights
    layer_in, inverse_one, rows, qkv, att, after, inverse_two, normed_two, x_all, gu, y = stored
    g_all = exp_gather(grad).reshape(1024, D)
    dx, dgu, dd, dr = experts_backward(x_all, g_all, gu, wgu, wd, router, mask_all, sel, layer)
    gates = masked_softmax(dot(normed_two, router[layer]), mask_own)
    gf = grad.astype(F32)
    gc = (gates * jnp.sum(gf * y, axis=1, keepdims=True)).astype(BF16)
    grad_n = exp_scatter(dx, 5) - dot_nt(gc, router[layer])
    dr = dr - dot_tn(gc, normed_two)[:E]
    scaled = grad_n * gains[layer, 1:2]
    grad_after = (
        gf
        + inverse_two * scaled
        - after * inverse_two**3 * jnp.mean(after * scaled, axis=1, keepdims=True)
    )
    d_mixture = jnp.sum(grad_n * after * inverse_two, axis=0, keepdims=True)
    ga = tp_gather(grad_after.astype(BF16).reshape(2, 32, D)).reshape(256, D)
    dn, dw = attention_backward(rows, ga, qkv, att, wqkv, wo, tables, layer)
    grad_n = tp_scatter(dn).reshape(64, D)
    scaled = grad_n * gains[layer, 0:1]
    grad_in = (
        grad_after
        + inverse_one * scaled
        - layer_in * inverse_one**3 * jnp.mean(layer_in * scaled, axis=1, keepdims=True)
    )
    d_attention = jnp.sum(grad_n * layer_in * inverse_one, axis=0, keepdims=True)
    small = jnp.concatenate([dr, d_attention, d_mixture, jnp.zeros((6, D), F32)], axis=0)
    return grad_in, (dgu, dd, dw, small)


def rope_tables(seg_rows):
    length = seg_rows.shape[0]
    before = jnp.sum((seg_rows[None, :] < seg_rows[:, None]).astype(jnp.int32), axis=1)
    places = (jnp.arange(length, dtype=jnp.int32) - before).astype(F32)
    powers = jnp.arange(0, HD, 2, dtype=jnp.int32).astype(F32) / HD
    angles = places[:, None] * (ROPE_BASE ** (-powers))[None, :]
    cosine, sine = jnp.cos(angles), jnp.sin(angles)
    indices = jnp.arange(length, dtype=jnp.int32)
    allowed = (seg_rows[:, None] == seg_rows[None, :]) & (indices[None, :] <= indices[:, None])
    return (
        jnp.concatenate([cosine] * 4, axis=1),
        jnp.concatenate([-sine, sine, -sine, sine], axis=1),
        allowed.astype(F32),
    )


def routed(routes):
    labels = jnp.arange(LANES, dtype=jnp.int32)
    return jnp.sum((routes[:, :, None] == labels[None, None, :]).astype(F32), axis=1)


def per_device(
    activations,
    cotangent,
    segments,
    routes,
    attention_gain,
    query_weight,
    key_weight,
    value_weight,
    output_weight,
    mixture_gain,
    router_weight,
    expert_gate_up,
    expert_down,
):
    section = lax.axis_index("section")
    expert = lax.axis_index("exp")

    def own_batches(array):
        return lax.dynamic_slice_in_dim(array, 2 * section, 2, 0)

    def to_owner(first, second):
        sent = jnp.where(section == 0, second, first)
        kept = jnp.where(section == 0, first, second)
        return kept, lax.ppermute(sent, "section", [(0, 1), (1, 0)])

    def by_layer(first, second):
        kept, got = to_owner(first, second)
        kept, got = kept.reshape(2, 32, D), got.reshape(2, 32, D)
        return jnp.where(
            section == 0,
            jnp.concatenate([kept, got], axis=0),
            jnp.concatenate([got, kept], axis=0),
        )[None]

    qkv_own = jnp.concatenate([query_weight, key_weight, value_weight], axis=2)
    gains_own = jnp.concatenate(
        [attention_gain, mixture_gain, jnp.zeros((6, D), BF16)], axis=0
    ).astype(F32)[None]
    router_own = jnp.pad(router_weight, ((0, 0), (0, 0), (0, LANES - E)))
    wqkv, wo, gains, router = pair_gather([qkv_own, output_weight, gains_own, router_own], 0)
    wgu, wd = pair_gather([expert_gate_up, expert_down], 1)
    weights = (wqkv, wo, gains, router, wgu, wd)

    cosine, sine, mask = jax.vmap(rope_tables)(own_batches(segments))
    tables = (cosine.reshape(256, LANES), sine.reshape(256, LANES), mask)
    routes_own = own_batches(routes).reshape(64, 8)
    routes_all = lax.all_gather(routes_own, "exp", axis=0, tiled=True)
    lanes = lax.broadcasted_iota(jnp.int32, (8, LANES), 1)
    sel = (lanes == 2 * expert + lax.broadcasted_iota(jnp.int32, (8, LANES), 0)).astype(F32)
    common = (tables, routed(routes_own), routed(routes_all), sel)

    start = own_batches(activations).reshape(64, D).astype(F32)
    result, kept_first = layer_forward(start, 0, common, weights)
    out_first = result.astype(BF16)
    result, kept_second = layer_forward(out_first.astype(F32), 1, common, weights)
    out_second = result.astype(BF16)
    grad = own_batches(cotangent).reshape(64, D)
    grad_second, pieces_second = layer_backward(grad, kept_second, 1, common, weights)
    grad_first, pieces_first = layer_backward(
        grad_second.astype(BF16), kept_first, 0, common, weights
    )

    def summed(first, second):
        kept, got = to_owner(first, second)
        return kept.astype(F32) + got.astype(F32)

    dgu, dd, dw, small = [summed(a, b) for a, b in zip(pieces_first, pieces_second)]
    dgu = lax.psum_scatter(dgu.astype(BF16), "tp", scatter_dimension=2, tiled=True)
    dd = lax.psum_scatter(dd.astype(BF16), "tp", scatter_dimension=2, tiled=True)
    dw = exp_scatter(dw.astype(BF16), 6)
    small = lax.psum(small, ("exp", "tp"))
    return (
        by_layer(out_first, out_second),
        by_layer(grad_first, grad_second),
        small[E : E + 1],
        dw[None, :, :256],
        dw[None, :, 256:384],
        dw[None, :, 384:512],
        dw[:, 512:].T[None],
        small[E + 1 : E + 2],
        small[:E].T[None],
        dgu.astype(F32)[None],
        dd.astype(F32)[None],
    )


def solution(mesh):
    placed = (
        P(None, ("exp", "tp"), None),
        P(None, ("exp", "tp"), None),
        P(None, "exp"),
        P(None, ("exp", "tp"), None),
        P("section", None),
        P("section", None, "tp"),
        P("section", None, "tp"),
        P("section", None, "tp"),
        P("section", "tp", None),
        P("section", None),
        P("section", None, None),
        P("section", "exp", None, None),
        P("section", "exp", None, None),
    )
    return jax.shard_map(
        per_device,
        mesh=mesh,
        in_specs=placed,
        out_specs=(
            P("section", None, ("exp", "tp"), None),
            P("section", None, ("exp", "tp"), None),
            P("section", None),
            P("section", "exp", "tp"),
            P("section", "exp", "tp"),
            P("section", "exp", "tp"),
            P("section", "tp", "exp"),
            P("section", None),
            P("section", None, None),
            P("section", "exp", None, "tp"),
            P("section", "exp", None, "tp"),
        ),
        check_vma=False,
    )
```

time: 1610 us -> 899 us (0.56)
  Pallas kernels: 0 us -> 636 us
  waiting for transfers between devices: 570 us -> 126 us
  blocking collectives: 249 us -> 20.3 us
  local copies, waits for them, and re-layouts: 212 us -> 12.9 us
  matrix products: 186 us -> 3.5 us
  other arithmetic: 206 us -> 63.2 us
  starting transfers between devices: 150 us -> 7.46 us
    pallas_call x0 -> x27, Pallas kernels: none -> 636 us  [the longest x2 259 us: pair_gather(): pl.pallas_call(functools.partial(pair_kernel, count), out_shape=[jax.Shap...]
    reduce_scatter x16 -> x2, waiting for transfers between devices: 278 us -> 0.01 us  [the longest x1 0.01 us: per_device(): lax.psum_scatter(dd.astype(BF16), 'tp', scatter_dimension=2, tiled=True)]
    dot_general x140 -> x6, matrix products: 186 us -> 3.5 us  [the longest x2 2.58 us: dot_nt(): lax.dot_general(a, b, (((1,), (1,)), ((), ())), preferred_element_type=F32)]
    psum x1 -> x0, blocking collectives: 150 us -> none  [settle(): small_totals = lax.psum(small_parts, ('exp', 'tp'))]
    all_to_all x20 -> x0, waiting for transfers between devices: 148 us -> none  [the longest x5 47.6 us: layer_backward(): lax.all_to_all(grad_incoming, 'exp', split_axis=1, concat_axis=0, tiled=T...]
    all_to_all x20 -> x0, starting transfers between devices: 122 us -> none  [the longest x5 34.8 us: layer_forward(): lax.all_to_all(outgoing, 'exp', split_axis=0, concat_axis=1, tiled=True)]
    all_gather x10 -> x1, blocking collectives: 98.5 us -> 20.3 us  [per_device(): routes_all = lax.all_gather(routes_own, 'exp', axis=0, tiled=True)]
    gather x20 -> x0, local copies, waits for them, and re-layouts: 66.1 us -> none  [the longest x5 18.8 us: layer_backward(): grad_normed_two = jnp.sum(coming_back[target].astype(jnp.float32), axis=1)]
  transfers between devices with their start and end apart: 45 -> 9, of which waited for: 34 -> 3; matrix products, arithmetic and copies ran while one was open for 18% -> 4% of each run, Pallas kernels for 0% -> 7%
where the time goes in v1:
time: 899 us; the launch traced here: 886 us
  Pallas kernels  636 us (71%)
  waiting for transfers between devices  126 us (14%)
  other arithmetic  63.2 us (7%)
  blocking collectives  20.3 us (2%)
  between operations  16.5 us (2%)
  local copies, waits for them, and re-layouts  12.9 us (1%)
    pallas_call x2, Pallas kernels, pair_gather(): pl.pallas_call(functools.partial(pair_kernel, count), out_shape=[jax.Shap...  259 us
    psum x1, waiting for transfers between devices, per_device(): small = lax.psum(small, ('exp', 'tp'))  121 us
    pallas_call x5, Pallas kernels, exp_scatter(): pl.pallas_call(exp_scatter_kernel, out_shape=jax.ShapeDtypeStruct((64, wi...  102 us
    pallas_call x4, Pallas kernels, exp_gather(): pl.pallas_call(exp_gather_kernel, out_shape=jax.ShapeDtypeStruct((16, 64,...  78.1 us
    pallas_call x2, Pallas kernels, experts_backward(): pl.pallas_call(experts_backward_kernel, grid=(2,), out_shape=[jax.ShapeDt...  60.7 us
    pallas_call x4, Pallas kernels, tp_gather(): pl.pallas_call(tp_gather_kernel, out_shape=jax.ShapeDtypeStruct((2, 128,...  45.3 us
    pallas_call x4, Pallas kernels, tp_scatter(): pl.pallas_call(tp_scatter_kernel, out_shape=jax.ShapeDtypeStruct((2, 32,...  38.7 us
    pallas_call x2, Pallas kernels, experts_forward(): pl.pallas_call(experts_forward_kernel, grid=(count // tile,), out_shape=[...  25.1 us
  transfers between devices with their start and end apart: 9, of which 3 were waited for; matrix products, arithmetic and copies ran while one was open for 4% of the time, Pallas kernels for 7%

profile of v1, /device:TPU:1, one launch (start us, length us, event | category | flops | bytes accessed | tf_op | source)
XLA Modules:
  0.0 885.7 jit_solution(13596624836103449001)
XLA Ops:
  11.7 20.3 %all-gather = s32[16,64,8]{1,2,0:T(8,128)S(1)} all-gather(s32[1,64,8]{1,2,0:T(8,128)S(1)} %reshape.478), channel_id=1, replica_groups=mesh['section'=2,'exp'=16,'tp'=4] {'exp'}, dimensions={0}, use_global_device_ids=true | all-gather | bytes 34816 | tf_op jit(solution)/shard_map/all_gather | solution.py:746
  34.7 6.5 convert_reduce_fusion.mask_ref
  41.3 17.1 %exp_gather.6 = bf16[16,64,1024]{2,1,0:T(8,128)(2,1)} custom-call(bf16[64,1024]{1,0:T(8,128)(2,1)} %bitcast.150), custom_call_target="tpu_custom_call" | custom-call | tf_op jit(solution)/shard_map/exp_gather/pallas_call | solution.py:225
  61.0 64.7 %pair_gather0.1 = (bf16[2,1024,512]{2,1,0:T(8,128)(2,1)}, bf16[2,256,1024]{2,1,0:T(8,128)(2,1)}, f32[2,8,1024]{2,1,0:T(8,128)}, bf16[2,1024,128]{2,1,0:T(8,128)(2,1)}) custom-call(bf16[1,1024,512]{2,1,0:T(8,128)(2,1)} %pad_maximum_fusion.refs_0_, bf16[1,256,1024]{2,1,0:T(8,128)(2,1)} %refs_1_.2, f32[1,8,1024]{2,1,0:T(8,128)} %maximum_convert_fusion.refs_2_, ...), custom_call_target="tpu_custom_call" | custom-call | tf_op jit(solution)/shard_map/pair_gather0/pallas_call | solution.py:90
  127.3 12.2 %tp_gather.4 = bf16[2,128,1024]{2,1,0:T(8,128)(2,1)} custom-call(bf16[2,32,1024]{2,1,0:T(8,128)(2,1)} %fusion.2.x_ref), custom_call_target="tpu_custom_call" | custom-call | tf_op jit(solution)/shard_map/tp_gather/pallas_call | solution.py:118
  141.0 5.6 attention_forward.2
  146.6 10.6 %tp_scatter.4 = f32[2,32,1024]{2,1,0:T(8,128)} custom-call(bf16[2,128,1024]{2,1,0:T(8,128)(2,1)} %get-tuple-element.42.x_ref), custom_call_target="tpu_custom_call" | custom-call | tf_op jit(solution)/shard_map/tp_scatter/pallas_call | solution.py:152
  159.4 1.7 multiply_convert_fusion.2
  161.1 18.6 %exp_gather.4 = bf16[16,64,1024]{2,1,0:T(8,128)(2,1)} custom-call(bf16[64,1024]{1,0:T(8,128)(2,1)} %get-tuple-element.86.x_ref), custom_call_target="tpu_custom_call" | custom-call | tf_op jit(solution)/shard_map/exp_gather/pallas_call | solution.py:225
  179.7 194.6 %pair_gather1.1 = (bf16[2,2,1024,1024]{3,2,1,0:T(8,128)(2,1)}, bf16[2,2,512,1024]{3,2,1,0:T(8,128)(2,1)}) custom-call(bf16[1,2,1024,1024]{3,2,1,0:T(8,128)(2,1)} %refs_0_.1, bf16[1,2,512,1024]{3,2,1,0:T(8,128)(2,1)} %refs_1_.3), custom_call_target="tpu_custom_call" | custom-call | tf_op jit(solution)/shard_map/pair_gather1/pallas_call | solution.py:90
  374.4 12.5 %experts_forward.2 = (bf16[1024,1024]{1,0:T(8,128)(2,1)}, bf16[2,1024,1024]{2,1,0:T(8,128)(2,1)}) custom-call(bf16[1024,1024]{1,0:T(8,128)(2,1)} %bitcast.137, bf16[2,2,1024,1024]{3,2,1,0:T(8,128)(2,1)} %get-tuple-element.43.wgu_ref, bf16[2,2,512,1024]{3,2,1,0:T(8,128)(2,1)} %get-tuple-element.44.wd_ref, bf16[2,1024,128]{2,1,0:T(8,128)(2,1)} %get-tuple-element.45.router_ref, ...), custom_call_target="tpu_custom_call" | custom-call | tf_op jit(solution)/shard_map/experts_forward/pallas_call | solution.py:490
  386.8 21.5 %exp_scatter5.4 = f32[64,1024]{1,0:T(8,128)} custom-call(bf16[4,4,64,1024]{3,2,1,0:T(8,128)(2,1)} %bitcast.153), custom_call_target="tpu_custom_call" | custom-call | tf_op jit(solution)/shard_map/exp_scatter5/pallas_call | solution.py:297
  410.2 9.9 %tp_gather.5 = bf16[2,128,1024]{2,1,0:T(8,128)(2,1)} custom-call(bf16[2,32,1024]{2,1,0:T(8,128)(2,1)} %bitcast.160), custom_call_target="tpu_custom_call" | custom-call | tf_op jit(solution)/shard_map/tp_gather/pallas_call | solution.py:118
  420.2 5.6 attention_forward.3
  425.8 10.9 %tp_scatter.5 = f32[2,32,1024]{2,1,0:T(8,128)} custom-call(bf16[2,128,1024]{2,1,0:T(8,128)(2,1)} %get-tuple-element.47.x_ref), custom_call_target="tpu_custom_call" | custom-call | tf_op jit(solution)/shard_map/tp_scatter/pallas_call | solution.py:152
  437.8 1.7 multiply_convert_fusion.1.x_ref
  439.5 19.3 %exp_gather.5 = bf16[16,64,1024]{2,1,0:T(8,128)(2,1)} custom-call(bf16[64,1024]{1,0:T(8,128)(2,1)} %multiply_convert_fusion.1.x_ref), custom_call_target="tpu_custom_call" | custom-call | tf_op jit(solution)/shard_map/exp_gather/pallas_call | solution.py:225
  459.4 12.6 %experts_forward.3 = (bf16[1024,1024]{1,0:T(8,128)(2,1)}, bf16[2,1024,1024]{2,1,0:T(8,128)(2,1)}) custom-call(bf16[1024,1024]{1,0:T(8,128)(2,1)} %bitcast.139, bf16[2,2,1024,1024]{3,2,1,0:T(8,128)(2,1)} %get-tuple-element.43.wgu_ref, bf16[2,2,512,1024]{3,2,1,0:T(8,128)(2,1)} %get-tuple-element.44.wd_ref, bf16[2,1024,128]{2,1,0:T(8,128)(2,1)} %get-tuple-element.45.router_ref, ...), custom_call_target="tpu_custom_call" | custom-call | tf_op jit(solution)/shard_map/experts_forward/pallas_call | solution.py:490
  472.0 21.1 %exp_scatter5.5 = f32[64,1024]{1,0:T(8,128)} custom-call(bf16[4,4,64,1024]{3,2,1,0:T(8,128)(2,1)} %bitcast.154), custom_call_target="tpu_custom_call" | custom-call | tf_op jit(solution)/shard_map/exp_scatter5/pallas_call | solution.py:297
  494.2 30.2 %experts_backward.2 = (bf16[1024,1024]{1,0:T(8,128)(2,1)}, bf16[2,1024,1024]{2,1,0:T(8,128)(2,1)}, bf16[2,512,1024]{2,1,0:T(8,128)(2,1)}, f32[32,1024]{1,0:T(8,128)}) custom-call(bf16[1024,1024]{1,0:T(8,128)(2,1)} %bitcast.140, bf16[1024,1024]{1,0:T(8,128)(2,1)} %bitcast.141, bf16[2,1024,1024]{2,1,0:T(8,128)(2,1)} %get-tuple-element.49.gu_ref, ...), custom_call_target="tpu_custom_call" | custom-call | tf_op jit(solution)/shard_map/experts_backward/pallas_call | solution.py:588
  524.4 20.8 %exp_scatter5.6 = f32[64,1024]{1,0:T(8,128)} custom-call(bf16[4,4,64,1024]{3,2,1,0:T(8,128)(2,1)} %bitcast.152), custom_call_target="tpu_custom_call" | custom-call | tf_op jit(solution)/shard_map/exp_scatter5/pallas_call | solution.py:297
  547.6 13.8 %tp_gather.6 = bf16[2,128,1024]{2,1,0:T(8,128)(2,1)} custom-call(bf16[2,32,1024]{2,1,0:T(8,128)(2,1)} %bitcast.159), custom_call_target="tpu_custom_call" | custom-call | tf_op jit(solution)/shard_map/tp_gather/pallas_call | solution.py:118
  561.4 7.5 attention_backward.2
  568.9 8.6 tp_scatter.6
  578.7 1.9 fusion.8
  580.6 23.0 %exp_gather.7 = bf16[16,64,1024]{2,1,0:T(8,128)(2,1)} custom-call(bf16[64,1024]{1,0:T(8,128)(2,1)} %get-tuple-element.80.x_ref), custom_call_target="tpu_custom_call" | custom-call | tf_op jit(solution)/shard_map/exp_gather/pallas_call | solution.py:225
  603.6 30.5 %experts_backward.3 = (bf16[1024,1024]{1,0:T(8,128)(2,1)}, bf16[2,1024,1024]{2,1,0:T(8,128)(2,1)}, bf16[2,512,1024]{2,1,0:T(8,128)(2,1)}, f32[32,1024]{1,0:T(8,128)}) custom-call(bf16[1024,1024]{1,0:T(8,128)(2,1)} %bitcast.138, bf16[1024,1024]{1,0:T(8,128)(2,1)} %bitcast.142, bf16[2,1024,1024]{2,1,0:T(8,128)(2,1)} %get-tuple-element.54.gu_ref, ...), custom_call_target="tpu_custom_call" | custom-call | tf_op jit(solution)/shard_map/experts_backward/pallas_call | solution.py:588
  634.2 3.2 broadcast_select_fusion.1
  637.3 1.9 collective-permute-start.5
  639.3 22.1 %exp_scatter5.7 = f32[64,1024]{1,0:T(8,128)} custom-call(bf16[4,4,64,1024]{3,2,1,0:T(8,128)(2,1)} %bitcast.151), custom_call_target="tpu_custom_call" | custom-call | tf_op jit(solution)/shard_map/exp_scatter5/pallas_call | solution.py:297
  663.6 9.5 %tp_gather.7 = bf16[2,128,1024]{2,1,0:T(8,128)(2,1)} custom-call(bf16[2,32,1024]{2,1,0:T(8,128)(2,1)} %bitcast.158), custom_call_target="tpu_custom_call" | custom-call | tf_op jit(solution)/shard_map/tp_gather/pallas_call | solution.py:118
  673.1 7.7 attention_backward.3
  680.8 8.6 tp_scatter.7
  691.1 4.5 collective-permute-start.2
  695.5 4.5 broadcast_select_fusion
  700.9 4.4 add_convert_fusion.1
  705.7 1.9 collective-permute-done.4
  707.6 8.6 add_convert_fusion
  717.6 2.8 broadcast_select_fusion.2
  721.5 2.9 collective-permute-done
  726.0 120.9 %all-reduce.3.cloned.1.call-done = f32[40,1024]{1,0:T(8,128)} async-done(((f32[40,1024]{1,0:T(8,128)}), f32[40,1024]{1,0:T(8,128)}) %all-reduce.3.cloned.1.call-update) | async-done | bytes 163856 | tf_op jit(solution)/shard_map/psum | solution.py:770
  846.9 1.4 fusion.42
  848.3 1.6 slice_bitcast_fusion
  849.9 3.2 add_convert_fusion.2
  853.0 17.0 %exp_scatter6.1 = f32[64,768]{1,0:T(8,128)} custom-call(bf16[4,4,64,768]{3,2,1,0:T(8,128)(2,1)} %bitcast.143), custom_call_target="tpu_custom_call" | custom-call | tf_op jit(solution)/shard_map/exp_scatter6/pallas_call | solution.py:297
  871.5 1.6 slice_bitcast_fusion.1
  873.1 2.1 bitcast_convert_fusion.1
  875.2 2.7 bitcast_convert_fusion
  (132 shorter events, 32.9 us)
Async XLA Ops:
  8.0 24.8 %copy-start = (bf16[4,32,1024]{2,1,0:T(8,128)(2,1)S(1)}, bf16[4,32,1024]{2,1,0:T(8,128)(2,1)}, u32[]{:S(2)}) copy-start(bf16[4,32,1024]{2,1,0:T(8,128)(2,1)} %param.14) | copy-start | bytes 786436
  8.0 838.8 %all-reduce.3.cloned.1.call-start = ((), (), s32[]{:S(2)}) async-start(), calls=%async_computation.2 | async-start | bytes 327680 | tf_op jit(solution)/shard_map/psum | solution.py:770
  34.5 24.8 %copy-start.22 = (bf16[1,1024]{1,0:T(2,128)(2,1)S(1)}, bf16[1,1024]{1,0:T(2,128)(2,1)}, u32[]{:S(2)}) copy-start(bf16[1,1024]{1,0:T(2,128)(2,1)} %param.22) | copy-start | bytes 6148
  34.5 24.7 %copy-start.23 = (bf16[1,1024]{1,0:T(2,128)(2,1)S(1)}, bf16[1,1024]{1,0:T(2,128)(2,1)}, u32[]{:S(2)}) copy-start(bf16[1,1024]{1,0:T(2,128)(2,1)} %param.17) | copy-start | bytes 6148
  34.5 25.4 %copy-start.17 = (bf16[1,1024,256]{2,1,0:T(8,128)(2,1)S(1)}, bf16[1,1024,256]{2,1,0:T(8,128)(2,1)}, u32[]{:S(2)}) copy-start(bf16[1,1024,256]{2,1,0:T(8,128)(2,1)} %param.18) | copy-start | bytes 1572868
  34.5 25.4 %copy-start.18 = (bf16[1,1024,128]{2,1,0:T(8,128)(2,1)S(1)}, bf16[1,1024,128]{2,1,0:T(8,128)(2,1)}, u32[]{:S(2)}) copy-start(bf16[1,1024,128]{2,1,0:T(8,128)(2,1)} %param.20) | copy-start | bytes 786436
  34.5 25.4 %copy-start.19 = (bf16[1,1024,128]{2,1,0:T(8,128)(2,1)S(1)}, bf16[1,1024,128]{2,1,0:T(8,128)(2,1)}, u32[]{:S(2)}) copy-start(bf16[1,1024,128]{2,1,0:T(8,128)(2,1)} %param.19) | copy-start | bytes 786436
  59.1 67.4 %copy-start.9 = (bf16[4,32,1024]{2,1,0:T(8,128)(2,1)S(1)}, bf16[4,32,1024]{2,1,0:T(8,128)(2,1)}, u32[]{:S(2)}) copy-start(bf16[4,32,1024]{2,1,0:T(8,128)(2,1)} %param.13) | copy-start | bytes 786436
  425.8 33.0 %copy-start.2 = (bf16[2,1024,128]{2,1,0:T(8,128)(2,1)S(1)}, bf16[2,1024,128]{2,1,0:T(8,128)(2,1)}, u32[]{:S(2)}) copy-start(bf16[2,1024,128]{2,1,0:T(8,128)(2,1)} %get-tuple-element.45.router_ref) | copy-start | bytes 1572868
  439.5 19.3 %copy-start.13 = (bf16[64,1024]{1,0:T(8,128)(2,1)S(1)}, bf16[64,1024]{1,0:T(8,128)(2,1)}, u32[]{:S(2)}) copy-start(bf16[64,1024]{1,0:T(8,128)(2,1)} %multiply_convert_fusion.1.x_ref) | copy-start | bytes 393220
  472.0 21.1 %copy-start.14 = (bf16[2,32,1024]{2,1,0:T(8,128)(2,1)S(1)}, bf16[2,32,1024]{2,1,0:T(8,128)(2,1)}, u32[]{:S(2)}) copy-start(bf16[2,32,1024]{2,1,0:T(8,128)(2,1)} %constant_dynamic-slice_fusion) | copy-start | bytes 393220
  524.4 21.1 %copy-start.3 = (bf16[2,1024,128]{2,1,0:T(8,128)(2,1)S(1)}, bf16[2,1024,128]{2,1,0:T(8,128)(2,1)}, u32[]{:S(2)}) copy-start(bf16[2,1024,128]{2,1,0:T(8,128)(2,1)} %get-tuple-element.45.router_ref) | copy-start | bytes 1572868
  524.4 21.1 %copy-start.6 = (f32[2,32,1024]{2,1,0:T(8,128)S(1)}, f32[2,32,1024]{2,1,0:T(8,128)}, u32[]{:S(2)}) copy-start(f32[2,32,1024]{2,1,0:T(8,128)} %tp_scatter.5) | copy-start | bytes 786436
  561.4 17.3 %copy-start.11 = (f32[64,1024]{1,0:T(8,128)S(1)}, f32[64,1024]{1,0:T(8,128)}, u32[]{:S(2)}) copy-start(f32[64,1024]{1,0:T(8,128)} %exp_scatter5.4) | copy-start | bytes 786436
  603.6 30.5 %copy-start.7 = (bf16[2,512,1024]{2,1,0:T(8,128)(2,1)S(1)}, bf16[2,512,1024]{2,1,0:T(8,128)(2,1)}, u32[]{:S(2)}) copy-start(bf16[2,512,1024]{2,1,0:T(8,128)(2,1)} %get-tuple-element.66) | copy-start | bytes 6291460
  637.3 24.1 %copy-start.4 = (bf16[2,1024,128]{2,1,0:T(8,128)(2,1)S(1)}, bf16[2,1024,128]{2,1,0:T(8,128)(2,1)}, u32[]{:S(2)}) copy-start(bf16[2,1024,128]{2,1,0:T(8,128)(2,1)} %get-tuple-element.45.router_ref) | copy-start | bytes 1572868
  637.3 25.5 %copy-start.15 = (bf16[64,1024]{1,0:T(8,128)(2,1)S(1)}, bf16[64,1024]{1,0:T(8,128)(2,1)}, u32[]{:S(2)}) copy-start(bf16[64,1024]{1,0:T(8,128)(2,1)} %get-tuple-element.80.x_ref) | copy-start | bytes 393220
  637.3 63.6 %collective-permute-start.5 = (bf16[2,512,1024]{2,1,0:T(8,128)(2,1)}, bf16[2,512,1024]{2,1,0:T(8,128)(2,1)}, u32[]{:S(2)}, u32[]{:S(2)}) collective-permute-start(bf16[2,512,1024]{2,1,0:T(8,128)(2,1)} %broadcast_select_fusion.1), channel_id=1, source_target_pairs={{0,64},{64,0},{1,65},{65,1},{2,66},{66,2},{3,67},{67,3},{4,68},{68... | collective-permute-start | bytes 6291464 | tf_op jit(solution)/shard_map/ppermute | solution.py:723
  673.1 17.5 %copy-start.20 = (f32[32,1024]{1,0:T(8,128)S(1)}, f32[32,1024]{1,0:T(8,128)}, u32[]{:S(2)}) copy-start(f32[32,1024]{1,0:T(8,128)} %get-tuple-element.60) | copy-start | bytes 393220
  673.1 17.7 %copy-start.16 = (bf16[64,1024]{1,0:T(8,128)(2,1)S(1)}, bf16[64,1024]{1,0:T(8,128)(2,1)}, u32[]{:S(2)}) copy-start(bf16[64,1024]{1,0:T(8,128)(2,1)} %get-tuple-element.86.x_ref) | copy-start | bytes 393220
  673.1 17.7 %copy-start.21 = (f32[32,1024]{1,0:T(8,128)S(1)}, f32[32,1024]{1,0:T(8,128)}, u32[]{:S(2)}) copy-start(f32[32,1024]{1,0:T(8,128)} %get-tuple-element.59) | copy-start | bytes 393220
  673.1 22.4 %copy-start.5 = (bf16[2,1024,1024]{2,1,0:T(8,128)(2,1)S(1)}, bf16[2,1024,1024]{2,1,0:T(8,128)(2,1)}, u32[]{:S(2)}) copy-start(bf16[2,1024,1024]{2,1,0:T(8,128)(2,1)} %get-tuple-element.64) | copy-start | bytes 12582916
  691.1 9.0 %collective-permute-start.2 = (f32[40,1024]{1,0:T(8,128)S(1)}, f32[40,1024]{1,0:T(8,128)S(1)}, u32[]{:S(2)}, u32[]{:S(2)}) collective-permute-start(f32[40,1024]{1,0:T(8,128)S(1)} %fusion.30), channel_id=1, source_target_pairs={{0,64},{64,0},{1,65},{65,1},{2,66},{66,2},{3,67},{67,3},{4,68},{68... | collective-permute-start | bytes 491528 | tf_op jit(solution)/shard_map/ppermute | solution.py:723
  700.1 7.5 collective-permute-start.4
  700.9 172.2 %reduce-scatter.5.cloned.1.call-start = ((), (), s32[]{:S(2)}) async-start(), calls=%async_computation.4 | async-start | bytes 2621440 | tf_op jit(solution)/shard_map/reduce_scatter | solution.py:768
  705.4 169.8 %reduce-scatter.3.cloned.1.call-start = ((), (), s32[]{:S(2)}) async-start(), calls=%async_computation.3 | async-start | bytes 5242880 | tf_op jit(solution)/shard_map/reduce_scatter | solution.py:767
  716.2 1.4 copy-start.8
  717.6 3.0 copy-start.12
  717.6 3.7 copy-start.10
  720.4 129.4 %collective-permute-start.3 = (bf16[1024,768]{1,0:T(8,128)(2,1)}, bf16[1024,768]{1,0:T(8,128)(2,1)}, u32[]{:S(2)}, u32[]{:S(2)}) collective-permute-start(bf16[1024,768]{1,0:T(8,128)(2,1)} %broadcast_select_fusion.2), channel_id=1, source_target_pairs={{0,64},{64,0},{1,65},{65,1},{2,66},{66,2},{3,67},{67,3},{4,68},{68... | collective-permute-start | bytes 4718600 | tf_op jit(solution)/shard_map/ppermute | solution.py:723
  720.8 4.4 collective-permute-start.1
  721.4 3.0 collective-permute-start
  871.5 6.4 copy-start.1
Sparse Core Ops, SparseCore 0:
  701.0 145.8 all-reduce.2
Sparse Core Ops, SparseCore 1:
  705.4 29.8 reduce-scatter.4
  737.5 46.6 reduce-scatter.2

commit v2 on v1

--- a/solution.py
+++ b/solution.py
@@ -66,248 +66,561 @@
     )
 
 
-def pair_kernel(count, *refs):
-    ins, outs = refs[:count], refs[count : 2 * count]
-    send_sem, recv_sem, own_sem = refs[2 * count :]
-    me = lax.axis_index("section")
-    peer = {"section": 1 - me}
-    greet([peer])
-    sends, owns = [], []
-    for at in range(count):
-        sends.append(
-            remote(ins[at].at[0], outs[at].at[me], send_sem.at[at], recv_sem.at[at], peer)
-        )
-        owns.append(pltpu.make_async_copy(ins[at].at[0], outs[at].at[me], own_sem.at[at]))
-        sends[-1].start()
-        owns[-1].start()
-    for at in range(count):
-        owns[at].wait()
-        sends[at].wait()
-
-
-def pair_gather(arrays, number):
-    count = len(arrays)
-    return pl.pallas_call(
-        functools.partial(pair_kernel, count),
-        out_shape=[jax.ShapeDtypeStruct((2,) + a.shape[1:], a.dtype) for a in arrays],
-        in_specs=[in_any()] * count,
-        out_specs=[in_any()] * count,
-        scratch_shapes=[pltpu.SemaphoreType.DMA((count,))] * 3,
-        compiler_params=comm_params(number),
-        name="pair_gather%d" % number,
-    )(*arrays)
-
-
-def tp_gather_kernel(x_ref, out_ref, send_sem, recv_sem):
-    me = lax.axis_index("tp")
-    peers = [{"tp": lax.rem(me + j, 4)} for j in (1, 2, 3)]
-    greet(peers)
-    mine = pl.ds(pl.multiple_of(me * 32, 32), 32)
-    copies = [
-        remote(x_ref, out_ref.at[:, mine], send_sem.at[j], recv_sem.at[j], peers[j])
-        for j in range(3)
-    ]
-    for copy in copies:
-        copy.start()
-    out_ref[:, mine] = x_ref[...]
-    for copy in copies:
-        copy.wait()
-
-
-def tp_gather(x):
-    return pl.pallas_call(
-        tp_gather_kernel,
-        out_shape=jax.ShapeDtypeStruct((2, 128, D), BF16),
-        in_specs=[in_vmem()],
-        out_specs=in_vmem(),
-        scratch_shapes=[pltpu.SemaphoreType.DMA((3,))] * 2,
-        compiler_params=comm_params(2),
-        name="tp_gather",
-    )(x)
-
-
-def tp_scatter_kernel(x_ref, out_ref, held, send_sem, recv_sem):
-    me = lax.axis_index("tp")
-    places = [lax.rem(me + j, 4) for j in (1, 2, 3)]
-    greet([{"tp": place} for place in places])
-    copies = []
-    for j in range(3):
-        theirs = pl.ds(pl.multiple_of(places[j] * 32, 32), 32)
-        copies.append(
-            remote(
-                x_ref.at[:, theirs], held.at[j], send_sem.at[j], recv_sem.at[j], {"tp": places[j]}
-            )
-        )
-        copies[-1].start()
-    total = x_ref[:, pl.ds(pl.multiple_of(me * 32, 32), 32)].astype(F32)
-    for j in range(3):
-        copies[j].wait_recv()
-        total = total + held[j].astype(F32)
-    out_ref[...] = total
-    for copy in copies:
-        copy.wait_send()
-
-
-def tp_scatter(x):
-    return pl.pallas_call(
-        tp_scatter_kernel,
-        out_shape=jax.ShapeDtypeStruct((2, 32, D), F32),
-        in_specs=[in_vmem()],
-        out_specs=in_vmem(),
-        scratch_shapes=[pltpu.VMEM((3, 2, 32, D), BF16)] + [pltpu.SemaphoreType.DMA((3,))] * 2,
-        compiler_params=comm_params(3),
-        name="tp_scatter",
-    )(x)
-
-
-def exp_places():
+class Part:
+    def __init__(self, arrays, in_specs, out_shapes, out_specs, scratch, axes, body):
+        self.arrays, self.in_specs = arrays, in_specs
+        self.out_shapes, self.out_specs = out_shapes, out_specs
+        self.scratch, self.axes, self.body = scratch, axes, body
+
+
+def around(axis):
+    if axis == "section":
+        return [{"section": 1 - lax.axis_index("section")}]
+    if axis == "tp":
+        me = lax.axis_index("tp")
+        return [{"tp": lax.rem(me + j, 4)} for j in (3, 1)]
+    if axis == "tp_opposite":
+        return [{"tp": lax.rem(lax.axis_index("tp") + 2, 4)}]
     me = lax.axis_index("exp")
     at_x, at_z = me // 4, lax.rem(me, 4)
-    return me, at_x, at_z
-
-
-def exp_gather_kernel(x_ref, out_ref, send_one, recv_one, send_two, recv_two):
-    me, at_x, at_z = exp_places()
-
-    def place(by_x, by_z):
-        return lax.rem(at_x + by_x, 4) * 4 + lax.rem(at_z + by_z, 4)
-
-    peers = [[{"exp": place(j, 0)} for j in (1, 2, 3)], [{"exp": place(0, j)} for j in (1, 2, 3)]]
-    greet(peers[0] + peers[1])
-    rows = [pl.ds(0, 32), pl.ds(32, 32)]
-    first = [[], []]
-    second = [[], []]
-    for j in range(3):
+    if axis == "x":
+        return [{"exp": lax.rem(at_x + j, 4) * 4 + at_z} for j in (3, 1)]
+    return [{"exp": at_x * 4 + lax.rem(at_z + j, 4)} for j in (3, 1)]
+
+
+def fused_kernel(parts, *refs):
+    refs = list(refs)
+
+    def take(count):
+        taken = refs[:count]
+        del refs[:count]
+        return taken
+
+    ins = [take(len(part.arrays)) for part in parts]
+    outs = [take(len(part.out_shapes)) for part in parts]
+    scratch = [take(len(part.scratch)) for part in parts]
+    axes = []
+    for part in parts:
+        axes += [axis for axis in part.axes if axis not in axes]
+    greet([peer for axis in axes for peer in around(axis)])
+    running = [part.body(i, o, s) for part, i, o, s in zip(parts, ins, outs, scratch)]
+    while running:
+        for one in list(running):
+            if next(one, "end") == "end":
+                running.remove(one)
+
+
+def fuse(parts, number, name):
+    outs = pl.pallas_call(
+        functools.partial(fused_kernel, parts),
+        out_shape=[o for part in parts for o in part.out_shapes],
+        in_specs=[s for part in parts for s in part.in_specs],
+        out_specs=[s for part in parts for s in part.out_specs],
+        scratch_shapes=[s for part in parts for s in part.scratch],
+        compiler_params=comm_params(number),
+        name=name,
+    )(*[a for part in parts for a in part.arrays])
+    outs = list(outs)
+    results = []
+    for part in parts:
+        count = len(part.out_shapes)
+        results.append(outs[:count] if count > 1 else outs[0])
+        outs = outs[count:]
+    return results
+
+
+def sems(*shape):
+    return [pltpu.SemaphoreType.DMA(shape)] * 2
+
+
+def pair_part(arrays):
+    count = len(arrays)
+
+    def body(ins, outs, scratch):
+        held, (send, recv, read, write) = scratch[:count], scratch[count:]
+        me = lax.axis_index("section")
+        (peer,) = around("section")
+        sends, reads, writes = [], [], []
+        for at in range(count):
+            sends.append(remote(ins[at].at[0], outs[at].at[me], send.at[at], recv.at[at], peer))
+            reads.append(pltpu.make_async_copy(ins[at].at[0], held[at], read.at[at]))
+            writes.append(pltpu.make_async_copy(held[at], outs[at].at[me], write.at[at]))
+            sends[-1].start()
+            reads[-1].start()
+        yield
+        for at in range(count):
+            reads[at].wait()
+            writes[at].start()
+        yield
+        yield
+        yield
+        for at in range(count):
+            writes[at].wait()
+            sends[at].wait()
+
+    return Part(
+        arrays,
+        [in_any()] * count,
+        [jax.ShapeDtypeStruct((2,) + a.shape[1:], a.dtype) for a in arrays],
+        [in_any()] * count,
+        [pltpu.VMEM(a.shape[1:], a.dtype) for a in arrays]
+        + [pltpu.SemaphoreType.DMA((count,))] * 4,
+        ["section"],
+        body,
+    )
+
+
+class RingGather:
+    def __init__(self, view, own, left, right, send, recv):
+        self.view, self.own = view, own
+        self.left, self.right, self.send, self.recv = left, right, send, recv
+        self.copies = []
+
+    def go(self, src, dst, at, peer):
+        copy = remote(src, dst, self.send[at], self.recv[at], peer)
+        copy.start()
+        self.copies.append(copy)
+
+    def start(self):
+        own = self.view(0, None) if self.own is None else self.own
+        self.go(own, self.view(0, None), 0, self.right)
+        self.go(own, self.view(0, None), 1, self.left)
+
+    def forward(self):
+        self.copies[0].wait_recv()
+        self.go(self.view(3, 0), self.view(3, 0), 2, self.right)
+        self.copies[1].wait_recv()
+        self.go(self.view(1, 1), self.view(1, 1), 3, self.left)
+
+    def finish(self):
+        self.copies[2].wait_recv()
+        self.copies[3].wait_recv()
+
+    def drain(self):
+        for copy in self.copies:
+            copy.wait_send()
+
+
+class RingScatter:
+    def __init__(self, view, temp, block, stage, left, right, send, recv):
+        self.view, self.temp, self.block, self.stage = view, temp, block, stage
+        self.left, self.right, self.send, self.recv = left, right, send, recv
+        self.copies = []
+
+    def go(self, src, dst, at, peer):
+        copy = remote(src, dst, self.send[at], self.recv[at], peer)
+        copy.start()
+        self.copies.append(copy)
+
+    def start(self):
+        self.go(self.view(2, 0), self.temp(0), 0, self.right)
+        self.go(self.view(2, 1), self.temp(1), 1, self.left)
+        self.go(self.view(1, 1), self.block(0, 1), 2, self.right)
+        self.go(self.view(3, 0), self.block(1, 0), 3, self.left)
+
+    def middle(self):
+        for side, nearer, peer in ((0, 1, self.right), (1, 3, self.left)):
+            self.copies[side].wait_recv()
+            term = self.view(nearer, side)[...].astype(F32) + self.temp(side)[...].astype(F32)
+            self.stage(side)[...] = term.astype(BF16)
+            self.go(self.stage(side), self.block(side, side), 4 + side, peer)
+
+    def finish(self):
+        for copy in self.copies[2:]:
+            copy.wait_recv()
+
+    def total(self, part):
+        return (
+            self.view(0, part)[...].astype(F32)
+            + self.block(0, part)[...].astype(F32)
+            + self.block(1, part)[...].astype(F32)
+        )
+
+    def drain(self):
+        for copy in self.copies:
+            copy.wait_send()
+
+
+def tp_block(ref, k, part):
+    place = lax.rem(lax.axis_index("tp") + k, 4)
+    rows = pl.ds(pl.multiple_of(place * 32, 32), 32)
+    return ref.at[:, rows] if part is None else ref.at[part, rows]
+
+
+def tp_gather_part(x):
+    def body(ins, outs, scratch):
+        (x_ref,), (out_ref,), (send, recv) = ins, outs, scratch
+        left, right = around("tp")
+        ring = RingGather(
+            functools.partial(tp_block, out_ref),
+            x_ref,
+            left,
+            right,
+            [send.at[i] for i in range(4)],
+            [recv.at[i] for i in range(4)],
+        )
+        ring.start()
+        tp_block(out_ref, 0, None)[...] = x_ref[...]
+        yield
+        ring.forward()
+        yield
+        ring.finish()
+        ring.drain()
+
+    return Part(
+        [x],
+        [in_vmem()],
+        [jax.ShapeDtypeStruct((2, 128, D), BF16)],
+        [in_vmem()],
+        sems(4),
+        ["tp"],
+        body,
+    )
+
+
+def tp_scatter_part(x):
+    def body(ins, outs, scratch):
+        (x_ref,), (out_ref,), (temp, block, stage, send, recv) = ins, outs, scratch
+        left, right = around("tp")
+        ring = RingScatter(
+            functools.partial(tp_block, x_ref),
+            lambda side: temp.at[side],
+            lambda side, part: block.at[side, part],
+            lambda side: stage.at[side],
+            left,
+            right,
+            [send.at[i] for i in range(6)],
+            [recv.at[i] for i in range(6)],
+        )
+        ring.start()
+        yield
+        ring.middle()
+        yield
+        ring.finish()
+        out_ref[0] = ring.total(0)
+        out_ref[1] = ring.total(1)
+        ring.drain()
+
+    return Part(
+        [x],
+        [in_vmem()],
+        [jax.ShapeDtypeStruct((2, 32, D), F32)],
+        [in_vmem()],
+        [
+            pltpu.VMEM((2, 32, D), BF16),
+            pltpu.VMEM((2, 2, 32, D), BF16),
+            pltpu.VMEM((2, 32, D), BF16),
+        ]
+        + sems(6),
+        ["tp"],
+        body,
+    )
+
+
+def exp_block(ref, half, i, j, part):
+    me = lax.axis_index("exp")
+    at_x, at_z = me // 4, lax.rem(me, 4)
+    i, j = (i, j) if half == 0 else (j, i)
+    rows = pl.ds(32 * half, 32) if part is None else pl.ds(32 * half + 16 * part, 16)
+    return ref.at[lax.rem(at_x + i, 4), lax.rem(at_z + j, 4), rows]
+
+
+def exp_gather_steps(x_ref, out_ref, send, recv):
+    sides = [around("x"), around("z")]
+    first, second = [], []
+    for half in range(2):
+
+        def ring(view, own, at, axis, half=half):
+            return RingGather(
+                view,
+                own,
+                sides[axis][0],
+                sides[axis][1],
+                [send.at[half, at, n] for n in range(4)],
+                [recv.at[half, at, n] for n in range(4)],
+            )
+
+        def along(k, part, half=half):
+            return exp_block(out_ref, half, k, 0, part)
+
+        own = x_ref.at[pl.ds(32 * half, 32)]
+        first.append(ring(along, own, 4, half))
+        second.append([])
+        for i in range(4):
+
+            def across(k, part, half=half, i=i):
+                return exp_block(out_ref, half, i, k, part)
+
+            second[half].append(ring(across, own if i == 0 else None, i, 1 - half))
+    for half in range(2):
+        first[half].start()
+    for half in range(2):
+        second[half][0].start()
+        exp_block(out_ref, half, 0, 0, None)[...] = x_ref[pl.ds(32 * half, 32)]
+    yield
+    for half in range(2):
+        first[half].forward()
+        second[half][3].start()
+        second[half][1].start()
+    yield
+    for half in range(2):
+        second[half][0].forward()
+    yield
+    for half in range(2):
+        first[half].finish()
+        second[half][2].start()
+    yield
+    for i in (3, 1):
         for half in range(2):
-            copy = remote(
-                x_ref.at[rows[half]],
-                out_ref.at[me, rows[half]],
-                send_one.at[half, j],
-                recv_one.at[half, j],
-                peers[half][j],
+            second[half][i].forward()
+    yield
+    for half in range(2):
+        second[half][2].forward()
+    yield
+    for half in range(2):
+        for ring in second[half]:
+            ring.finish()
+        for ring in second[half] + [first[half]]:
+            ring.drain()
+
+
+def exp_gather_part(x):
+    def body(ins, outs, scratch):
+        yield from exp_gather_steps(ins[0], outs[0], *scratch)
+
+    return Part(
+        [x],
+        [in_vmem()],
+        [jax.ShapeDtypeStruct((4, 4, 64, x.shape[1]), x.dtype)],
+        [in_vmem()],
+        sems(2, 5, 4),
+        ["x", "z"],
+        body,
+    )
+
+
+def exp_scatter_steps(x_ref, out_ref, temp, block, stage, ready, send, recv):
+    sides = [around("x"), around("z")]
+    first, second = [], []
+    for half in range(2):
+
+        def ring(view, at, axis, half=half):
+            return RingScatter(
+                view,
+                lambda side: temp.at[half, at, side],
+                lambda side, part: block.at[half, at, side, pl.ds(16 * part, 16)],
+                lambda side: stage.at[half, at, side],
+                sides[axis][0],
+                sides[axis][1],
+                [send.at[half, at, n] for n in range(6)],
+                [recv.at[half, at, n] for n in range(6)],
             )
+
+        first.append([])
+        for j in range(4):
+
+            def along(k, part, half=half, j=j):
+                return exp_block(x_ref, half, k, j, part)
+
+            first[half].append(ring(along, j, half))
+
+        def across(k, part, half=half):
+            return ready.at[half, k, pl.ds(16 * part, 16)]
+
+        second.append(ring(across, 4, 1 - half))
+    order = (2, 1, 3, 0)
+    for j in order:
+        for half in range(2):
+            first[half][j].start()
+    yield
+    for j in order:
+        for half in range(2):
+            first[half][j].middle()
+        yield
+    for j in order:
+        for half in range(2):
+            first[half][j].finish()
+            for part in range(2):
+                ready[half, j, pl.ds(16 * part, 16)] = first[half][j].total(part).astype(BF16)
+            if j == 3:
+                second[half].start()
+    yield
+    for half in range(2):
+        second[half].middle()
+    yield
+    for half in range(2):
+        second[half].finish()
+        for part in range(2):
+            out_ref[pl.ds(32 * half + 16 * part, 16)] = second[half].total(part)
+    for half in range(2):
+        for ring in first[half] + [second[half]]:
+            ring.drain()
+
+
+def exp_scatter_scratch(width):
+    return [
+        pltpu.VMEM((2, 5, 2, 16, width), BF16),
+        pltpu.VMEM((2, 5, 2, 32, width), BF16),
+        pltpu.VMEM((2, 5, 2, 16, width), BF16),
+        pltpu.VMEM((2, 4, 32, width), BF16),
+    ] + sems(2, 5, 6)
+
+
+def exp_scatter_part(x):
+    width = x.shape[-1]
+
+    def body(ins, outs, scratch):
+        yield from exp_scatter_steps(ins[0], outs[0], *scratch)
+
+    return Part(
+        [x.reshape(4, 4, 64, width)],
+        [in_vmem()],
+        [jax.ShapeDtypeStruct((64, width), F32)],
+        [in_vmem()],
+        exp_scatter_scratch(width),
+        ["x", "z"],
+        body,
+    )
+
+
+def expert_part(grads, first_row):
+    rows = pl.ds(first_row, 512)
+
+    def body(ins, outs, scratch):
+        (g_ref,), (out_ref,) = ins, outs
+        own, got, temp, block, stage, send, recv, read, swap_send, swap_recv = scratch
+        me = lax.axis_index("section")
+        place = lax.axis_index("tp")
+        left, right = around("tp")
+        (peer,) = around("section")
+        swap = remote(g_ref.at[1 - me, rows], got, swap_send.at[0], swap_recv.at[0], peer)
+        swap.start()
+        kept = pltpu.make_async_copy(g_ref.at[me, rows], own, read.at[0])
+        kept.start()
+        yield
+        kept.wait()
+        swap.wait_recv()
+
+        @pl.loop(0, 8)
+        def _(i):
+            r = pl.ds(pl.multiple_of(i * 64, 64), 64)
+            own[r] = (own[r].astype(F32) + got[r].astype(F32)).astype(BF16)
+
+        def view(k, part):
+            columns = pl.multiple_of(lax.rem(place + k, 4) * 256, 256)
+            return own.at[pl.ds(256 * part, 256), pl.ds(columns, 256)]
+
+        ring = RingScatter(
+            view,
+            lambda side: temp.at[side],
+            lambda side, part: block.at[side, part],
+            lambda side: stage.at[side],
+            left,
+            right,
+            [send.at[i] for i in range(6)],
+            [recv.at[i] for i in range(6)],
+        )
+        ring.start()
+        yield
+        yield
+        yield
+        ring.middle()
+        yield
+        yield
+        yield
+        ring.finish()
+        out_ref[:256] = ring.total(0).astype(BF16)
+        out_ref[256:] = ring.total(1).astype(BF16)
+        ring.drain()
+        swap.wait_send()
+
+    return Part(
+        [grads],
+        [in_any()],
+        [jax.ShapeDtypeStruct((512, 256), BF16)],
+        [in_vmem()],
+        [
+            pltpu.VMEM((512, D), BF16),
+            pltpu.VMEM((512, D), BF16),
+            pltpu.VMEM((2, 256, 256), BF16),
+            pltpu.VMEM((2, 2, 256, 256), BF16),
+            pltpu.VMEM((2, 256, 256), BF16),
+        ]
+        + sems(6)
+        + [pltpu.SemaphoreType.DMA((1,))] * 3,
+        ["section", "tp"],
+        body,
+    )
+
+
+WIDE = 896
+
+
+def settle_part(first, second):
+    def body(ins, outs, scratch):
+        first_ref, second_ref = ins
+        out_ref, small_ref = outs
+        got, x_ref, total, piece, held = scratch[:5]
+        scatter, rest = scratch[5:11], scratch[11:]
+        swap_send, swap_recv, tp_send, tp_recv, gather_send, gather_recv = rest
+        me = lax.axis_index("section")
+        (peer,) = around("section")
+        copies = [
+            remote(ref, got, swap_send.at[0], swap_recv.at[0], peer)
+            for ref in (second_ref, first_ref)
+        ]
+        for layer in range(2):
+
+            @pl.when(me == layer)
+            def _():
+                copies[layer].start()
+
+        yield
+        copies[0].wait_recv()
+        for at_x in range(4):
+            for at_z in range(4):
+                mine = jnp.where(me == 0, first_ref[at_x, at_z], second_ref[at_x, at_z])
+                summed = mine.astype(F32) + got[at_x, at_z].astype(F32)
+                x_ref[at_x, at_z] = summed.astype(BF16)
+        yield from exp_scatter_steps(x_ref, total, *scatter)
+        out_ref[...] = total[:, :768]
+        piece[...] = total[:, 768:]
+        partners = around("tp") + around("tp_opposite")
+        sent = [
+            remote(piece, held.at[at], tp_send.at[at], tp_recv.at[at], partner)
+            for at, partner in enumerate(partners)
+        ]
+        for copy in sent:
             copy.start()
-            first[half].append(copy)
-    for j in range(3):
-        for half in range(2):
-            copy = remote(
-                x_ref.at[rows[half]],
-                out_ref.at[me, rows[half]],
-                send_two.at[half, 0, j],
-                recv_two.at[half, 0, j],
-                peers[1 - half][j],
-            )
-            copy.start()
-            second[half].append(copy)
-    out_ref[me] = x_ref[...]
-    for back in range(1, 4):
-        for half in range(2):
-            first[half][back - 1].wait_recv()
-            origin = place(4 - back, 0) if half == 0 else place(0, 4 - back)
-            for j in range(3):
-                copy = remote(
-                    out_ref.at[origin, rows[half]],
-                    out_ref.at[origin, rows[half]],
-                    send_two.at[half, back, j],
-                    recv_two.at[half, back, j],
-                    peers[1 - half][j],
-                )
-                copy.start()
-                second[half].append(copy)
-    for half in range(2):
-        for copy in first[half]:
-            copy.wait_send()
-        for copy in second[half]:
+        yield
+        for copy in sent:
             copy.wait()
-
-
-def exp_gather(x):
-    return pl.pallas_call(
-        exp_gather_kernel,
-        out_shape=jax.ShapeDtypeStruct((16, 64, D), BF16),
-        in_specs=[in_vmem()],
-        out_specs=in_vmem(),
-        scratch_shapes=[
-            pltpu.SemaphoreType.DMA((2, 3)),
-            pltpu.SemaphoreType.DMA((2, 3)),
-            pltpu.SemaphoreType.DMA((2, 4, 3)),
-            pltpu.SemaphoreType.DMA((2, 4, 3)),
+        piece[...] = piece[...] + ((held[0] + held[1]) + held[2])
+        yield from exp_gather_steps(piece, small_ref, gather_send, gather_recv)
+        copies[0].wait_send()
+
+    return Part(
+        [first.reshape(4, 4, 64, WIDE), second.reshape(4, 4, 64, WIDE)],
+        [in_vmem()] * 2,
+        [
+            jax.ShapeDtypeStruct((64, 768), F32),
+            jax.ShapeDtypeStruct((4, 4, 64, LANES), F32),
         ],
-        compiler_params=comm_params(4),
-        name="exp_gather",
-    )(x)
-
-
-def exp_scatter_kernel(
-    x_ref, out_ref, held_one, ready, held_two, send_one, recv_one, send_two, recv_two
-):
-    me, at_x, at_z = exp_places()
-    to_x = [lax.rem(at_x + j, 4) for j in (1, 2, 3)]
-    to_z = [lax.rem(at_z + j, 4) for j in (1, 2, 3)]
-    peers = [[{"exp": x * 4 + at_z} for x in to_x], [{"exp": at_x * 4 + z} for z in to_z]]
-    greet(peers[0] + peers[1])
-    rows = [pl.ds(0, 32), pl.ds(32, 32)]
-    first = [[], []]
-    second = [[], []]
-    for j in range(3):
-        for half in range(2):
-            src = (
-                x_ref.at[to_x[j], :, rows[0]] if half == 0 else x_ref.at[:, to_z[j], rows[1]]
-            )
-            copy = remote(
-                src, held_one.at[half, j], send_one.at[half, j], recv_one.at[half, j], peers[half][j]
-            )
-            copy.start()
-            first[half].append(copy)
-    for half in range(2):
-        for j in range(3):
-            first[half][j].wait_recv()
-        for j in range(3):
-            to = to_z[j] if half == 0 else to_x[j]
-            own = x_ref[at_x, to, rows[0]] if half == 0 else x_ref[to, at_z, rows[1]]
-            total = own.astype(F32)
-            for k in range(3):
-                total = total + held_one[half, k, to].astype(F32)
-            ready[half, j] = total.astype(BF16)
-            copy = remote(
-                ready.at[half, j],
-                held_two.at[half, j],
-                send_two.at[half, j],
-                recv_two.at[half, j],
-                peers[1 - half][j],
-            )
-            copy.start()
-            second[half].append(copy)
-    for half in range(2):
-        total = x_ref[at_x, at_z, rows[half]].astype(F32)
-        mine = at_z if half == 0 else at_x
-        for k in range(3):
-            total = total + held_one[half, k, mine].astype(F32)
-        for k in range(3):
-            second[half][k].wait_recv()
-            total = total + held_two[half, k].astype(F32)
-        out_ref[rows[half]] = total
-    for half in range(2):
-        for copy in first[half] + second[half]:
-            copy.wait_send()
-
-
-def exp_scatter(x, number):
-    width = x.shape[-1]
-    return pl.pallas_call(
-        exp_scatter_kernel,
-        out_shape=jax.ShapeDtypeStruct((64, width), F32),
-        in_specs=[in_vmem()],
-        out_specs=in_vmem(),
-        scratch_shapes=[
-            pltpu.VMEM((2, 3, 4, 32, width), BF16),
-            pltpu.VMEM((2, 3, 32, width), BF16),
-            pltpu.VMEM((2, 3, 32, width), BF16),
+        [in_vmem()] * 2,
+        [
+            pltpu.VMEM((4, 4, 64, WIDE), BF16),
+            pltpu.VMEM((4, 4, 64, WIDE), BF16),
+            pltpu.VMEM((64, WIDE), F32),
+            pltpu.VMEM((64, LANES), F32),
+            pltpu.VMEM((3, 64, LANES), F32),
         ]
-        + [pltpu.SemaphoreType.DMA((2, 3))] * 4,
-        compiler_params=comm_params(number),
-        name="exp_scatter%d" % number,
-    )(x.reshape(4, 4, 64, width))
+        + exp_scatter_scratch(WIDE)
+        + [pltpu.SemaphoreType.DMA((1,))] * 2
+        + sems(3)
+        + sems(2, 5, 4),
+        ["section", "x", "z", "tp", "tp_opposite"],
+        body,
+    )
 
 
 def half_swapped(values):
@@ -580,7 +893,7 @@
 
     @pl.when(e == 1)
     def _():
-        dr_ref[...] = dot_tn(gl[...].astype(BF16), x_ref[...])[:E]
+        dr_ref[...] = dot_tn(x_ref[...], gl[...].astype(BF16))
 
 
 def experts_backward(x, g, gu, wgu, wd, router, mask, sel, layer):
@@ -592,7 +905,7 @@
             jax.ShapeDtypeStruct((count, D), BF16),
             jax.ShapeDtypeStruct((2, D, 2 * F), BF16),
             jax.ShapeDtypeStruct((2, F, D), BF16),
-            jax.ShapeDtypeStruct((E, D), F32),
+            jax.ShapeDtypeStruct((D, LANES), F32),
         ],
         in_specs=[
             whole(count, D),
@@ -608,7 +921,7 @@
             whole(count, D),
             pl.BlockSpec((1, D, 2 * F), lambda e: (e, 0, 0)),
             pl.BlockSpec((1, F, D), lambda e: (e, 0, 0)),
-            whole(E, D),
+            whole(D, LANES),
         ],
         scratch_shapes=[
             pltpu.VMEM((count, LANES), F32),
@@ -629,50 +942,73 @@
 def layer_forward(layer_in, layer, common, weights):
     tables, mask_own, mask_all, sel = common
     wqkv, wo, gains, router, wgu, wd = weights
+    unpaired = wgu.shape[0] == 1
     inverse_one = inverse_rms(layer_in)
     normed = (layer_in * inverse_one * gains[layer, 0:1]).astype(BF16)
-    rows = tp_gather(normed.reshape(2, 32, D)).reshape(256, D)
+    rows = fuse([tp_gather_part(normed.reshape(2, 32, D))], 2, "tp_gather")[0].reshape(256, D)
     part, qkv, att = attention_forward(rows, wqkv, wo, tables, layer)
-    after = layer_in + tp_scatter(part).reshape(64, D)
+    after = layer_in + fuse([tp_scatter_part(part)], 3, "tp_scatter")[0].reshape(64, D)
     inverse_two = inverse_rms(after)
     normed_two = (after * inverse_two * gains[layer, 1:2]).astype(BF16)
-    x_all = exp_gather(normed_two).reshape(1024, D)
+    if unpaired:
+        x_all, (wgu, wd) = fuse([exp_gather_part(normed_two), pair_part([wgu, wd])], 1, "gather_pair")
+    else:
+        (x_all,) = fuse([exp_gather_part(normed_two)], 4, "exp_gather")
+    x_all = x_all.reshape(1024, D)
     made, gu = experts_forward(x_all, wgu, wd, router, mask_all, sel, layer)
-    y = exp_scatter(made, 5)
+    (y,) = fuse([exp_scatter_part(made)], 5, "exp_scatter")
     stored = (layer_in, inverse_one, rows, qkv, att, after, inverse_two, normed_two, x_all, gu, y)
-    return after + y, stored
-
-
-def layer_backward(grad, stored, layer, common, weights):
+    return after + y, stored, (wgu, wd)
+
+
+def layer_backward(grad, stored, layer, common, weights, pending):
     tables, mask_own, mask_all, sel = common
     wqkv, wo, gains, router, wgu, wd = weights
     layer_in, inverse_one, rows, qkv, att, after, inverse_two, normed_two, x_all, gu, y = stored
-    g_all = exp_gather(grad).reshape(1024, D)
+    done = []
+    if layer == 1:
+        (g_all,) = fuse([exp_gather_part(grad)], 4, "exp_gather")
+    else:
+        g_all, more = fuse([exp_gather_part(grad), expert_part(*pending[0])], 7, "gather_expert")
+        done.append(more)
+    g_all = g_all.reshape(1024, D)
     dx, dgu, dd, dr = experts_backward(x_all, g_all, gu, wgu, wd, router, mask_all, sel, layer)
+    pending = [(dgu, 0), (dgu, 512), (dd, 0)]
     gates = masked_softmax(dot(normed_two, router[layer]), mask_own)
     gf = grad.astype(F32)
     gc = (gates * jnp.sum(gf * y, axis=1, keepdims=True)).astype(BF16)
-    grad_n = exp_scatter(dx, 5) - dot_nt(gc, router[layer])
-    dr = dr - dot_tn(gc, normed_two)[:E]
+    count = 2 if layer == 1 else 1
+    results = fuse(
+        [exp_scatter_part(dx)] + [expert_part(*piece) for piece in pending[:count]],
+        8 + layer,
+        "scatter_expert",
+    )
+    done += results[1:]
+    pending = pending[count:]
+    grad_n = results[0] - dot_nt(gc, router[layer])
+    dr = dr - dot_tn(normed_two, gc)
     scaled = grad_n * gains[layer, 1:2]
     grad_after = (
         gf
         + inverse_two * scaled
         - after * inverse_two**3 * jnp.mean(after * scaled, axis=1, keepdims=True)
     )
-    d_mixture = jnp.sum(grad_n * after * inverse_two, axis=0, keepdims=True)
-    ga = tp_gather(grad_after.astype(BF16).reshape(2, 32, D)).reshape(256, D)
+    d_mixture = jnp.sum(grad_n * after * inverse_two, axis=0)
+    ga = grad_after.astype(BF16).reshape(2, 32, D)
+    ga = fuse([tp_gather_part(ga)], 2, "tp_gather")[0].reshape(256, D)
     dn, dw = attention_backward(rows, ga, qkv, att, wqkv, wo, tables, layer)
-    grad_n = tp_scatter(dn).reshape(64, D)
+    grad_n = fuse([tp_scatter_part(dn)], 3, "tp_scatter")[0].reshape(64, D)
     scaled = grad_n * gains[layer, 0:1]
     grad_in = (
         grad_after
         + inverse_one * scaled
         - layer_in * inverse_one**3 * jnp.mean(layer_in * scaled, axis=1, keepdims=True)
     )
-    d_attention = jnp.sum(grad_n * layer_in * inverse_one, axis=0, keepdims=True)
-    small = jnp.concatenate([dr, d_attention, d_mixture, jnp.zeros((6, D), F32)], axis=0)
-    return grad_in, (dgu, dd, dw, small)
+    d_attention = jnp.sum(grad_n * layer_in * inverse_one, axis=0)
+    lane = jnp.arange(LANES)[None, :]
+    small = jnp.where(lane == E, d_attention[:, None], jnp.where(lane == E + 1, d_mixture[:, None], dr))
+    wide = jnp.concatenate([dw, small.astype(BF16)], axis=1)
+    return grad_in, wide, done, pending
 
 
 def rope_tables(seg_rows):
@@ -736,9 +1072,8 @@
         [attention_gain, mixture_gain, jnp.zeros((6, D), BF16)], axis=0
     ).astype(F32)[None]
     router_own = jnp.pad(router_weight, ((0, 0), (0, 0), (0, LANES - E)))
-    wqkv, wo, gains, router = pair_gather([qkv_own, output_weight, gains_own, router_own], 0)
-    wgu, wd = pair_gather([expert_gate_up, expert_down], 1)
-    weights = (wqkv, wo, gains, router, wgu, wd)
+    (paired,) = fuse([pair_part([qkv_own, output_weight, gains_own, router_own])], 0, "pair")
+    weights = tuple(paired) + (expert_gate_up, expert_down)
 
     cosine, sine, mask = jax.vmap(rope_tables)(own_batches(segments))
     tables = (cosine.reshape(256, LANES), sine.reshape(256, LANES), mask)
@@ -749,37 +1084,45 @@
     common = (tables, routed(routes_own), routed(routes_all), sel)
 
     start = own_batches(activations).reshape(64, D).astype(F32)
-    result, kept_first = layer_forward(start, 0, common, weights)
+    result, kept_first, experts = layer_forward(start, 0, common, weights)
+    weights = tuple(paired) + tuple(experts)
     out_first = result.astype(BF16)
-    result, kept_second = layer_forward(out_first.astype(F32), 1, common, weights)
+    result, kept_second, _ = layer_forward(out_first.astype(F32), 1, common, weights)
     out_second = result.astype(BF16)
     grad = own_batches(cotangent).reshape(64, D)
-    grad_second, pieces_second = layer_backward(grad, kept_second, 1, common, weights)
-    grad_first, pieces_first = layer_backward(
-        grad_second.astype(BF16), kept_first, 0, common, weights
-    )
-
-    def summed(first, second):
+    grad_second, wide_second, done_second, pending = layer_backward(
+        grad, kept_second, 1, common, weights, []
+    )
+    grad_first, wide_first, done_first, pending = layer_backward(
+        grad_second.astype(BF16), kept_first, 0, common, weights, pending
+    )
+    done_second.append(done_first.pop(0))
+    (dw, small), *rest = fuse(
+        [settle_part(wide_first, wide_second)] + [expert_part(*piece) for piece in pending],
+        6,
+        "settle",
+    )
+    done_first += rest
+    small = small.reshape(D, LANES)
+    experts = []
+    for first, second in zip(done_first, done_second):
         kept, got = to_owner(first, second)
-        return kept.astype(F32) + got.astype(F32)
-
-    dgu, dd, dw, small = [summed(a, b) for a, b in zip(pieces_first, pieces_second)]
-    dgu = lax.psum_scatter(dgu.astype(BF16), "tp", scatter_dimension=2, tiled=True)
-    dd = lax.psum_scatter(dd.astype(BF16), "tp", scatter_dimension=2, tiled=True)
-    dw = exp_scatter(dw.astype(BF16), 6)
-    small = lax.psum(small, ("exp", "tp"))
+        kept, got = kept.astype(F32), got.astype(F32)
+        experts.append(
+            jnp.where(section == 0, jnp.stack([kept, got]), jnp.stack([got, kept]))[None]
+        )
     return (
         by_layer(out_first, out_second),
         by_layer(grad_first, grad_second),
-        small[E : E + 1],
+        small[:, E][None],
         dw[None, :, :256],
         dw[None, :, 256:384],
         dw[None, :, 384:512],
         dw[:, 512:].T[None],
-        small[E + 1 : E + 2],
-        small[:E].T[None],
-        dgu.astype(F32)[None],
-        dd.astype(F32)[None],
+        small[:, E + 1][None],
+        small[None, :, :E],
+        jnp.concatenate(experts[:2], axis=2),
+        experts[2],
     )
 
 

time: 899 us -> 545 us (0.61)
  Pallas kernels: 636 us -> 419 us
  waiting for transfers between devices: 126 us -> 0.01 us
  starting transfers between devices: 7.46 us -> 31.3 us
  other arithmetic: 63.2 us -> 47.7 us
  between operations: 16.5 us -> 1.57 us
    pallas_call x19 -> x18, Pallas kernels: 524 us -> 306 us  [fuse(): pl.pallas_call(functools.partial(fused_kernel, parts), out_shape=[o for p...]
    psum x1 -> x0, waiting for transfers between devices: 121 us -> none  [per_device(): small = lax.psum(small, ('exp', 'tp'))]
    ppermute x6 -> x5, starting transfers between devices: 7.09 us -> 31.3 us  [to_owner(): return (kept, lax.ppermute(sent, 'section', [(0, 1), (1, 0)]))]
    convert_element_type x7 -> x2, other arithmetic: 18 us -> 1.6 us  [layer_backward(): ga = grad_after.astype(BF16).reshape(2, 32, D)]
    select_n x4 -> x3, other arithmetic: 10.6 us -> 1.18 us  [per_device(): jnp.where(section == 0, jnp.stack([kept, got]), jnp.stack([got, kept]))]
  transfers between devices with their start and end apart: 9 -> 5, of which waited for: 3 -> 0; matrix products, arithmetic and copies ran while one was open for 4% -> 6% of each run, Pallas kernels for 7% -> 49%
where the time goes in v2:
time: 545 us; the launch traced here: 535 us
  Pallas kernels  419 us (77%)
  other arithmetic  47.7 us (9%)
  starting transfers between devices  31.3 us (6%)
  blocking collectives  20.3 us (4%)
  local copies, waits for them, and re-layouts  10.1 us (2%)
    pallas_call x18, Pallas kernels, fuse(): pl.pallas_call(functools.partial(fused_kernel, parts), out_shape=[o for p...  306 us
    pallas_call x2, Pallas kernels, experts_backward(): pl.pallas_call(experts_backward_kernel, grid=(2,), out_shape=[jax.ShapeDt...  61.5 us
    ppermute x5, starting transfers between devices, to_owner(): return (kept, lax.ppermute(sent, 'section', [(0, 1), (1, 0)]))  31.3 us
    pallas_call x2, Pallas kernels, experts_forward(): pl.pallas_call(experts_forward_kernel, grid=(count // tile,), out_shape=[...  25.2 us
    all_gather x1, blocking collectives, per_device(): routes_all = lax.all_gather(routes_own, 'exp', axis=0, tiled=True)  20.3 us
    pallas_call x2, Pallas kernels, attention_backward(): pl.pallas_call(attention_backward_kernel, grid=(1,), out_shape=[jax.Shape...  15.1 us
    pallas_call x2, Pallas kernels, attention_forward(): pl.pallas_call(attention_forward_kernel, grid=(1,), out_shape=[jax.ShapeD...  11.3 us
  transfers between devices with their start and end apart: 5, of which 0 were waited for; matrix products, arithmetic and copies ran while one was open for 6% of the time, Pallas kernels for 49%

profile of v2, /device:TPU:1, one launch (start us, length us, event | category | flops | bytes accessed | tf_op | source)
XLA Modules:
  0.0 535.5 jit_solution(9006823120763463680)
XLA Ops:
  4.2 20.3 %all-gather = s32[16,64,8]{1,2,0:T(8,128)S(1)} all-gather(s32[1,64,8]{1,2,0:T(8,128)S(1)} %reshape.687), channel_id=1, replica_groups=mesh['section'=2,'exp'=16,'tp'=4] {'exp'}, dimensions={0}, use_global_device_ids=true | all-gather | bytes 34816 | tf_op jit(solution)/shard_map/all_gather | solution.py:1081
  26.5 6.6 %convert_reduce_fusion.mask_ref = f32[1024,128]{1,0:T(8,128)} fusion(s32[1024,8]{1,0:T(8,128)S(1)} %bitcast.166), kind=kLoop, calls=%fused_computation | loop fusion | flops 3014656 | bytes 557056 | tf_op jit(solution)/shard_map/reduce_sum | solution.py:1032
  35.7 10.1 %pair.1 = (bf16[2,1024,512]{2,1,0:T(8,128)(2,1)}, bf16[2,256,1024]{2,1,0:T(8,128)(2,1)}, f32[2,8,1024]{2,1,0:T(8,128)}, bf16[2,1024,128]{2,1,0:T(8,128)(2,1)}) custom-call(bf16[1,1024,512]{2,1,0:T(8,128)(2,1)} %pad_maximum_fusion.3.refs_0_, bf16[1,256,1024]{2,1,0:T(8,128)(2,1)} %refs_1_.2, f32[1,8,1024]{2,1,0:T(8,128)} %maximum_convert_fusion.refs_2_, ...), custom_call_target="tpu_custom_call" | custom-call | tf_op jit(solution)/shard_map/pair/pallas_call | solution.py:114
  47.4 10.9 %tp_gather.4 = bf16[2,128,1024]{2,1,0:T(8,128)(2,1)} custom-call(bf16[2,32,1024]{2,1,0:T(8,128)(2,1)} %fusion.8.refs_0_), custom_call_target="tpu_custom_call" | custom-call | tf_op jit(solution)/shard_map/tp_gather/pallas_call | solution.py:114
  59.8 5.6 %attention_forward.2 = (bf16[2,128,1024]{2,1,0:T(8,128)(2,1)}, bf16[256,512]{1,0:T(8,128)(2,1)}, bf16[256,256]{1,0:T(8,128)(2,1)}) custom-call(bf16[256,1024]{1,0:T(8,128)(2,1)} %bitcast.154, bf16[2,1024,512]{2,1,0:T(8,128)(2,1)} %get-tuple-element.52.wqkv_ref, bf16[2,256,1024]{2,1,0:T(8,128)(2,1)} %get-tuple-element.53.wo_ref, ...), custom_call_target="tpu_custom_call" | custom-call | tf_op jit(solution)/shard_map/attention_forward/pallas_call | solution.py:680
  65.4 9.4 %tp_scatter.4 = f32[2,32,1024]{2,1,0:T(8,128)} custom-call(bf16[2,128,1024]{2,1,0:T(8,128)(2,1)} %get-tuple-element.54.refs_0_), custom_call_target="tpu_custom_call" | custom-call | tf_op jit(solution)/shard_map/tp_scatter/pallas_call | solution.py:114
  76.0 1.7 multiply_convert_fusion.2
  77.7 21.0 %gather_pair.1 = (bf16[4,4,64,1024]{3,2,1,0:T(8,128)(2,1)}, bf16[2,2,1024,1024]{3,2,1,0:T(8,128)(2,1)}, bf16[2,2,512,1024]{3,2,1,0:T(8,128)(2,1)}) custom-call(bf16[64,1024]{1,0:T(8,128)(2,1)} %get-tuple-element.110.refs_0_, bf16[1,2,1024,1024]{3,2,1,0:T(8,128)(2,1)} %refs_1_.3, bf16[1,2,512,1024]{3,2,1,0:T(8,128)(2,1)} %refs_2_.1), custom_call_target="tpu_custom_call" | custom-call | tf_op jit(solution)/shard_map/gather_pair/pallas_call | solution.py:114
  98.7 12.4 %experts_forward.2 = (bf16[1024,1024]{1,0:T(8,128)(2,1)}, bf16[2,1024,1024]{2,1,0:T(8,128)(2,1)}) custom-call(bf16[1024,1024]{1,0:T(8,128)(2,1)} %bitcast.147, bf16[2,2,1024,1024]{3,2,1,0:T(8,128)(2,1)} %get-tuple-element.56.wgu_ref, bf16[2,2,512,1024]{3,2,1,0:T(8,128)(2,1)} %get-tuple-element.57.wd_ref, bf16[2,1024,128]{2,1,0:T(8,128)(2,1)} %get-tuple-element.58.router_ref, ...), custom_call_target="tpu_custom_call" | custom-call | tf_op jit(solution)/shard_map/experts_forward/pallas_call | solution.py:803
  111.2 19.2 %exp_scatter.2 = f32[64,1024]{1,0:T(8,128)} custom-call(bf16[4,4,64,1024]{3,2,1,0:T(8,128)(2,1)} %bitcast.164), custom_call_target="tpu_custom_call" | custom-call | tf_op jit(solution)/shard_map/exp_scatter/pallas_call | solution.py:114
  132.2 9.2 %tp_gather.5 = bf16[2,128,1024]{2,1,0:T(8,128)(2,1)} custom-call(bf16[2,32,1024]{2,1,0:T(8,128)(2,1)} %bitcast.171), custom_call_target="tpu_custom_call" | custom-call | tf_op jit(solution)/shard_map/tp_gather/pallas_call | solution.py:114
  141.5 5.6 %attention_forward.3 = (bf16[2,128,1024]{2,1,0:T(8,128)(2,1)}, bf16[256,512]{1,0:T(8,128)(2,1)}, bf16[256,256]{1,0:T(8,128)(2,1)}) custom-call(bf16[256,1024]{1,0:T(8,128)(2,1)} %bitcast.156, bf16[2,1024,512]{2,1,0:T(8,128)(2,1)} %get-tuple-element.52.wqkv_ref, bf16[2,256,1024]{2,1,0:T(8,128)(2,1)} %get-tuple-element.53.wo_ref, ...), custom_call_target="tpu_custom_call" | custom-call | tf_op jit(solution)/shard_map/attention_forward/pallas_call | solution.py:680
  147.1 8.7 %tp_scatter.5 = f32[2,32,1024]{2,1,0:T(8,128)} custom-call(bf16[2,128,1024]{2,1,0:T(8,128)(2,1)} %get-tuple-element.60.refs_0_), custom_call_target="tpu_custom_call" | custom-call | tf_op jit(solution)/shard_map/tp_scatter/pallas_call | solution.py:114
  156.9 1.7 multiply_convert_fusion.1.refs_0_
  158.6 15.7 %exp_gather.2 = bf16[4,4,64,1024]{3,2,1,0:T(8,128)(2,1)} custom-call(bf16[64,1024]{1,0:T(8,128)(2,1)} %multiply_convert_fusion.1.refs_0_), custom_call_target="tpu_custom_call" | custom-call | tf_op jit(solution)/shard_map/exp_gather/pallas_call | solution.py:114
  174.3 12.7 %experts_forward.3 = (bf16[1024,1024]{1,0:T(8,128)(2,1)}, bf16[2,1024,1024]{2,1,0:T(8,128)(2,1)}) custom-call(bf16[1024,1024]{1,0:T(8,128)(2,1)} %bitcast.145, bf16[2,2,1024,1024]{3,2,1,0:T(8,128)(2,1)} %get-tuple-element.56.wgu_ref, bf16[2,2,512,1024]{3,2,1,0:T(8,128)(2,1)} %get-tuple-element.57.wd_ref, bf16[2,1024,128]{2,1,0:T(8,128)(2,1)} %get-tuple-element.58.router_ref, ...), custom_call_target="tpu_custom_call" | custom-call | tf_op jit(solution)/shard_map/experts_forward/pallas_call | solution.py:803
  187.0 18.6 %exp_scatter.3 = f32[64,1024]{1,0:T(8,128)} custom-call(bf16[4,4,64,1024]{3,2,1,0:T(8,128)(2,1)} %bitcast.165), custom_call_target="tpu_custom_call" | custom-call | tf_op jit(solution)/shard_map/exp_scatter/pallas_call | solution.py:114
  205.6 1.7 broadcast_select_fusion.6
  207.4 18.0 %collective-permute-start = (bf16[64,1024]{1,0:T(8,128)(2,1)}, bf16[64,1024]{1,0:T(8,128)(2,1)}, u32[]{:S(2)}, u32[]{:S(2)}) collective-permute-start(bf16[64,1024]{1,0:T(8,128)(2,1)} %get-tuple-element.115), channel_id=1, source_target_pairs={{0,64},{64,0},{1,65},{65,1},{2,66},{66,2},{3,67},{67,3},{4,68},{68... | collective-permute-start | bytes 393224 | tf_op jit(solution)/shard_map/ppermute | solution.py:1059
  227.0 19.3 %exp_gather.3 = bf16[4,4,64,1024]{3,2,1,0:T(8,128)(2,1)} custom-call(bf16[64,1024]{1,0:T(8,128)(2,1)} %bitcast.163), custom_call_target="tpu_custom_call" | custom-call | tf_op jit(solution)/shard_map/exp_gather/pallas_call | solution.py:114
  246.9 30.6 %experts_backward.2 = (bf16[1024,1024]{1,0:T(8,128)(2,1)}, bf16[2,1024,1024]{2,1,0:T(8,128)(2,1)}, bf16[2,512,1024]{2,1,0:T(8,128)(2,1)}, f32[1024,128]{1,0:T(8,128)}) custom-call(bf16[1024,1024]{1,0:T(8,128)(2,1)} %bitcast.146, bf16[1024,1024]{1,0:T(8,128)(2,1)} %bitcast.149, bf16[2,1024,1024]{2,1,0:T(8,128)(2,1)} %get-tuple-element.62.gu_ref, ...), custom_call_target="tpu_custom_call" | custom-call | tf_op jit(solution)/shard_map/experts_backward/pallas_call | solution.py:901
  277.5 30.1 %scatter_expert.2 = (f32[64,1024]{1,0:T(8,128)}, bf16[512,256]{1,0:T(8,128)(2,1)}, bf16[512,256]{1,0:T(8,128)(2,1)}) custom-call(bf16[4,4,64,1024]{3,2,1,0:T(8,128)(2,1)} %bitcast.160, bf16[2,1024,1024]{2,1,0:T(8,128)(2,1)} %get-tuple-element.64.refs_1_.refs_2_, bf16[2,1024,1024]{2,1,0:T(8,128)(2,1)} %get-tuple-element.64.refs_1_.refs_2_), custom_call_target="tpu_custom_call" | custom-call | tf_op jit(solution)/shard_map/scatter_expert/pallas_call | solution.py:114
  307.8 1.4 multiply_reduce_fusion
  310.0 10.3 %tp_gather.6 = bf16[2,128,1024]{2,1,0:T(8,128)(2,1)} custom-call(bf16[2,32,1024]{2,1,0:T(8,128)(2,1)} %bitcast.169), custom_call_target="tpu_custom_call" | custom-call | tf_op jit(solution)/shard_map/tp_gather/pallas_call | solution.py:114
  320.3 7.5 %attention_backward.2 = (bf16[2,128,1024]{2,1,0:T(8,128)(2,1)}, bf16[1024,768]{1,0:T(8,128)(2,1)}) custom-call(bf16[256,1024]{1,0:T(8,128)(2,1)} %bitcast.157, bf16[256,1024]{1,0:T(8,128)(2,1)} %bitcast.162, bf16[256,512]{1,0:T(8,128)(2,1)} %get-tuple-element.66.qkv_ref, bf16[256,256]{1,0:T(8,128)(2,1)} %get-tuple-element.67.att_ref, ...), custom_call_target="tpu_custom_call" | custom-call | tf_op jit(solution)/shard_map/attention_backward/pallas_call | solution.py:754
  327.9 8.3 %tp_scatter.6 = f32[2,32,1024]{2,1,0:T(8,128)} custom-call(bf16[2,128,1024]{2,1,0:T(8,128)(2,1)} %get-tuple-element.68.refs_0_), custom_call_target="tpu_custom_call" | custom-call | tf_op jit(solution)/shard_map/tp_scatter/pallas_call | solution.py:114
  336.2 1.2 fusion.23
  337.3 1.8 fusion.14
  339.2 25.8 %gather_expert.1 = (bf16[4,4,64,1024]{3,2,1,0:T(8,128)(2,1)}, bf16[512,256]{1,0:T(8,128)(2,1)}) custom-call(bf16[64,1024]{1,0:T(8,128)(2,1)} %get-tuple-element.104.refs_0_, bf16[2,512,1024]{2,1,0:T(8,128)(2,1)} %get-tuple-element.69.refs_1_), custom_call_target="tpu_custom_call" | custom-call | tf_op jit(solution)/shard_map/gather_expert/pallas_call | solution.py:114
  365.0 30.9 %experts_backward.3 = (bf16[1024,1024]{1,0:T(8,128)(2,1)}, bf16[2,1024,1024]{2,1,0:T(8,128)(2,1)}, bf16[2,512,1024]{2,1,0:T(8,128)(2,1)}, f32[1024,128]{1,0:T(8,128)}) custom-call(bf16[1024,1024]{1,0:T(8,128)(2,1)} %bitcast.148, bf16[1024,1024]{1,0:T(8,128)(2,1)} %bitcast.158, bf16[2,1024,1024]{2,1,0:T(8,128)(2,1)} %get-tuple-element.71.gu_ref, ...), custom_call_target="tpu_custom_call" | custom-call | tf_op jit(solution)/shard_map/experts_backward/pallas_call | solution.py:901
  395.9 24.0 %scatter_expert.3 = (f32[64,1024]{1,0:T(8,128)}, bf16[512,256]{1,0:T(8,128)(2,1)}) custom-call(bf16[4,4,64,1024]{3,2,1,0:T(8,128)(2,1)} %bitcast.159, bf16[2,1024,1024]{2,1,0:T(8,128)(2,1)} %get-tuple-element.73.refs_1_.refs_2_), custom_call_target="tpu_custom_call" | custom-call | tf_op jit(solution)/shard_map/scatter_expert/pallas_call | solution.py:114
  419.9 1.3 multiply_reduce_fusion.1
  422.0 8.9 %tp_gather.7 = bf16[2,128,1024]{2,1,0:T(8,128)(2,1)} custom-call(bf16[2,32,1024]{2,1,0:T(8,128)(2,1)} %bitcast.170), custom_call_target="tpu_custom_call" | custom-call | tf_op jit(solution)/shard_map/tp_gather/pallas_call | solution.py:114
  431.0 7.6 %attention_backward.3 = (bf16[2,128,1024]{2,1,0:T(8,128)(2,1)}, bf16[1024,768]{1,0:T(8,128)(2,1)}) custom-call(bf16[256,1024]{1,0:T(8,128)(2,1)} %bitcast.155, bf16[256,1024]{1,0:T(8,128)(2,1)} %bitcast.161, bf16[256,512]{1,0:T(8,128)(2,1)} %get-tuple-element.75.qkv_ref, bf16[256,256]{1,0:T(8,128)(2,1)} %get-tuple-element.76.att_ref, ...), custom_call_target="tpu_custom_call" | custom-call | tf_op jit(solution)/shard_map/attention_backward/pallas_call | solution.py:754
  438.5 9.0 %tp_scatter.7 = f32[2,32,1024]{2,1,0:T(8,128)} custom-call(bf16[2,128,1024]{2,1,0:T(8,128)(2,1)} %get-tuple-element.77.refs_0_), custom_call_target="tpu_custom_call" | custom-call | tf_op jit(solution)/shard_map/tp_scatter/pallas_call | solution.py:114
  448.7 1.8 broadcast_select_fusion.4
  450.5 8.6 %collective-permute-start.1 = (f32[64,1024]{1,0:T(8,128)}, f32[64,1024]{1,0:T(8,128)}, u32[]{:S(2)}, u32[]{:S(2)}) collective-permute-start(f32[64,1024]{1,0:T(8,128)} %get-tuple-element.113), channel_id=1, source_target_pairs={{0,64},{64,0},{1,65},{65,1},{2,66},{66,2},{3,67},{67,3},{4,68},{68... | collective-permute-start | bytes 786440 | tf_op jit(solution)/shard_map/ppermute | solution.py:1059
  459.1 1.5 fusion.5
  460.7 1.4 pad_maximum_fusion.2
  462.9 1.4 pad_maximum_fusion.1
  464.3 47.8 %settle.1 = (f32[64,768]{1,0:T(8,128)}, f32[4,4,64,128]{3,2,1,0:T(8,128)}, bf16[512,256]{1,0:T(8,128)(2,1)}, bf16[512,256]{1,0:T(8,128)(2,1)}) custom-call(bf16[4,4,64,896]{3,2,1,0:T(8,128)(2,1)} %bitcast.151, bf16[4,4,64,896]{3,2,1,0:T(8,128)(2,1)} %bitcast.150, bf16[2,1024,1024]{2,1,0:T(8,128)(2,1)} %get-tuple-element.73.refs_1_.refs_2_, ...), custom_call_target="tpu_custom_call" | custom-call | tf_op jit(solution)/shard_map/settle/pallas_call | solution.py:114
  512.2 1.8 bitcast_convert_fusion.2
  514.0 4.2 collective-permute-start.3
  518.2 1.7 bitcast_convert_fusion
  524.6 1.4 slice_bitcast_fusion.2
  526.0 1.7 maximum_select_fusion.4
  529.8 1.9 maximum_select_fusion.3
  533.8 1.5 pad_maximum_fusion
  (129 shorter events, 30.1 us)
Async XLA Ops:
  0.6 225.2 %copy-start = (bf16[4,32,1024]{2,1,0:T(8,128)(2,1)S(1)}, bf16[4,32,1024]{2,1,0:T(8,128)(2,1)}, u32[]{:S(2)}) copy-start(bf16[4,32,1024]{2,1,0:T(8,128)(2,1)} %param.14) | copy-start | bytes 786436
  0.7 33.2 %copy-start.25 = (bf16[1,1024]{1,0:T(2,128)(2,1)S(1)}, bf16[1,1024]{1,0:T(2,128)(2,1)}, u32[]{:S(2)}) copy-start(bf16[1,1024]{1,0:T(2,128)(2,1)} %param.22) | copy-start | bytes 6148
  0.7 33.2 %copy-start.26 = (bf16[1,1024]{1,0:T(2,128)(2,1)S(1)}, bf16[1,1024]{1,0:T(2,128)(2,1)}, u32[]{:S(2)}) copy-start(bf16[1,1024]{1,0:T(2,128)(2,1)} %param.17) | copy-start | bytes 6148
  0.7 33.9 %copy-start.22 = (bf16[1,1024,128]{2,1,0:T(8,128)(2,1)S(1)}, bf16[1,1024,128]{2,1,0:T(8,128)(2,1)}, u32[]{:S(2)}) copy-start(bf16[1,1024,128]{2,1,0:T(8,128)(2,1)} %param.20) | copy-start | bytes 786436
  0.7 33.9 %copy-start.23 = (bf16[1,1024,128]{2,1,0:T(8,128)(2,1)S(1)}, bf16[1,1024,128]{2,1,0:T(8,128)(2,1)}, u32[]{:S(2)}) copy-start(bf16[1,1024,128]{2,1,0:T(8,128)(2,1)} %param.19) | copy-start | bytes 786436
  0.7 33.9 %copy-start.17 = (bf16[1,1024,256]{2,1,0:T(8,128)(2,1)S(1)}, bf16[1,1024,256]{2,1,0:T(8,128)(2,1)}, u32[]{:S(2)}) copy-start(bf16[1,1024,256]{2,1,0:T(8,128)(2,1)} %param.18) | copy-start | bytes 1572868
  33.8 12.8 %copy-start.8 = (bf16[4,32,1024]{2,1,0:T(8,128)(2,1)S(1)}, bf16[4,32,1024]{2,1,0:T(8,128)(2,1)}, u32[]{:S(2)}) copy-start(bf16[4,32,1024]{2,1,0:T(8,128)(2,1)} %param.13) | copy-start | bytes 786436
  187.0 18.6 %copy-start.5 = (f32[2,32,1024]{2,1,0:T(8,128)S(1)}, f32[2,32,1024]{2,1,0:T(8,128)}, u32[]{:S(2)}) copy-start(f32[2,32,1024]{2,1,0:T(8,128)} %tp_scatter.5) | copy-start | bytes 786436
  187.0 38.5 %copy-start.7 = (f32[2,32,1024]{2,1,0:T(8,128)S(1)}, f32[2,32,1024]{2,1,0:T(8,128)}, u32[]{:S(2)}) copy-start(f32[2,32,1024]{2,1,0:T(8,128)} %tp_scatter.4) | copy-start | bytes 786436
  205.6 40.7 %copy-start.2 = (bf16[2,1024,128]{2,1,0:T(8,128)(2,1)S(1)}, bf16[2,1024,128]{2,1,0:T(8,128)(2,1)}, u32[]{:S(2)}) copy-start(bf16[2,1024,128]{2,1,0:T(8,128)(2,1)} %get-tuple-element.58.router_ref) | copy-start | bytes 1572868
  205.6 40.7 %copy-start.15 = (bf16[64,1024]{1,0:T(8,128)(2,1)S(1)}, bf16[64,1024]{1,0:T(8,128)(2,1)}, u32[]{:S(2)}) copy-start(bf16[64,1024]{1,0:T(8,128)(2,1)} %multiply_convert_fusion.1.refs_0_) | copy-start | bytes 393220
  207.4 318.6 %collective-permute-start = (bf16[64,1024]{1,0:T(8,128)(2,1)}, bf16[64,1024]{1,0:T(8,128)(2,1)}, u32[]{:S(2)}, u32[]{:S(2)}) collective-permute-start(bf16[64,1024]{1,0:T(8,128)(2,1)} %get-tuple-element.115), channel_id=1, source_target_pairs={{0,64},{64,0},{1,65},{65,1},{2,66},{66,2},{3,67},{67,3},{4,68},{68... | collective-permute-start | bytes 393224 | tf_op jit(solution)/shard_map/ppermute | solution.py:1059
  225.8 1.1 copy-start.10
  277.5 30.3 %copy-start.3 = (bf16[2,1024,128]{2,1,0:T(8,128)(2,1)S(1)}, bf16[2,1024,128]{2,1,0:T(8,128)(2,1)}, u32[]{:S(2)}) copy-start(bf16[2,1024,128]{2,1,0:T(8,128)(2,1)} %get-tuple-element.58.router_ref) | copy-start | bytes 1572868
  277.5 31.7 %copy-start.11 = (bf16[2,32,1024]{2,1,0:T(8,128)(2,1)S(1)}, bf16[2,32,1024]{2,1,0:T(8,128)(2,1)}, u32[]{:S(2)}) copy-start(bf16[2,32,1024]{2,1,0:T(8,128)(2,1)} %copy-done.10) | copy-start | bytes 393220
  320.3 17.0 %copy-start.9 = (f32[64,1024]{1,0:T(8,128)S(1)}, f32[64,1024]{1,0:T(8,128)}, u32[]{:S(2)}) copy-start(f32[64,1024]{1,0:T(8,128)} %exp_scatter.2) | copy-start | bytes 786436
  395.8 24.0 %copy-start.4 = (bf16[2,1024,128]{2,1,0:T(8,128)(2,1)S(1)}, bf16[2,1024,128]{2,1,0:T(8,128)(2,1)}, u32[]{:S(2)}) copy-start(bf16[2,1024,128]{2,1,0:T(8,128)(2,1)} %get-tuple-element.58.router_ref) | copy-start | bytes 1572868
  395.9 25.4 %copy-start.14 = (bf16[64,1024]{1,0:T(8,128)(2,1)S(1)}, bf16[64,1024]{1,0:T(8,128)(2,1)}, u32[]{:S(2)}) copy-start(bf16[64,1024]{1,0:T(8,128)(2,1)} %get-tuple-element.104.refs_0_) | copy-start | bytes 393220
  438.5 22.1 %copy-start.12 = (bf16[1024,768]{1,0:T(8,128)(2,1)S(1)}, bf16[1024,768]{1,0:T(8,128)(2,1)}, u32[]{:S(2)}) copy-start(bf16[1024,768]{1,0:T(8,128)(2,1)} %get-tuple-element.80) | copy-start | bytes 4718596
  450.5 79.3 %collective-permute-start.1 = (f32[64,1024]{1,0:T(8,128)}, f32[64,1024]{1,0:T(8,128)}, u32[]{:S(2)}, u32[]{:S(2)}) collective-permute-start(f32[64,1024]{1,0:T(8,128)} %get-tuple-element.113), channel_id=1, source_target_pairs={{0,64},{64,0},{1,65},{65,1},{2,66},{66,2},{3,67},{67,3},{4,68},{68... | collective-permute-start | bytes 786440 | tf_op jit(solution)/shard_map/ppermute | solution.py:1059
  460.6 1.5 copy-start.16
  460.6 1.4 copy-start.27
  460.7 2.3 copy-start.13
  464.3 47.8 %copy-start.19 = (bf16[512,256]{1,0:T(8,128)(2,1)S(1)}, bf16[512,256]{1,0:T(8,128)(2,1)}, u32[]{:S(2)}) copy-start(bf16[512,256]{1,0:T(8,128)(2,1)} %get-tuple-element.88) | copy-start | bytes 786436
  464.3 53.9 %copy-start.20 = (bf16[512,256]{1,0:T(8,128)(2,1)S(1)}, bf16[512,256]{1,0:T(8,128)(2,1)}, u32[]{:S(2)}) copy-start(bf16[512,256]{1,0:T(8,128)(2,1)} %get-tuple-element.90) | copy-start | bytes 786436
  512.1 7.8 %copy-start.18 = (bf16[512,256]{1,0:T(8,128)(2,1)S(1)}, bf16[512,256]{1,0:T(8,128)(2,1)}, u32[]{:S(2)}) copy-start(bf16[512,256]{1,0:T(8,128)(2,1)} %get-tuple-element.86) | copy-start | bytes 786436
  512.1 7.8 %copy-start.21 = (bf16[512,256]{1,0:T(8,128)(2,1)S(1)}, bf16[512,256]{1,0:T(8,128)(2,1)}, u32[]{:S(2)}) copy-start(bf16[512,256]{1,0:T(8,128)(2,1)} %get-tuple-element.85) | copy-start | bytes 786436
  512.1 9.1 %copy-start.24 = (f32[64,768]{1,0:T(8,128)S(1)}, f32[64,768]{1,0:T(8,128)}, u32[]{:S(2)}) copy-start(f32[64,768]{1,0:T(8,128)} %get-tuple-element.84) | copy-start | bytes 589828
  512.1 9.7 %copy-start.6 = (f32[4,4,64,128]{3,2,1,0:T(8,128)S(1)}, f32[4,4,64,128]{3,2,1,0:T(8,128)}, u32[]{:S(2)}) copy-start(f32[4,4,64,128]{3,2,1,0:T(8,128)} %get-tuple-element.83) | copy-start | bytes 1572868
  514.0 13.8 %collective-permute-start.3 = (bf16[512,256]{1,0:T(8,128)(2,1)}, bf16[512,256]{1,0:T(8,128)(2,1)}, u32[]{:S(2)}, u32[]{:S(2)}) collective-permute-start(bf16[512,256]{1,0:T(8,128)(2,1)} %get-tuple-element.121), channel_id=1, source_target_pairs={{0,64},{64,0},{1,65},{65,1},{2,66},{66,2},{3,67},{67,3},{4,68},{68... | collective-permute-start | bytes 786440 | tf_op jit(solution)/shard_map/ppermute | solution.py:1059
  519.9 8.9 %collective-permute-start.4 = (bf16[512,256]{1,0:T(8,128)(2,1)}, bf16[512,256]{1,0:T(8,128)(2,1)}, u32[]{:S(2)}, u32[]{:S(2)}) collective-permute-start(bf16[512,256]{1,0:T(8,128)(2,1)} %get-tuple-element.117), channel_id=1, source_target_pairs={{0,64},{64,0},{1,65},{65,1},{2,66},{66,2},{3,67},{67,3},{4,68},{68... | collective-permute-start | bytes 786440 | tf_op jit(solution)/shard_map/ppermute | solution.py:1059
  520.7 12.0 %collective-permute-start.2 = (bf16[512,256]{1,0:T(8,128)(2,1)}, bf16[512,256]{1,0:T(8,128)(2,1)}, u32[]{:S(2)}, u32[]{:S(2)}) collective-permute-start(bf16[512,256]{1,0:T(8,128)(2,1)} %get-tuple-element.119), channel_id=1, source_target_pairs={{0,64},{64,0},{1,65},{65,1},{2,66},{66,2},{3,67},{67,3},{4,68},{68... | collective-permute-start | bytes 786440 | tf_op jit(solution)/shard_map/ppermute | solution.py:1059
  533.7 1.6 copy-start.1

commit v3 on v2

--- a/solution.py
+++ b/solution.py
@@ -639,30 +639,6 @@
     return values[batch * 128 : batch * 128 + 128, first : first + HD]
 
 
-def attention_forward_kernel(
-    rows_ref, wqkv_ref, wo_ref, cos_ref, sin_ref, mask_ref, part_ref, qkv_ref, att_ref
-):
-    joined = dot(rows_ref[...], wqkv_ref[0])
-    turned = joined[:, :384]
-    turned = turned * three(cos_ref[...]) + half_swapped(turned) * three(sin_ref[...])
-    qkv = jnp.concatenate([turned, joined[:, 384:]], axis=1).astype(BF16)
-    qkv_ref[...] = qkv
-    for batch in range(2):
-        allowed = mask_ref[batch] > 0.5
-        outs = []
-        for h in range(4):
-            q = head(qkv, batch, h * HD)
-            k = head(qkv, batch, 256 + (h // 2) * HD)
-            v = head(qkv, batch, 384 + (h // 2) * HD)
-            scores = jnp.where(allowed, dot_nt(q, k) * SCORE_SCALE, MASKED)
-            lifted = jnp.exp(scores - jnp.max(scores, axis=1, keepdims=True))
-            share = lifted / jnp.sum(lifted, axis=1, keepdims=True)
-            outs.append(dot(share.astype(BF16), v))
-        attended = jnp.concatenate(outs, axis=1).astype(BF16)
-        att_ref[batch * 128 : batch * 128 + 128] = attended
-        part_ref[batch] = dot(attended, wo_ref[0]).astype(BF16)
-
-
 def layer_block(shape, layer):
     return pl.BlockSpec((1,) + shape, lambda i: (layer,) + (0,) * len(shape))
 
@@ -673,30 +649,6 @@
 
 def local_params():
     return pltpu.CompilerParams(vmem_limit_bytes=VMEM_LIMIT)
-
-
-def attention_forward(rows, wqkv, wo, tables, layer):
-    cosine, sine, mask = tables
-    return pl.pallas_call(
-        attention_forward_kernel,
-        grid=(1,),
-        out_shape=[
-            jax.ShapeDtypeStruct((2, 128, D), BF16),
-            jax.ShapeDtypeStruct((256, 512), BF16),
-            jax.ShapeDtypeStruct((256, 256), BF16),
-        ],
-        in_specs=[
-            whole(256, D),
-            layer_block((D, 512), layer),
-            layer_block((256, D), layer),
-            whole(256, LANES),
-            whole(256, LANES),
-            whole(2, 128, 128),
-        ],
-        out_specs=[whole(2, 128, D), whole(256, 512), whole(256, 256)],
-        compiler_params=local_params(),
-        name="attention_forward",
-    )(rows, wqkv, wo, cosine, sine, mask)
 
 
 def attention_backward_kernel(
@@ -782,48 +734,6 @@
     return lifted / jnp.sum(lifted, axis=1, keepdims=True)
 
 
-def experts_forward_kernel(x_ref, wgu_ref, wd_ref, router_ref, mask_ref, sel_ref, y_ref, gu_ref):
-    x = x_ref[...]
-    gates = masked_softmax(dot(x, router_ref[0]), mask_ref[...])
-    total = None
-    for e in range(2):
-        gate = jnp.sum(gates * sel_ref[e : e + 1], axis=1, keepdims=True)
-        gu = dot(x, wgu_ref[0, e])
-        gu_ref[e] = gu.astype(BF16)
-        part, upper = gu[:, :F], gu[:, F:]
-        hidden = part * jax.nn.sigmoid(part) * upper
-        made = dot((hidden * gate).astype(BF16), wd_ref[0, e])
-        total = made if total is None else total + made
-    y_ref[...] = total.astype(BF16)
-
-
-def experts_forward(x, wgu, wd, router, mask, sel, layer):
-    count = x.shape[0]
-    tile = 256
-    return pl.pallas_call(
-        experts_forward_kernel,
-        grid=(count // tile,),
-        out_shape=[
-            jax.ShapeDtypeStruct((count, D), BF16),
-            jax.ShapeDtypeStruct((2, count, 2 * F), BF16),
-        ],
-        in_specs=[
-            pl.BlockSpec((tile, D), lambda i: (i, 0)),
-            layer_block((2, D, 2 * F), layer),
-            layer_block((2, F, D), layer),
-            layer_block((D, LANES), layer),
-            pl.BlockSpec((tile, LANES), lambda i: (i, 0)),
-            whole(8, LANES),
-        ],
-        out_specs=[
-            pl.BlockSpec((tile, D), lambda i: (i, 0)),
-            pl.BlockSpec((2, tile, 2 * F), lambda i: (0, i, 0)),
-        ],
-        compiler_params=local_params(),
-        name="experts_forward",
-    )(x, wgu, wd, router, mask, sel)
-
-
 def experts_backward_kernel(
     x_ref,
     g_ref,
@@ -939,26 +849,434 @@
     return lax.rsqrt(jnp.mean(values * values, axis=1, keepdims=True) + EPSILON)
 
 
-def layer_forward(layer_in, layer, common, weights):
-    tables, mask_own, mask_all, sel = common
+class Names:
+    pass
+
+
+def take_turns(running):
+    running = list(running)
+    while running:
+        for one in list(running):
+            if next(one, "end") == "end":
+                running.remove(one)
+
+
+def one_kernel(name, number, axes, ins, outs, scratch, chains):
+    names = list(ins) + list(outs) + list(scratch)
+
+    def kernel(*refs):
+        at = Names()
+        for key, ref in zip(names, refs):
+            setattr(at, key, ref)
+        greet([peer for axis in axes for peer in around(axis)])
+        take_turns(chains(at))
+
+    results = pl.pallas_call(
+        kernel,
+        out_shape=[jax.ShapeDtypeStruct(o[0], o[1]) for o in outs.values()],
+        in_specs=[i[1] for i in ins.values()],
+        out_specs=[o[2] for o in outs.values()],
+        scratch_shapes=list(scratch.values()),
+        compiler_params=comm_params(number),
+        name=name,
+    )(*[i[0] for i in ins.values()])
+    made = Names()
+    for key, result in zip(outs, results):
+        setattr(made, key, result)
+    return made
+
+
+def chain_tp_block(ref, c, k, part):
+    place = lax.rem(lax.axis_index("tp") + k, 4)
+    if part is None:
+        return ref.at[c, pl.ds(pl.multiple_of(place * 32, 32), 32)]
+    return ref.at[c, pl.ds(pl.multiple_of(place * 32 + 16 * part, 16), 16)]
+
+
+def chain_tp_gather(own, ref, c, send, recv):
+    left, right = around("tp")
+    ring = RingGather(
+        lambda k, part: chain_tp_block(ref, c, k, part),
+        own,
+        left,
+        right,
+        [send.at[c, i] for i in range(4)],
+        [recv.at[c, i] for i in range(4)],
+    )
+    ring.start()
+    chain_tp_block(ref, c, 0, None)[...] = own[...]
+    yield
+    ring.forward()
+    yield
+    ring.finish()
+    ring.drain()
+
+
+def chain_tp_scatter(ref, c, temp, block, stage, send, recv, out):
+    left, right = around("tp")
+    ring = RingScatter(
+        lambda k, part: chain_tp_block(ref, c, k, part),
+        lambda side: temp.at[c, side],
+        lambda side, part: block.at[c, side, part],
+        lambda side: stage.at[c, side],
+        left,
+        right,
+        [send.at[c, i] for i in range(6)],
+        [recv.at[c, i] for i in range(6)],
+    )
+    ring.start()
+    yield
+    ring.middle()
+    yield
+    ring.finish()
+    for part in range(2):
+        out[c, pl.ds(16 * part, 16)] = ring.total(part)
+    ring.drain()
+
+
+TP_SCRATCH = dict(
+    tp_temp=pltpu.VMEM((2, 2, 16, D), BF16),
+    tp_block=pltpu.VMEM((2, 2, 2, 16, D), BF16),
+    tp_stage=pltpu.VMEM((2, 2, 16, D), BF16),
+    tp_sum=pltpu.VMEM((2, 32, D), F32),
+    tp_send=pltpu.SemaphoreType.DMA((2, 6)),
+    tp_recv=pltpu.SemaphoreType.DMA((2, 6)),
+    tg_send=pltpu.SemaphoreType.DMA((2, 4)),
+    tg_recv=pltpu.SemaphoreType.DMA((2, 4)),
+)
+
+
+def chain_block(ref, c, half, i, j, part, width):
+    me = lax.axis_index("exp")
+    at_x, at_z = me // 4, lax.rem(me, 4)
+    i, j = (i, j) if half == 0 else (j, i)
+    rows = pl.ds(0, 32) if part is None else pl.ds(16 * part, 16)
+    columns = pl.ds(width * half, width)
+    return ref.at[c, lax.rem(at_x + i, 4), lax.rem(at_z + j, 4), rows, columns]
+
+
+def chain_exp_gather(own, ref, c, send, recv, width=512):
+    sides = [around("x"), around("z")]
+    first, second = [], []
+    for half in range(2):
+
+        def ring(view, src, at, axis, half=half):
+            return RingGather(
+                view,
+                src,
+                sides[axis][0],
+                sides[axis][1],
+                [send.at[c, half, at, n] for n in range(4)],
+                [recv.at[c, half, at, n] for n in range(4)],
+            )
+
+        def along(k, part, half=half):
+            return chain_block(ref, c, half, k, 0, part, width)
+
+        src = own.at[:, pl.ds(width * half, width)]
+        first.append(ring(along, src, 4, half))
+        second.append([])
+        for i in range(4):
+
+            def across(k, part, half=half, i=i):
+                return chain_block(ref, c, half, i, k, part, width)
+
+            second[half].append(ring(across, src if i == 0 else None, i, 1 - half))
+    for half in range(2):
+        first[half].start()
+    for half in range(2):
+        second[half][0].start()
+        chain_block(ref, c, half, 0, 0, None, width)[...] = own[:, pl.ds(width * half, width)]
+    yield
+    for half in range(2):
+        first[half].forward()
+        second[half][3].start()
+        second[half][1].start()
+    yield
+    for half in range(2):
+        second[half][0].forward()
+    for half in range(2):
+        first[half].finish()
+        second[half][2].start()
+    yield
+    for i in (3, 1):
+        for half in range(2):
+            second[half][i].forward()
+    yield
+    for half in range(2):
+        second[half][2].forward()
+    yield
+    for half in range(2):
+        for ring in second[half]:
+            ring.finish()
+        for ring in second[half] + [first[half]]:
+            ring.drain()
+
+
+def chain_exp_scatter(ref, c, temp, block, stage, ready, send, recv, out):
+    sides = [around("x"), around("z")]
+    first, second = [], []
+    for half in range(2):
+
+        def ring(view, at, axis, half=half):
+            return RingScatter(
+                view,
+                lambda side: temp.at[c, half, at, side],
+                lambda side, part: block.at[c, half, at, side, pl.ds(16 * part, 16)],
+                lambda side: stage.at[c, half, at, side],
+                sides[axis][0],
+                sides[axis][1],
+                [send.at[c, half, at, n] for n in range(6)],
+                [recv.at[c, half, at, n] for n in range(6)],
+            )
+
+        first.append([])
+        for j in range(4):
+
+            def along(k, part, half=half, j=j):
+                return chain_block(ref, c, half, k, j, part, 512)
+
+            first[half].append(ring(along, j, half))
+
+        def across(k, part, half=half):
+            return ready.at[c, half, k, pl.ds(16 * part, 16)]
+
+        second.append(ring(across, 4, 1 - half))
+    order = (2, 1, 3, 0)
+    for j in order:
+        for half in range(2):
+            first[half][j].start()
+    yield
+    for j in order:
+        for half in range(2):
+            first[half][j].middle()
+    yield
+    for j in order:
+        for half in range(2):
+            first[half][j].finish()
+            for part in range(2):
+                ready[c, half, j, pl.ds(16 * part, 16)] = first[half][j].total(part).astype(BF16)
+            if j == 3:
+                second[half].start()
+    yield
+    for half in range(2):
+        second[half].middle()
+    yield
+    for half in range(2):
+        second[half].finish()
+        for part in range(2):
+            out[c, pl.ds(16 * part, 16), pl.ds(512 * half, 512)] = second[half].total(part)
+    for half in range(2):
+        for ring in first[half] + [second[half]]:
+            ring.drain()
+
+
+EXP_SCRATCH = dict(
+    es_temp=pltpu.VMEM((2, 2, 5, 2, 16, 512), BF16),
+    es_block=pltpu.VMEM((2, 2, 5, 2, 32, 512), BF16),
+    es_stage=pltpu.VMEM((2, 2, 5, 2, 16, 512), BF16),
+    es_ready=pltpu.VMEM((2, 2, 4, 32, 512), BF16),
+    es_made=pltpu.VMEM((2, 4, 4, 32, D), BF16),
+    es_send=pltpu.SemaphoreType.DMA((2, 2, 5, 6)),
+    es_recv=pltpu.SemaphoreType.DMA((2, 2, 5, 6)),
+    eg_send=pltpu.SemaphoreType.DMA((2, 2, 5, 4)),
+    eg_recv=pltpu.SemaphoreType.DMA((2, 2, 5, 4)),
+)
+
+
+def rope(values, cosine, sine):
+    return values * three(cosine) + half_swapped(values) * three(sine)
+
+
+def unrope(values, cosine, sine):
+    return values * three(cosine) - half_swapped(values) * three(sine)
+
+
+def shares(q, k, allowed):
+    scores = jnp.where(allowed, dot_nt(q, k) * SCORE_SCALE, MASKED)
+    lifted = jnp.exp(scores - jnp.max(scores, axis=1, keepdims=True))
+    return lifted / jnp.sum(lifted, axis=1, keepdims=True)
+
+
+def forward_chain(at, c, layer, loads):
+    x = at.xin[c].astype(F32)
+    at.normed[c] = (x * inverse_rms(x) * at.gains[layer, 0:1]).astype(BF16)
+    yield from chain_tp_gather(at.normed.at[c], at.rows, c, at.tg_send, at.tg_recv)
+    if c == 0:
+        loads["wqkv"].wait()
+        loads["wo"].wait()
+    joined = dot(at.rows[c], at.v_wqkv[...])
+    spot = slice(c * 128, c * 128 + 128)
+    turned = rope(joined[:, :384], at.cosine[spot], at.sine[spot])
+    qkv = jnp.concatenate([turned, joined[:, 384:]], axis=1).astype(BF16)
+    at.qkv[c] = qkv
+    allowed = at.mask[c] > 0.5
+    outs = []
+    for h in range(4):
+        kv = h // 2
+        share = shares(head(qkv, 0, h * HD), head(qkv, 0, 256 + kv * HD), allowed)
+        outs.append(dot(share.astype(BF16), head(qkv, 0, 384 + kv * HD)))
+    attended = jnp.concatenate(outs, axis=1).astype(BF16)
+    at.att[c] = attended
+    at.part[c] = dot(attended, at.v_wo[...]).astype(BF16)
+    yield from chain_tp_scatter(
+        at.part, c, at.tp_temp, at.tp_block, at.tp_stage, at.tp_send, at.tp_recv, at.tp_sum
+    )
+    after = x + at.tp_sum[c]
+    at.after[c] = after
+    at.normed_two[c] = (after * inverse_rms(after) * at.gains[layer, 1:2]).astype(BF16)
+    yield from chain_exp_gather(at.normed_two.at[c], at.v_x, c, at.eg_send, at.eg_recv)
+    at.saves[c].start()
+    if c == 0:
+        for key in ("router", "wgu", "wd"):
+            loads[key].wait()
+    for tile in range(2):
+        pair = pl.ds(2 * tile, 2)
+        rows = pl.ds(256 * tile, 256)
+        xt = at.v_x[c, pair].reshape(256, D)
+        gates = masked_softmax(
+            dot(xt, at.v_router[...]), at.routed[c, pair, :, :, :LANES].reshape(256, LANES).astype(F32)
+        )
+        total = None
+        for e in range(2):
+            gate = jnp.sum(gates * at.sel[e : e + 1], axis=1, keepdims=True)
+            gu = dot(xt, at.v_wgu[e])
+            at.v_gu[c, e, rows] = gu.astype(BF16)
+            part, upper = gu[:, :F], gu[:, F:]
+            hidden = part * jax.nn.sigmoid(part) * upper
+            made = dot((hidden * gate).astype(BF16), at.v_wd[e])
+            total = made if total is None else total + made
+        at.es_made[c, pair] = total.astype(BF16).reshape(2, 4, 32, D)
+    at.saves[2 + c].start()
+    yield from chain_exp_scatter(
+        at.es_made,
+        c,
+        at.es_temp,
+        at.es_block,
+        at.es_stage,
+        at.es_ready,
+        at.es_send,
+        at.es_recv,
+        at.y,
+    )
+    at.out[c] = (at.after[c] + at.y[c]).astype(BF16)
+    at.saves[c].wait()
+    at.saves[2 + c].wait()
+
+
+def mask_chain(at, c):
+    yield from chain_exp_gather(
+        at.routed_own.at[c], at.routed, c, at.mg_send, at.mg_recv, width=LANES
+    )
+
+
+def pair_chain(at, loads):
+    me = lax.axis_index("section")
+    (peer,) = around("section")
+    sends, reads, writes = [], [], []
+    pieces = ((at.own_gu, at.held_gu, at.wgu), (at.own_d, at.held_d, at.wd))
+    for n, (own, held, both) in enumerate(pieces):
+        sends.append(
+            remote(own.at[0], both.at[me], at.pair_sems.at[0, n], at.pair_sems.at[1, n], peer)
+        )
+        reads.append(pltpu.make_async_copy(own.at[0], held, at.pair_sems.at[2, n]))
+        writes.append(pltpu.make_async_copy(held, both.at[me], at.pair_sems.at[3, n]))
+        sends[-1].start()
+        reads[-1].start()
+    yield
+    yield
+    for n in range(2):
+        reads[n].wait()
+        writes[n].start()
+    for _ in range(6):
+        yield
+    for n in range(2):
+        writes[n].wait()
+        sends[n].wait()
+    loads["wgu"].start()
+    loads["wd"].start()
+
+
+def forward_pass(xin, layer, tables, sel, weights, routed_own, routed):
+    cosine, sine, mask = tables
     wqkv, wo, gains, router, wgu, wd = weights
-    unpaired = wgu.shape[0] == 1
-    inverse_one = inverse_rms(layer_in)
-    normed = (layer_in * inverse_one * gains[layer, 0:1]).astype(BF16)
-    rows = fuse([tp_gather_part(normed.reshape(2, 32, D))], 2, "tp_gather")[0].reshape(256, D)
-    part, qkv, att = attention_forward(rows, wqkv, wo, tables, layer)
-    after = layer_in + fuse([tp_scatter_part(part)], 3, "tp_scatter")[0].reshape(64, D)
-    inverse_two = inverse_rms(after)
-    normed_two = (after * inverse_two * gains[layer, 1:2]).astype(BF16)
-    if unpaired:
-        x_all, (wgu, wd) = fuse([exp_gather_part(normed_two), pair_part([wgu, wd])], 1, "gather_pair")
+    swap = layer == 0
+    v, a = in_vmem(), in_any()
+    ins = dict(
+        xin=(xin, v),
+        gains=(gains, v),
+        cosine=(cosine, v),
+        sine=(sine, v),
+        mask=(mask, v),
+        sel=(sel, v),
+        wqkv=(wqkv, a),
+        wo=(wo, a),
+        router=(router, a),
+    )
+    if swap:
+        ins.update(routed_own=(routed_own, v), own_gu=(wgu, a), own_d=(wd, a))
     else:
-        (x_all,) = fuse([exp_gather_part(normed_two)], 4, "exp_gather")
-    x_all = x_all.reshape(1024, D)
-    made, gu = experts_forward(x_all, wgu, wd, router, mask_all, sel, layer)
-    (y,) = fuse([exp_scatter_part(made)], 5, "exp_scatter")
-    stored = (layer_in, inverse_one, rows, qkv, att, after, inverse_two, normed_two, x_all, gu, y)
-    return after + y, stored, (wgu, wd)
+        ins.update(routed=(routed, v), wgu=(wgu, a), wd=(wd, a))
+    outs = dict(
+        out=((2, 32, D), BF16, v),
+        rows=((2, 128, D), BF16, v),
+        qkv=((2, 128, 512), BF16, v),
+        att=((2, 128, 256), BF16, v),
+        after=((2, 32, D), F32, v),
+        y=((2, 32, D), F32, v),
+        x_all=((2, 4, 4, 32, D), BF16, a),
+        gu=((2, 2, 512, 2 * F), BF16, a),
+    )
+    scratch = dict(
+        normed=pltpu.VMEM((2, 32, D), BF16),
+        normed_two=pltpu.VMEM((2, 32, D), BF16),
+        part=pltpu.VMEM((2, 128, D), BF16),
+        v_wqkv=pltpu.VMEM((D, 512), BF16),
+        v_wo=pltpu.VMEM((256, D), BF16),
+        v_router=pltpu.VMEM((D, LANES), BF16),
+        v_wgu=pltpu.VMEM((2, D, 2 * F), BF16),
+        v_wd=pltpu.VMEM((2, F, D), BF16),
+        v_x=pltpu.VMEM((2, 4, 4, 32, D), BF16),
+        v_gu=pltpu.VMEM((2, 2, 512, 2 * F), BF16),
+        load_sems=pltpu.SemaphoreType.DMA((5,)),
+        save_sems=pltpu.SemaphoreType.DMA((4,)),
+        **TP_SCRATCH,
+        **EXP_SCRATCH,
+    )
+    if swap:
+        outs.update(
+            wgu=((2, 2, D, 2 * F), BF16, a),
+            wd=((2, 2, F, D), BF16, a),
+            routed=((2, 4, 4, 32, 2 * LANES), BF16, v),
+        )
+        scratch.update(
+            held_gu=pltpu.VMEM((2, D, 2 * F), BF16),
+            held_d=pltpu.VMEM((2, F, D), BF16),
+            pair_sems=pltpu.SemaphoreType.DMA((4, 2)),
+            mg_send=pltpu.SemaphoreType.DMA((2, 2, 5, 4)),
+            mg_recv=pltpu.SemaphoreType.DMA((2, 2, 5, 4)),
+        )
+
+    def chains(at):
+        loads = {}
+        for n, key in enumerate(("wqkv", "wo", "router", "wgu", "wd")):
+            loads[key] = pltpu.make_async_copy(
+                getattr(at, key).at[layer], getattr(at, "v_" + key), at.load_sems.at[n]
+            )
+        at.saves = [
+            pltpu.make_async_copy(src.at[c], dst.at[c], at.save_sems.at[2 * n + c])
+            for n, (src, dst) in enumerate(((at.v_x, at.x_all), (at.v_gu, at.gu)))
+            for c in range(2)
+        ]
+        for key in ("wqkv", "wo", "router") if swap else loads:
+            loads[key].start()
+        running = [forward_chain(at, c, layer, loads) for c in range(2)]
+        if swap:
+            running = [pair_chain(at, loads), mask_chain(at, 0), mask_chain(at, 1)] + running
+        return running
+
+    axes = ["tp", "x", "z"] + (["section"] if swap else [])
+    return one_kernel("forward%d" % layer, 10 + layer, axes, ins, outs, scratch, chains)
 
 
 def layer_backward(grad, stored, layer, common, weights, pending):
@@ -1078,17 +1396,41 @@
     cosine, sine, mask = jax.vmap(rope_tables)(own_batches(segments))
     tables = (cosine.reshape(256, LANES), sine.reshape(256, LANES), mask)
     routes_own = own_batches(routes).reshape(64, 8)
-    routes_all = lax.all_gather(routes_own, "exp", axis=0, tiled=True)
     lanes = lax.broadcasted_iota(jnp.int32, (8, LANES), 1)
     sel = (lanes == 2 * expert + lax.broadcasted_iota(jnp.int32, (8, LANES), 0)).astype(F32)
-    common = (tables, routed(routes_own), routed(routes_all), sel)
-
-    start = own_batches(activations).reshape(64, D).astype(F32)
-    result, kept_first, experts = layer_forward(start, 0, common, weights)
-    weights = tuple(paired) + tuple(experts)
-    out_first = result.astype(BF16)
-    result, kept_second, _ = layer_forward(out_first.astype(F32), 1, common, weights)
-    out_second = result.astype(BF16)
+    routed_own = routed(routes_own)
+    doubled = jnp.concatenate([routed_own] * 2, axis=1).astype(BF16).reshape(2, 32, 2 * LANES)
+
+    start = own_batches(activations)
+    made = forward_pass(start, 0, tables, sel, weights, doubled, None)
+    out_first = made.out
+    weights = tuple(paired) + (made.wgu, made.wd)
+    routed_all = made.routed[..., :LANES]
+    kept = forward_pass(out_first, 1, tables, sel, weights, None, made.routed)
+    out_second = kept.out
+
+    def old(made, layer_in):
+        layer_in = layer_in.reshape(64, D).astype(F32)
+        after = made.after.reshape(64, D)
+        inverse_two = inverse_rms(after)
+        return (
+            layer_in,
+            inverse_rms(layer_in),
+            made.rows.reshape(256, D),
+            made.qkv.reshape(256, 512),
+            made.att.reshape(256, 256),
+            after,
+            inverse_two,
+            (after * inverse_two * paired[2][0 if made is first_made else 1, 1:2]).astype(BF16),
+            made.x_all.transpose(1, 2, 0, 3, 4).reshape(1024, D),
+            made.gu.reshape(2, 2, 16, 32, D).transpose(1, 2, 0, 3, 4).reshape(2, 1024, D),
+            made.y.reshape(64, D),
+        )
+
+    first_made = made
+    kept_first, kept_second = old(made, start), old(kept, out_first)
+    mask_all = routed_all.transpose(1, 2, 0, 3, 4).reshape(1024, LANES).astype(F32)
+    common = (tables, routed_own, mask_all, sel)
     grad = own_batches(cotangent).reshape(64, D)
     grad_second, wide_second, done_second, pending = layer_backward(
         grad, kept_second, 1, common, weights, []
@@ -1112,7 +1454,7 @@
             jnp.where(section == 0, jnp.stack([kept, got]), jnp.stack([got, kept]))[None]
         )
     return (
-        by_layer(out_first, out_second),
+        by_layer(out_first.reshape(64, D), out_second.reshape(64, D)),
         by_layer(grad_first, grad_second),
         small[:, E][None],
         dw[None, :, :256],

time: 545 us -> 494 us (0.906)
  starting transfers between devices: 31.3 us -> 4.89 us
  blocking collectives: 20.3 us -> 0 us
  local copies, waits for them, and re-layouts: 10.1 us -> 24.9 us
  other arithmetic: 47.7 us -> 37 us
  Pallas kernels: 419 us -> 411 us
    pallas_call x18 -> x10, Pallas kernels: 306 us -> 209 us  [fuse(): pl.pallas_call(functools.partial(fused_kernel, parts), out_shape=[o for p...]
    pallas_call x4 -> x2, Pallas kernels: 36.5 us -> 126 us  [one_kernel(): pl.pallas_call(kernel, out_shape=[jax.ShapeDtypeStruct(o[0], o[1]) for o...]
    ppermute x5, starting transfers between devices: 31.3 us -> 4.89 us  [to_owner(): return (kept, lax.ppermute(sent, 'section', [(0, 1), (1, 0)]))]
    all_gather x1 -> x0, blocking collectives: 20.3 us -> none  [per_device(): routes_all = lax.all_gather(routes_own, 'exp', axis=0, tiled=True)]
    reshape x1 -> x2, local copies, waits for them, and re-layouts: 0.08 us -> 10.1 us  [old(): made.gu.reshape(2, 2, 16, 32, D).transpose(1, 2, 0, 3, 4)]
    reduce_sum x2 -> x1, other arithmetic: 6.7 us -> 0.16 us  [routed(): jnp.sum((routes[:, :, None] == labels[None, None, :]).astype(F32), axis=1)]
  transfers between devices with their start and end apart: 5 -> 5, of which waited for: 0 -> 0; matrix products, arithmetic and copies ran while one was open for 6% -> 4% of each run, Pallas kernels for 49% -> 0%
where the time goes in v3:
time: 494 us; the launch traced here: 484 us
  Pallas kernels  411 us (83%)
  other arithmetic  37 us (7%)
  local copies, waits for them, and re-layouts  24.9 us (5%)
    pallas_call x10, Pallas kernels, fuse(): pl.pallas_call(functools.partial(fused_kernel, parts), out_shape=[o for p...  209 us
    pallas_call x2, Pallas kernels, one_kernel(): pl.pallas_call(kernel, out_shape=[jax.ShapeDtypeStruct(o[0], o[1]) for o...  126 us
    pallas_call x2, Pallas kernels, experts_backward(): pl.pallas_call(experts_backward_kernel, grid=(2,), out_shape=[jax.ShapeDt...  61.5 us
    pallas_call x2, Pallas kernels, attention_backward(): pl.pallas_call(attention_backward_kernel, grid=(1,), out_shape=[jax.Shape...  15.2 us
    reshape x2, local copies, waits for them, and re-layouts, old(): made.gu.reshape(2, 2, 16, 32, D).transpose(1, 2, 0, 3, 4)  10.1 us
  transfers between devices with their start and end apart: 5, of which 0 were waited for; matrix products, arithmetic and copies ran while one was open for 4% of the time, Pallas kernels for 0%

profile of v3, /device:TPU:1, one launch (start us, length us, event | category | flops | bytes accessed | tf_op | source)
XLA Modules:
  0.0 483.8 jit_solution(13233806950952319573)
XLA Ops:
  3.3 1.6 multiply_reduce_fusion.3
  5.5 1.0 copy.59
  8.0 2.3 pad_maximum_fusion.3.refs_0_
  11.0 5.4 %pair.1 = (bf16[2,1024,512]{2,1,0:T(8,128)(2,1)}, bf16[2,256,1024]{2,1,0:T(8,128)(2,1)}, f32[2,8,1024]{2,1,0:T(8,128)}, bf16[2,1024,128]{2,1,0:T(8,128)(2,1)}) custom-call(bf16[1,1024,512]{2,1,0:T(8,128)(2,1)} %pad_maximum_fusion.3.refs_0_, bf16[1,256,1024]{2,1,0:T(8,128)(2,1)} %refs_1_.1, f32[1,8,1024]{2,1,0:T(8,128)} %maximum_convert_fusion.refs_2_, ...), custom_call_target="tpu_custom_call" | custom-call | tf_op jit(solution)/shard_map/pair/pallas_call | solution.py:114
  17.8 1.0 pad_maximum_fusion.4
  18.7 61.8 %forward0.1 = (bf16[2,32,1024]{2,1,0:T(8,128)(2,1)}, bf16[2,128,1024]{2,1,0:T(8,128)(2,1)}, bf16[2,128,512]{2,1,0:T(8,128)(2,1)}, bf16[2,128,256]{2,1,0:T(8,128)...) custom-call(bf16[2,32,1024]{2,1,0:T(8,128)(2,1)} %get-tuple-element., ...), custom_call_target="tpu_custom_call" | custom-call | tf_op jit(solution)/shard_map/forward0/pallas_call | solution.py:874
  80.5 1.1 multiply_reduce_fusion.4
  81.7 1.0 multiply_convert_fusion
  82.7 1.0 convert_bitcast_fusion
  83.7 1.0 multiply_reduce_fusion.6
  84.8 63.8 %forward1.1 = (bf16[2,32,1024]{2,1,0:T(8,128)(2,1)}, bf16[2,128,1024]{2,1,0:T(8,128)(2,1)}, bf16[2,128,512]{2,1,0:T(8,128)(2,1)}, bf16[2,128,256]{2,1,0:T(8,128)...) custom-call(bf16[2,32,1024]{2,1,0:T(8,128)(2,1)} %get-tuple-element., ...), custom_call_target="tpu_custom_call" | custom-call | tf_op jit(solution)/shard_map/forward1/pallas_call | solution.py:874
  148.6 1.1 multiply_reduce_fusion.8
  149.7 1.0 multiply_convert_fusion.1
  151.3 5.0 %copy.64 = bf16[2,2,16,32,1024]{4,3,0,2,1:T(8,128)(2,1)} copy(bf16[2,2,16,32,1024]{4,3,2,1,0:T(8,128)(2,1)} %bitcast.199) | data formatting | bytes 8388608 | tf_op jit(solution)/shard_map/reshape | solution.py:1426
  157.0 15.4 %exp_gather.1 = bf16[4,4,64,1024]{3,2,1,0:T(8,128)(2,1)} custom-call(bf16[64,1024]{1,0:T(8,128)(2,1)} %bitcast.207), custom_call_target="tpu_custom_call" | custom-call | tf_op jit(solution)/shard_map/exp_gather/pallas_call | solution.py:114
  172.5 1.6 copy.63
  175.0 30.6 %experts_backward.2 = (bf16[1024,1024]{1,0:T(8,128)(2,1)}, bf16[2,1024,1024]{2,1,0:T(8,128)(2,1)}, bf16[2,512,1024]{2,1,0:T(8,128)(2,1)}, f32[1024,128]{1,0:T(8,128)}) custom-call(bf16[1024,1024]{1,0:T(8,128)(2,1)} %bitcast.191, bf16[1024,1024]{1,0:T(8,128)(2,1)} %bitcast.190, bf16[2,1024,1024]{2,1,0:T(8,128)(2,1)} %bitcast.188, ...), custom_call_target="tpu_custom_call" | custom-call | tf_op jit(solution)/shard_map/experts_backward/pallas_call | solution.py:811
  205.7 50.1 %scatter_expert.2 = (f32[64,1024]{1,0:T(8,128)}, bf16[512,256]{1,0:T(8,128)(2,1)}, bf16[512,256]{1,0:T(8,128)(2,1)}) custom-call(bf16[4,4,64,1024]{3,2,1,0:T(8,128)(2,1)} %bitcast.202, bf16[2,1024,1024]{2,1,0:T(8,128)(2,1)} %get-tuple-element.70.refs_1_.refs_2_, bf16[2,1024,1024]{2,1,0:T(8,128)(2,1)} %get-tuple-element.70.refs_1_.refs_2_), custom_call_target="tpu_custom_call" | custom-call | tf_op jit(solution)/shard_map/scatter_expert/pallas_call | solution.py:114
  256.0 1.4 fusion.28
  258.1 8.2 %tp_gather.2 = bf16[2,128,1024]{2,1,0:T(8,128)(2,1)} custom-call(bf16[2,32,1024]{2,1,0:T(8,128)(2,1)} %bitcast.211), custom_call_target="tpu_custom_call" | custom-call | tf_op jit(solution)/shard_map/tp_gather/pallas_call | solution.py:114
  266.4 7.5 %attention_backward.2 = (bf16[2,128,1024]{2,1,0:T(8,128)(2,1)}, bf16[1024,768]{1,0:T(8,128)(2,1)}) custom-call(bf16[256,1024]{1,0:T(8,128)(2,1)} %bitcast.210, bf16[256,1024]{1,0:T(8,128)(2,1)} %bitcast.204, bf16[256,512]{1,0:T(8,128)(2,1)} %bitcast.216, bf16[256,256]{1,0:T(8,128)(2,1)} %bitcast.218, ...), custom_call_target="tpu_custom_call" | custom-call | tf_op jit(solution)/shard_map/attention_backward/pallas_call | solution.py:706
  273.9 9.7 %tp_scatter.2 = f32[2,32,1024]{2,1,0:T(8,128)} custom-call(bf16[2,128,1024]{2,1,0:T(8,128)(2,1)} %get-tuple-element.76.refs_0_), custom_call_target="tpu_custom_call" | custom-call | tf_op jit(solution)/shard_map/tp_scatter/pallas_call | solution.py:114
  283.8 1.1 multiply_reduce_fusion
  285.0 5.1 %copy.67 = bf16[2,2,16,32,1024]{4,3,0,2,1:T(8,128)(2,1)} copy(bf16[2,2,16,32,1024]{4,3,2,1,0:T(8,128)(2,1)} %bitcast.198) | data formatting | bytes 8388608 | tf_op jit(solution)/shard_map/reshape | solution.py:1426
  290.1 1.5 copy.66
  291.6 0.9 fusion.6
  292.5 23.2 %gather_expert.1 = (bf16[4,4,64,1024]{3,2,1,0:T(8,128)(2,1)}, bf16[512,256]{1,0:T(8,128)(2,1)}) custom-call(bf16[64,1024]{1,0:T(8,128)(2,1)} %get-tuple-element.118.refs_0_, bf16[2,512,1024]{2,1,0:T(8,128)(2,1)} %get-tuple-element.79.refs_1_), custom_call_target="tpu_custom_call" | custom-call | tf_op jit(solution)/shard_map/gather_expert/pallas_call | solution.py:114
  315.6 30.9 %experts_backward.3 = (bf16[1024,1024]{1,0:T(8,128)(2,1)}, bf16[2,1024,1024]{2,1,0:T(8,128)(2,1)}, bf16[2,512,1024]{2,1,0:T(8,128)(2,1)}, f32[1024,128]{1,0:T(8,128)}) custom-call(bf16[1024,1024]{1,0:T(8,128)(2,1)} %bitcast.189, bf16[1024,1024]{1,0:T(8,128)(2,1)} %bitcast.200, bf16[2,1024,1024]{2,1,0:T(8,128)(2,1)} %bitcast.187, ...), custom_call_target="tpu_custom_call" | custom-call | tf_op jit(solution)/shard_map/experts_backward/pallas_call | solution.py:811
  346.6 24.6 %scatter_expert.3 = (f32[64,1024]{1,0:T(8,128)}, bf16[512,256]{1,0:T(8,128)(2,1)}) custom-call(bf16[4,4,64,1024]{3,2,1,0:T(8,128)(2,1)} %bitcast.201, bf16[2,1024,1024]{2,1,0:T(8,128)(2,1)} %get-tuple-element.83.refs_1_.refs_2_), custom_call_target="tpu_custom_call" | custom-call | tf_op jit(solution)/shard_map/scatter_expert/pallas_call | solution.py:114
  371.2 1.4 fusion.15
  373.3 8.5 %tp_gather.3 = bf16[2,128,1024]{2,1,0:T(8,128)(2,1)} custom-call(bf16[2,32,1024]{2,1,0:T(8,128)(2,1)} %bitcast.212), custom_call_target="tpu_custom_call" | custom-call | tf_op jit(solution)/shard_map/tp_gather/pallas_call | solution.py:114
  381.8 7.6 %attention_backward.3 = (bf16[2,128,1024]{2,1,0:T(8,128)(2,1)}, bf16[1024,768]{1,0:T(8,128)(2,1)}) custom-call(bf16[256,1024]{1,0:T(8,128)(2,1)} %bitcast.209, bf16[256,1024]{1,0:T(8,128)(2,1)} %bitcast.203, bf16[256,512]{1,0:T(8,128)(2,1)} %bitcast.215, bf16[256,256]{1,0:T(8,128)(2,1)} %bitcast.217, ...), custom_call_target="tpu_custom_call" | custom-call | tf_op jit(solution)/shard_map/attention_backward/pallas_call | solution.py:706
  389.5 9.5 %tp_scatter.3 = f32[2,32,1024]{2,1,0:T(8,128)} custom-call(bf16[2,128,1024]{2,1,0:T(8,128)(2,1)} %get-tuple-element.89.refs_0_), custom_call_target="tpu_custom_call" | custom-call | tf_op jit(solution)/shard_map/tp_scatter/pallas_call | solution.py:114
  399.6 1.4 pad_maximum_fusion.2
  401.9 1.4 pad_maximum_fusion.1
  403.3 54.3 %settle.1 = (f32[64,768]{1,0:T(8,128)}, f32[4,4,64,128]{3,2,1,0:T(8,128)}, bf16[512,256]{1,0:T(8,128)(2,1)}, bf16[512,256]{1,0:T(8,128)(2,1)}) custom-call(bf16[4,4,64,896]{3,2,1,0:T(8,128)(2,1)} %bitcast.193, bf16[4,4,64,896]{3,2,1,0:T(8,128)(2,1)} %bitcast.192, bf16[2,1024,1024]{2,1,0:T(8,128)(2,1)} %get-tuple-element.83.refs_1_.refs_2_, ...), custom_call_target="tpu_custom_call" | custom-call | tf_op jit(solution)/shard_map/settle/pallas_call | solution.py:114
  457.6 1.8 bitcast_convert_fusion
  459.4 3.9 collective-permute-start.4
  466.4 1.6 select_bitcast_fusion
  470.3 1.5 slice_bitcast_fusion
  472.7 1.4 slice_bitcast_fusion.2
  474.1 1.7 maximum_select_fusion.4
  475.8 1.0 bitcast_convert_fusion.1
  476.8 1.0 bitcast_convert_fusion.5
  477.8 1.0 maximum_select_fusion.2
  478.9 1.0 bitcast_convert_fusion.3
  480.0 1.5 pad_maximum_fusion
  481.5 1.9 maximum_select_fusion.3
  (128 shorter events, 19.1 us)
Async XLA Ops:
  0.6 0.7 copy-start
  0.7 9.6 %copy-start.27 = (bf16[1,1024]{1,0:T(2,128)(2,1)S(1)}, bf16[1,1024]{1,0:T(2,128)(2,1)}, u32[]{:S(2)}) copy-start(bf16[1,1024]{1,0:T(2,128)(2,1)} %param.17) | copy-start | bytes 6148
  0.7 9.6 %copy-start.26 = (bf16[1,1024]{1,0:T(2,128)(2,1)S(1)}, bf16[1,1024]{1,0:T(2,128)(2,1)}, u32[]{:S(2)}) copy-start(bf16[1,1024]{1,0:T(2,128)(2,1)} %param.22) | copy-start | bytes 6148
  84.8 66.0 %copy-start.2 = (bf16[2,1024,128]{2,1,0:T(8,128)(2,1)S(1)}, bf16[2,1024,128]{2,1,0:T(8,128)(2,1)}, u32[]{:S(2)}) copy-start(bf16[2,1024,128]{2,1,0:T(8,128)(2,1)} %get-tuple-element.60.refs_8_.router_ref) | copy-start | bytes 1572868
  151.3 5.0 %copy-start.24 = (f32[2,32,1024]{2,1,0:T(8,128)S(1)}, f32[2,32,1024]{2,1,0:T(8,128)}, u32[]{:S(2)}) copy-start(f32[2,32,1024]{2,1,0:T(8,128)} %get-tuple-element.72) | copy-start | bytes 786436
  151.3 5.0 %copy-start.25 = (bf16[4,32,1024]{2,1,0:T(8,128)(2,1)S(1)}, bf16[4,32,1024]{2,1,0:T(8,128)(2,1)}, u32[]{:S(2)}) copy-start(bf16[4,32,1024]{2,1,0:T(8,128)(2,1)} %param.14) | copy-start | bytes 786436
  156.4 16.1 %copy-start.13 = (bf16[2,4,4,32,1024]{4,3,2,1,0:T(8,128)(2,1)S(1)}, bf16[2,4,4,32,1024]{4,3,2,1,0:T(8,128)(2,1)}, u32[]{:S(2)}) copy-start(bf16[2,4,4,32,1024]{4,3,2,1,0:T(8,128)(2,1)} %get-tuple-element.67) | copy-start | bytes 6291460
  205.6 50.3 %copy-start.3 = (bf16[2,1024,128]{2,1,0:T(8,128)(2,1)S(1)}, bf16[2,1024,128]{2,1,0:T(8,128)(2,1)}, u32[]{:S(2)}) copy-start(bf16[2,1024,128]{2,1,0:T(8,128)(2,1)} %get-tuple-element.60.refs_8_.router_ref) | copy-start | bytes 1572868
  205.6 50.3 %copy-start.7 = (f32[2,32,1024]{2,1,0:T(8,128)S(1)}, f32[2,32,1024]{2,1,0:T(8,128)}, u32[]{:S(2)}) copy-start(f32[2,32,1024]{2,1,0:T(8,128)} %get-tuple-element.66) | copy-start | bytes 786436
  205.6 51.7 %copy-start.17 = (bf16[2,32,1024]{2,1,0:T(8,128)(2,1)S(1)}, bf16[2,32,1024]{2,1,0:T(8,128)(2,1)}, u32[]{:S(2)}) copy-start(bf16[2,32,1024]{2,1,0:T(8,128)(2,1)} %get-tuple-element.123) | copy-start | bytes 393220
  266.4 17.4 %copy-start.8 = (bf16[2,32,1024]{2,1,0:T(8,128)(2,1)S(1)}, bf16[2,32,1024]{2,1,0:T(8,128)(2,1)}, u32[]{:S(2)}) copy-start(bf16[2,32,1024]{2,1,0:T(8,128)(2,1)} %get-tuple-element.61.refs_0_) | copy-start | bytes 393220
  285.0 5.1 %copy-start.12 = (bf16[2,4,4,32,1024]{4,3,2,1,0:T(8,128)(2,1)S(1)}, bf16[2,4,4,32,1024]{4,3,2,1,0:T(8,128)(2,1)}, u32[]{:S(2)}) copy-start(bf16[2,4,4,32,1024]{4,3,2,1,0:T(8,128)(2,1)} %get-tuple-element.78) | copy-start | bytes 6291460
  290.1 1.5 copy-start.9
  290.1 1.5 copy-start.20
  346.5 24.6 %copy-start.4 = (bf16[2,1024,128]{2,1,0:T(8,128)(2,1)S(1)}, bf16[2,1024,128]{2,1,0:T(8,128)(2,1)}, u32[]{:S(2)}) copy-start(bf16[2,1024,128]{2,1,0:T(8,128)(2,1)} %get-tuple-element.60.refs_8_.router_ref) | copy-start | bytes 1572868
  346.5 24.6 %copy-start.6 = (f32[2,32,1024]{2,1,0:T(8,128)S(1)}, f32[2,32,1024]{2,1,0:T(8,128)}, u32[]{:S(2)}) copy-start(f32[2,32,1024]{2,1,0:T(8,128)} %get-tuple-element.77) | copy-start | bytes 786436
  346.6 26.0 %copy-start.16 = (bf16[64,1024]{1,0:T(8,128)(2,1)S(1)}, bf16[64,1024]{1,0:T(8,128)(2,1)}, u32[]{:S(2)}) copy-start(bf16[64,1024]{1,0:T(8,128)(2,1)} %get-tuple-element.118.refs_0_) | copy-start | bytes 393220
  381.8 17.2 %copy-start.28 = (f32[1024,128]{1,0:T(8,128)S(1)}, f32[1024,128]{1,0:T(8,128)}, u32[]{:S(2)}) copy-start(f32[1024,128]{1,0:T(8,128)} %get-tuple-element.93) | copy-start | bytes 1572868
  389.5 10.1 %copy-start.14 = (bf16[1024,768]{1,0:T(8,128)(2,1)S(1)}, bf16[1024,768]{1,0:T(8,128)(2,1)}, u32[]{:S(2)}) copy-start(bf16[1024,768]{1,0:T(8,128)(2,1)} %get-tuple-element.92) | copy-start | bytes 4718596
  399.5 1.5 copy-start.10
  399.5 1.5 copy-start.11
  399.5 1.6 copy-start.29
  399.5 2.4 copy-start.15
  403.3 54.3 %copy-start.21 = (bf16[512,256]{1,0:T(8,128)(2,1)S(1)}, bf16[512,256]{1,0:T(8,128)(2,1)}, u32[]{:S(2)}) copy-start(bf16[512,256]{1,0:T(8,128)(2,1)} %get-tuple-element.102) | copy-start | bytes 786436
  403.3 60.0 %copy-start.19 = (bf16[512,256]{1,0:T(8,128)(2,1)S(1)}, bf16[512,256]{1,0:T(8,128)(2,1)}, u32[]{:S(2)}) copy-start(bf16[512,256]{1,0:T(8,128)(2,1)} %get-tuple-element.98) | copy-start | bytes 786436
  403.3 60.0 %copy-start.22 = (bf16[512,256]{1,0:T(8,128)(2,1)S(1)}, bf16[512,256]{1,0:T(8,128)(2,1)}, u32[]{:S(2)}) copy-start(bf16[512,256]{1,0:T(8,128)(2,1)} %get-tuple-element.97) | copy-start | bytes 786436
  457.6 6.5 %copy-start.18 = (bf16[512,256]{1,0:T(8,128)(2,1)S(1)}, bf16[512,256]{1,0:T(8,128)(2,1)}, u32[]{:S(2)}) copy-start(bf16[512,256]{1,0:T(8,128)(2,1)} %get-tuple-element.100) | copy-start | bytes 786436
  457.6 6.4 %copy-start.23 = (bf16[512,256]{1,0:T(8,128)(2,1)S(1)}, bf16[512,256]{1,0:T(8,128)(2,1)}, u32[]{:S(2)}) copy-start(bf16[512,256]{1,0:T(8,128)(2,1)} %get-tuple-element.99) | copy-start | bytes 786436
  459.4 16.5 %collective-permute-start.4 = (bf16[512,256]{1,0:T(8,128)(2,1)}, bf16[512,256]{1,0:T(8,128)(2,1)}, u32[]{:S(2)}, u32[]{:S(2)}) collective-permute-start(bf16[512,256]{1,0:T(8,128)(2,1)} %get-tuple-element.127), channel_id=1, source_target_pairs={{0,64},{64,0},{1,65},{65,1},{2,66},{66,2},{3,67},{67,3},{4,68},{68... | collective-permute-start | bytes 786440 | tf_op jit(solution)/shard_map/ppermute | solution.py:1377
  463.3 5.2 %copy-start.5 = (f32[4,4,64,128]{3,2,1,0:T(8,128)S(1)}, f32[4,4,64,128]{3,2,1,0:T(8,128)}, u32[]{:S(2)}) copy-start(f32[4,4,64,128]{3,2,1,0:T(8,128)} %get-tuple-element.95) | copy-start | bytes 1572868
  464.0 12.8 %collective-permute-start.2 = (bf16[512,256]{1,0:T(8,128)(2,1)}, bf16[512,256]{1,0:T(8,128)(2,1)}, u32[]{:S(2)}, u32[]{:S(2)}) collective-permute-start(bf16[512,256]{1,0:T(8,128)(2,1)} %get-tuple-element.129), channel_id=1, source_target_pairs={{0,64},{64,0},{1,65},{65,1},{2,66},{66,2},{3,67},{67,3},{4,68},{68... | collective-permute-start | bytes 786440 | tf_op jit(solution)/shard_map/ppermute | solution.py:1377
  464.8 14.1 %collective-permute-start.3 = (bf16[512,256]{1,0:T(8,128)(2,1)}, bf16[512,256]{1,0:T(8,128)(2,1)}, u32[]{:S(2)}, u32[]{:S(2)}) collective-permute-start(bf16[512,256]{1,0:T(8,128)(2,1)} %get-tuple-element.131), channel_id=1, source_target_pairs={{0,64},{64,0},{1,65},{65,1},{2,66},{66,2},{3,67},{67,3},{4,68},{68... | collective-permute-start | bytes 786440 | tf_op jit(solution)/shard_map/ppermute | solution.py:1377
  466.3 15.1 %collective-permute-start.1 = (f32[64,1024]{1,0:T(8,128)}, f32[64,1024]{1,0:T(8,128)}, u32[]{:S(2)}, u32[]{:S(2)}) collective-permute-start(f32[64,1024]{1,0:T(8,128)} %get-tuple-element.125), channel_id=1, source_target_pairs={{0,64},{64,0},{1,65},{65,1},{2,66},{66,2},{3,67},{67,3},{4,68},{68... | collective-permute-start | bytes 786440 | tf_op jit(solution)/shard_map/ppermute | solution.py:1377
  467.9 6.2 %collective-permute-start = (bf16[64,1024]{1,0:T(8,128)(2,1)}, bf16[64,1024]{1,0:T(8,128)(2,1)}, u32[]{:S(2)}, u32[]{:S(2)}) collective-permute-start(bf16[64,1024]{1,0:T(8,128)(2,1)} %bitcast.6), channel_id=1, source_target_pairs={{0,64},{64,0},{1,65},{65,1},{2,66},{66,2},{3,67},{67,3},{4,68},{68... | collective-permute-start | bytes 393224 | tf_op jit(solution)/shard_map/ppermute | solution.py:1377
  479.9 3.4 copy-start.1
